TPU v7x, 32 devices: a whole 2x2x4 slice. The times are simulated.
32 devices in a mesh: sub: 4 (over z), crow: 4 (over x, core), ccol: 2 (over y).
Axes of the slice: x: 2, y: 2, z: 4, core: 2. Of those that a mesh axis runs over, the one named last changes fastest.
Arguments:
- load_cases: float32 [8, 1536, 256], P('sub', 'crow', 'ccol'), may hold values from -6 to 6
- stiffness: float32 [8, 1536, 1536], P('sub', 'crow'), may hold values from -1 to 6
- local_inverse: float32 [8, 1536, 1536], P('sub', 'crow'), may hold values from -1 to 1
- coarse_basis: float32 [8, 96, 1536], P('sub', None, 'crow'), may hold values from -0.15625 to 0.15625
- coarse_inverse: float32 [768, 768], P(('sub', 'crow')), may hold values from -1 to 3
- coupling: float32 [8, 6, 128, 128], P('sub'), may hold values from -0.5 to 0.5
- target_local_rows: int32 [8, 6, 128], P('sub'), may hold values from 0 to 1535
- neighbour_read_rows: int32 [8, 6, 128], P('sub'), may hold values from 0 to 1535
- neighbour: int32 [8, 6], P('sub'), may hold values from 0 to 7, as said below
- counts: int32 [8], P('sub'), may hold values from 1 to 6
Outputs:
- solution: float32 [8, 1536, 256], P('sub', 'crow', 'ccol')
- residual: float32 [8, 1536, 256], P('sub', 'crow', 'ccol')
Inputs may be any that keep to these rules, and one draw needn't show every extreme that they name: neighbour[s, k] is a subdomain other than s, at most 2 away from s in the numbering. Only the first counts[s] interface blocks of subdomain s act. `target_local_rows`: rows may repeat within a block.
All inputs are finite; a program needn't handle non-finite values.
Results may differ from a plain program's by a relative error of at most 0.00013.
Values sent between devices are 32-bit elements; how exact they have to be, the bound alone decides.
No kernel may reach another device: no remote copies, remote signals or barrier semaphores. Data moves between devices by JAX's collectives and lax.ppermute only.
A program may use at most 64 MiB of HBM per device.

v0:
```python
import jax
import jax.numpy as jnp
from jax import lax
from jax.sharding import PartitionSpec as P

ITERS = 2


damping = 0.7
highest_mode = lax.Precision.HIGHEST


def extended(x, sides, width):
    for axis, dim in sides:
        size, length = (lax.axis_size(axis), x.shape[dim])
        up = [(i, (i + 1) % size) for i in range(size - 1)]
        down = [(j, i) for i, j in up]
        last = lax.slice_in_dim(x, length - width, length, axis=dim)
        initial = lax.slice_in_dim(x, 0, width, axis=dim)
        before = lax.ppermute(last, axis, up)
        after = lax.ppermute(initial, axis, down)
        x = jnp.concatenate([before, x, after], axis=dim)
    return x


def from_behind(block, axis, distance):
    devices = range(lax.axis_size(axis))
    route = [(i - distance, i) for i in devices if i - distance in devices]
    return lax.ppermute(block, axis, route)


def take_requested(full_corr, lists, sub_first):
    sub_count, local_order, case_count = full_corr.shape
    wanted = lists[:, :, -1]
    source_rows = lists[:, :, :-1]
    relative = wanted - sub_first
    present = (relative >= 0) & (relative < sub_count)
    clipped = jnp.clip(relative, 0, sub_count - 1)
    flat_rows = clipped[:, :, None] * local_order + source_rows
    picked = jnp.take(full_corr.reshape(-1, case_count), flat_rows.reshape(-1), axis=0)
    picked = picked.reshape(flat_rows.shape + (case_count,))
    return picked * present[:, :, None, None].astype(jnp.float32)


def per_device(
    load_cases,
    stiffness,
    local_inverse,
    coarse_basis,
    coarse_inverse,
    coupling,
    target_local_rows,
    neighbour_read_rows,
    neighbour,
    counts,
):
    sub_count, row_count, case_count = load_cases.shape
    local_order = stiffness.shape[2]
    mode_count = coarse_basis.shape[1]
    sub_first = lax.axis_index("sub") * sub_count
    row_first = lax.axis_index("crow") * row_count
    target_block = jnp.arange(sub_count, dtype=jnp.int32)[:, None] * local_order
    slot_limit = jnp.max(counts)
    own_lists = jnp.concatenate([neighbour_read_rows, neighbour[:, :, None]], axis=2)
    wider_lists = extended(own_lists, (("sub", 0),), sub_count)
    lower_lists = wider_lists[:sub_count]
    upper_lists = wider_lists[2 * sub_count :]
    solution = jnp.zeros_like(load_cases)
    residual = load_cases
    for sweep_index in range(ITERS):
        local_corr = jnp.einsum(
            "slm,smc->slc",
            local_inverse,
            lax.all_gather(residual, "crow", axis=1, tiled=True),
            precision=highest_mode,
        )
        restricted = jnp.einsum("sel,slc->sec", coarse_basis, residual, precision=highest_mode)
        restricted = restricted.reshape(sub_count * mode_count, case_count)
        group_share = lax.psum_scatter(restricted, "crow", scatter_dimension=0, tiled=True)
        coarse_own = jnp.dot(
            coarse_inverse,
            lax.all_gather(group_share, ("sub", "crow"), axis=0, tiled=True),
            precision=highest_mode,
        )
        coarse_mine = lax.all_gather(coarse_own, "crow", axis=0, tiled=True).reshape(
            sub_count, mode_count, case_count
        )
        correction = local_corr + jnp.einsum(
            "sel,sec->slc", coarse_basis, coarse_mine, precision=highest_mode
        )
        solution = solution + damping * correction
        full_corr = lax.all_gather(correction, "crow", axis=1, tiled=True)
        local_part = jnp.einsum("slm,smc->slc", stiffness, full_corr, precision=highest_mode)
        for_upper = take_requested(full_corr, upper_lists, sub_first)
        for_lower = take_requested(full_corr, lower_lists, sub_first)
        from_lower = from_behind(for_upper, "sub", 1)
        from_upper = from_behind(for_lower, "sub", -1)
        slot_sources = take_requested(full_corr, own_lists, sub_first) + from_lower + from_upper

        def fetch(slot_index):
            return slot_sources[:, slot_index]

        def add_slot(slot_index, inflow):
            sources = fetch(slot_index)
            slot_terms = jnp.einsum(
                "snm,smc->snc", coupling[:, slot_index], sources, precision=highest_mode
            )
            active_flag = (slot_index < counts).astype(jnp.float32)
            target_rows = target_block + target_local_rows[:, slot_index, :]
            return inflow.at[target_rows].add(slot_terms * active_flag[:, None, None])

        inflow = lax.fori_loop(
            0, slot_limit, add_slot, jnp.zeros((sub_count * local_order, case_count), jnp.float32)
        )
        inflow_rows = lax.dynamic_slice_in_dim(
            inflow.reshape(sub_count, local_order, case_count), row_first, row_count, 1
        )
        residual = residual - damping * (local_part - inflow_rows)
    return (solution, residual)


def solution(mesh):
    return jax.shard_map(
        per_device,
        mesh=mesh,
        in_specs=(
            P("sub", "crow", "ccol"),
            P("sub", "crow", None),
            P("sub", "crow", None),
            P("sub", None, "crow"),
            P(("sub", "crow"), None),
            P("sub", None, None, None),
            P("sub", None, None),
            P("sub", None, None),
            P("sub", None),
            P("sub"),
        ),
        out_specs=(P("sub", "crow", "ccol"), P("sub", "crow", "ccol")),
        check_vma=False,
    )
```

profile of v0, /device:TPU:16, one launch (start us, length us, event | category | flops | bytes accessed | tf_op | source)
XLA Modules:
  0.0 328.4 jit_solution(12103398757538794636)
XLA Ops:
  8.1 2.1 fusion.31
  12.6 3.5 %collective-permute-start.2 = (s32[2,6,129]{1,0,2:T(2,128)S(1)}, s32[2,6,129]{1,0,2:T(2,128)S(1)}, u32[]{:S(2)}, u32[]{:S(2)}) collective-permute-start(s32[2,6,129]{1,0,2:T(2,128)S(1)} %pad_add_fusion), channel_id=1, source_target_pairs={{0,8},{8,16},{16,24},{1,9},{9,17},{17,25},{2,10},{10,18},{18,26},{... | collective-permute-start | bytes 18584 | tf_op jit(solution)/shard_map/ppermute | solution.py:20
  16.1 2.4 collective-permute-start
  20.5 11.2 %reduce-scatter.3.cloned.1.call-done = f32[48,128]{1,0:T(8,128)} async-done(((f32[192,128]{1,0:T(8,128)}), f32[48,128]{1,0:T(8,128)}) %reduce-scatter.3.cloned.1.call-update) | async-done | bytes 24592 | tf_op jit(solution)/shard_map/reduce_scatter | solution.py:79
  31.7 17.1 %all_gather.25 = f32[768,128]{1,0:T(8,128)S(1)} all-gather(f32[48,128]{1,0:T(8,128)} %reduce-scatter.3.cloned.1.call-done), channel_id=1, replica_groups=mesh['sub'=4,'crow'=4,'ccol'=2] {'sub','crow'}, dimensions={0}, use_global_device_ids=true | all-gather | bytes 417792 | tf_op jit(solution)/shard_map/all_gather | solution.py:82
  49.1 5.3 %all_gather.26 = f32[192,128]{1,0:T(8,128)S(1)} all-gather(f32[48,128]{1,0:T(8,128)S(1)} %convolution_bitcast_fusion.4), channel_id=1, replica_groups=mesh['sub'=4,'crow'=4,'ccol'=2] {'crow'}, dimensions={0}, use_global_device_ids=true | all-gather | bytes 122880 | tf_op jit(solution)/shard_map/all_gather | solution.py:85
  54.5 6.6 %fusion.30 = f32[2,384,128]{2,1,0:T(8,128)S(1)} fusion(f32[2,384,1536]{2,1,0:T(8,128)} %param.18, f32[2,1536,128]{2,1,0:T(8,128)} %all-gather.5.cloned.1.call-done), kind=kOutput, calls=%fused_computation.86 | convolution fusion | flops 1811939328 | bytes 6684672 | tf_op jit(solution)/shard_map/slm,smc->slc/dot_general | solution.py:71
  63.3 21.3 %all-gather.7.cloned.1.call-done = f32[2,1536,128]{2,1,0:T(8,128)} async-done(((f32[2,384,128]{2,1,0:T(8,128)}), f32[2,1536,128]{2,1,0:T(8,128)}) %all-gather.7.cloned.1.call-update) | async-done | bytes 1572880 | tf_op jit(solution)/shard_map/all_gather | solution.py:92
  84.7 4.1 %gather_fusion.2 = f32[1536,128]{1,0:T(8,128)S(1)} fusion(f32[3072,128]{1,0:T(8,128)} %bitcast.125, s32[2048]{0:T(1024)S(1)} %pad_clamp_fusion), kind=kCustom, calls=%fused_computation.2.clone | custom fusion | bytes 1579008 | tf_op jit(solution)/shard_map/jit(_take)/gather | solution.py:40
  88.8 2.6 gather_fusion.1
  91.8 3.4 %collective-permute-start.1 = (f32[2,6,128,128]{3,2,0,1:T(8,128)S(1)}, f32[2,6,128,128]{3,2,0,1:T(8,128)}, u32[]{:S(2)}, u32[]{:S(2)}) collective-permute-start(f32[2,6,128,128]{3,2,0,1:T(8,128)S(1)} %copy_multiply_fusion.4), channel_id=1, source_target_pairs={{0,8},{8,16},{16,24},{1,9},{9,17},{17,25},{2,10},{10,18},{18,26},{... | collective-permute-start | bytes 2359304 | tf_op jit(solution)/shard_map/ppermute | solution.py:29
  96.5 2.4 collective-permute-start.3
  99.0 2.6 gather_fusion
  101.8 11.6 %collective-permute-done.1 = f32[2,6,128,128]{3,2,0,1:T(8,128)} collective-permute-done((f32[2,6,128,128]{3,2,0,1:T(8,128)S(1)}, f32[2,6,128,128]{3,2,0,1:T(8,128)}, u32[]{:S(2)}, u32[]{:S(2)}) %collective-permute-start.1) | collective-permute-done | bytes 786464 | tf_op jit(solution)/shard_map/ppermute | solution.py:29
  113.5 4.6 %collective-permute-done.3 = f32[2,6,128,128]{3,2,0,1:T(8,128)} collective-permute-done((f32[2,6,128,128]{3,2,0,1:T(8,128)}, f32[2,6,128,128]{3,2,0,1:T(8,128)}, u32[]{:S(2)}, u32[]{:S(2)}) %collective-permute-start.3) | collective-permute-done | bytes 786464 | tf_op jit(solution)/shard_map/ppermute | solution.py:29
  118.1 2.4 fusion.27
  120.6 38.3 %while.22 = (s32[]{:T(128)}, f32[3072,128]{1,0:T(8,128)S(1)}, s32[]{:T(128)}, s32[2,6,128]{2,0,1:T(2,128)}, f32[2,6,128,128]{3,2,0,1:T(8,128)}, /*index=5*/f32[2...) while((s32[]{:T(128)}, f32[3072,128]{1,0:T(8,128)S(1)}, s32[]{:T(128)}, ...), condition=%wide.region_4.6_spmd.clone, body=%wide.region_2.0_spmd.clone.sunk | while | flops 50398216 | bytes 790719 | solution.py:112
  122.1 1.9 convolution_multiply_fusion.4
  124.0 2.9 scatter_fusion
  130.2 2.9 scatter_fusion
  134.6 1.9 convolution_multiply_fusion.4
  136.5 2.9 scatter_fusion
  142.7 2.9 scatter_fusion
  148.9 2.9 scatter_fusion
  155.2 2.9 scatter_fusion
  158.9 7.2 %fusion.20 = f32[2,384,128]{2,1,0:T(8,128)} fusion(f32[2,384,128]{2,1,0:T(8,128)} %param.16, f32[2,1536,128]{2,1,0:T(8,128)S(1)} %copy-done.1, f32[2,384,1536]{2,1,0:T(8,128)} %param.17, f32[2,1536,128]{2,1,0:T(8,128)S(1)} %bitcast.132, s32[]{:T(128)S(6)} %select_n.41), kind=kOutput, calls=%fused_computation.40 | convolution fusion | flops 1812234240 | bytes 7471108 | tf_op jit(solution)/shard_map/slm,smc->slc/dot_general | solution.py:93
  166.1 2.1 fusion.33
  168.9 18.1 %reduce-scatter.5.cloned.1.call-done = f32[48,128]{1,0:T(8,128)} async-done(((f32[192,128]{1,0:T(8,128)}), f32[48,128]{1,0:T(8,128)}) %reduce-scatter.5.cloned.1.call-update) | async-done | bytes 24592 | tf_op jit(solution)/shard_map/reduce_scatter | solution.py:79
  187.0 17.1 %all_gather.29 = f32[768,128]{1,0:T(8,128)S(1)} all-gather(f32[48,128]{1,0:T(8,128)} %reduce-scatter.5.cloned.1.call-done), channel_id=1, replica_groups=mesh['sub'=4,'crow'=4,'ccol'=2] {'sub','crow'}, dimensions={0}, use_global_device_ids=true | all-gather | bytes 417792 | tf_op jit(solution)/shard_map/all_gather | solution.py:82
  204.5 5.3 %all_gather.30 = f32[192,128]{1,0:T(8,128)S(1)} all-gather(f32[48,128]{1,0:T(8,128)S(1)} %convolution_bitcast_fusion.3), channel_id=1, replica_groups=mesh['sub'=4,'crow'=4,'ccol'=2] {'crow'}, dimensions={0}, use_global_device_ids=true | all-gather | bytes 122880 | tf_op jit(solution)/shard_map/all_gather | solution.py:85
  209.9 6.7 %fusion.32 = f32[2,128,384]{1,2,0:T(8,128)S(1)} fusion(f32[2,1536,128]{2,1,0:T(8,128)} %all-gather.9.cloned.1.call-done, f32[2,384,1536]{2,1,0:T(8,128)} %param.18), kind=kOutput, calls=%fused_computation.88 | convolution fusion | flops 1811939328 | bytes 6684672 | tf_op jit(solution)/shard_map/slm,smc->slc/dot_general | solution.py:71
  218.3 22.0 %all-gather.11.cloned.1.call-done = f32[2,1536,128]{2,1,0:T(8,128)} async-done(((f32[2,384,128]{2,1,0:T(8,128)}), f32[2,1536,128]{2,1,0:T(8,128)}) %all-gather.11.cloned.1.call-update) | async-done | bytes 1572880 | tf_op jit(solution)/shard_map/all_gather | solution.py:92
  240.2 4.1 %gather_fusion.5 = f32[1536,128]{1,0:T(8,128)S(1)} fusion(f32[3072,128]{1,0:T(8,128)} %bitcast.128, s32[2048]{0:T(1024)S(1)} %pad_clamp_fusion), kind=kCustom, calls=%fused_computation.5.clone | custom fusion | bytes 1579008 | tf_op jit(solution)/shard_map/jit(_take)/gather | solution.py:40
  244.4 2.6 gather_fusion.4
  248.7 3.4 %collective-permute-start.4 = (f32[2,6,128,128]{3,2,0,1:T(8,128)}, f32[2,6,128,128]{3,2,0,1:T(8,128)}, u32[]{:S(2)}, u32[]{:S(2)}) collective-permute-start(f32[2,6,128,128]{3,2,0,1:T(8,128)} %copy_multiply_fusion.1), channel_id=1, source_target_pairs={{0,8},{8,16},{16,24},{1,9},{9,17},{17,25},{2,10},{10,18},{18,26},{... | collective-permute-start | bytes 2359304 | tf_op jit(solution)/shard_map/ppermute | solution.py:29
  252.1 2.5 collective-permute-start.5
  254.5 2.6 gather_fusion.3
  257.4 13.2 %collective-permute-done.4 = f32[2,6,128,128]{3,2,0,1:T(8,128)} collective-permute-done((f32[2,6,128,128]{3,2,0,1:T(8,128)}, f32[2,6,128,128]{3,2,0,1:T(8,128)}, u32[]{:S(2)}, u32[]{:S(2)}) %collective-permute-start.4) | collective-permute-done | bytes 786464 | tf_op jit(solution)/shard_map/ppermute | solution.py:29
  270.6 2.9 collective-permute-done.5
  273.5 2.4 fusion.25
  276.0 38.3 %while.23 = (s32[]{:T(128)}, f32[3072,128]{1,0:T(8,128)S(1)}, s32[]{:T(128)}, s32[2,6,128]{2,0,1:T(2,128)}, f32[2,6,128,128]{3,2,0,1:T(8,128)}, /*index=5*/f32[2...) while((s32[]{:T(128)}, f32[3072,128]{1,0:T(8,128)S(1)}, s32[]{:T(128)}, ...), condition=%wide.region_8.10_spmd.clone, body=%wide.region_6.9_spmd.clone.sunk | while | flops 50398216 | bytes 790719 | solution.py:112
  279.6 2.9 scatter_fusion.1
  285.8 2.9 scatter_fusion.1
  292.1 2.9 scatter_fusion.1
  298.3 2.9 scatter_fusion.1
  304.5 2.9 scatter_fusion.1
  310.8 2.9 scatter_fusion.1
  314.3 7.2 %fusion.23 = f32[2,384,128]{2,1,0:T(8,128)} fusion(f32[2,384,128]{2,1,0:T(8,128)} %fusion.20, f32[2,1536,128]{2,1,0:T(8,128)S(1)} %copy-done.2, f32[2,384,1536]{2,1,0:T(8,128)} %param.17, f32[2,1536,128]{2,1,0:T(8,128)S(1)} %bitcast.131, s32[]{:T(128)S(6)} %select_n.41), kind=kOutput, calls=%fused_computation.43 | convolution fusion | flops 1812234240 | bytes 7471108 | tf_op jit(solution)/shard_map/slm,smc->slc/dot_general | solution.py:93
  (130 shorter events, 42.6 us)
Async XLA Ops:
  7.2 1.0 copy-start
  7.2 11.6 %copy-start.7 = (s32[2,6,128]{2,0,1:T(2,128)S(1)}, s32[2,6,128]{2,0,1:T(2,128)}, u32[]{:S(2)}) copy-start(s32[2,6,128]{2,0,1:T(2,128)} %param.23) | copy-start | bytes 18436
  7.2 11.3 %copy-start.8 = (s32[2,6]{1,0:T(2,128)S(1)}, s32[2,6]{1,0:T(2,128)}, u32[]{:S(2)}) copy-start(s32[2,6]{1,0:T(2,128)} %param.24) | copy-start | bytes 148
  7.2 11.6 %copy-start.4 = (f32[2,6,128,128]{3,2,1,0:T(8,128)S(1)}, f32[2,6,128,128]{3,2,1,0:T(8,128)}, u32[]{:S(2)}) copy-start(f32[2,6,128,128]{3,2,1,0:T(8,128)} %param.21) | copy-start | bytes 2359300
  7.2 12.6 %copy-start.9 = (s32[2]{0:T(128)S(1)}, s32[2]{0:T(128)}, u32[]{:S(2)}) copy-start(s32[2]{0:T(128)} %param.25) | copy-start | bytes 28
  7.2 24.5 %reduce-scatter.3.cloned.1.call-start = ((), (), s32[]{:S(2)}) async-start(), calls=%async_computation.3 | async-start | bytes 122880 | tf_op jit(solution)/shard_map/reduce_scatter | solution.py:79
  10.2 38.5 %copy-start.5 = (f32[48,768]{1,0:T(8,128)S(1)}, f32[48,768]{1,0:T(8,128)}, u32[]{:S(2)}) copy-start(f32[48,768]{1,0:T(8,128)} %param.20) | copy-start | bytes 442372
  10.3 44.2 %all-gather.5.cloned.1.call-start = ((), (), s32[]{:S(2)}) async-start(), calls=%async_computation.2 | async-start | bytes 1966080 | tf_op jit(solution)/shard_map/all_gather | solution.py:74
  11.0 73.6 %all-gather.7.cloned.1.call-start = ((), (), s32[]{:S(2)}) async-start(), calls=%async_computation.4 | async-start | bytes 1966080 | tf_op jit(solution)/shard_map/all_gather | solution.py:92
  12.6 50.0 %collective-permute-start.2 = (s32[2,6,129]{1,0,2:T(2,128)S(1)}, s32[2,6,129]{1,0,2:T(2,128)S(1)}, u32[]{:S(2)}, u32[]{:S(2)}) collective-permute-start(s32[2,6,129]{1,0,2:T(2,128)S(1)} %pad_add_fusion), channel_id=1, source_target_pairs={{0,8},{8,16},{16,24},{1,9},{9,17},{17,25},{2,10},{10,18},{18,26},{... | collective-permute-start | bytes 18584 | tf_op jit(solution)/shard_map/ppermute | solution.py:20
  16.1 46.8 %collective-permute-start = (s32[2,6,129]{1,0,2:T(2,128)S(1)}, s32[2,6,129]{1,0,2:T(2,128)S(1)}, u32[]{:S(2)}, u32[]{:S(2)}) collective-permute-start(s32[2,6,129]{1,0,2:T(2,128)S(1)} %pad_add_fusion), channel_id=1, source_target_pairs={{8,0},{16,8},{24,16},{9,1},{17,9},{25,17},{10,2},{18,10},{26,18},{... | collective-permute-start | bytes 18584 | tf_op jit(solution)/shard_map/ppermute | solution.py:21
  62.6 124.4 %reduce-scatter.5.cloned.1.call-start = ((), (), s32[]{:S(2)}) async-start(), calls=%async_computation.6 | async-start | bytes 122880 | tf_op jit(solution)/shard_map/reduce_scatter | solution.py:79
  84.7 4.1 %copy-start.1 = (f32[2,1536,128]{2,1,0:T(8,128)S(1)}, f32[2,1536,128]{2,1,0:T(8,128)}, u32[]{:S(2)}) copy-start(f32[2,1536,128]{2,1,0:T(8,128)} %all-gather.7.cloned.1.call-done) | copy-start | bytes 4718596
  91.8 21.7 %collective-permute-start.1 = (f32[2,6,128,128]{3,2,0,1:T(8,128)S(1)}, f32[2,6,128,128]{3,2,0,1:T(8,128)}, u32[]{:S(2)}, u32[]{:S(2)}) collective-permute-start(f32[2,6,128,128]{3,2,0,1:T(8,128)S(1)} %copy_multiply_fusion.4), channel_id=1, source_target_pairs={{0,8},{8,16},{16,24},{1,9},{9,17},{17,25},{2,10},{10,18},{18,26},{... | collective-permute-start | bytes 2359304 | tf_op jit(solution)/shard_map/ppermute | solution.py:29
  96.5 21.6 %collective-permute-start.3 = (f32[2,6,128,128]{3,2,0,1:T(8,128)}, f32[2,6,128,128]{3,2,0,1:T(8,128)}, u32[]{:S(2)}, u32[]{:S(2)}) collective-permute-start(f32[2,6,128,128]{3,2,0,1:T(8,128)} %copy_multiply_fusion.3), channel_id=1, source_target_pairs={{8,0},{16,8},{24,16},{9,1},{17,9},{25,17},{10,2},{18,10},{26,18},{... | collective-permute-start | bytes 2359304 | tf_op jit(solution)/shard_map/ppermute | solution.py:29
  166.1 38.1 %copy-start.6 = (f32[48,768]{1,0:T(8,128)S(1)}, f32[48,768]{1,0:T(8,128)}, u32[]{:S(2)}) copy-start(f32[48,768]{1,0:T(8,128)} %param.20) | copy-start | bytes 442372
  168.2 41.6 %all-gather.9.cloned.1.call-start = ((), (), s32[]{:S(2)}) async-start(), calls=%async_computation.5 | async-start | bytes 1966080 | tf_op jit(solution)/shard_map/all_gather | solution.py:74
  168.8 71.4 %all-gather.11.cloned.1.call-start = ((), (), s32[]{:S(2)}) async-start(), calls=%async_computation.7 | async-start | bytes 1966080 | tf_op jit(solution)/shard_map/all_gather | solution.py:92
  209.8 6.7 %copy-start.3 = (f32[2,384,128]{2,1,0:T(8,128)S(1)}, f32[2,384,128]{2,1,0:T(8,128)}, u32[]{:S(2)}) copy-start(f32[2,384,128]{2,1,0:T(8,128)} %fusion.17) | copy-start | bytes 1179652
  240.2 4.1 %copy-start.2 = (f32[2,1536,128]{2,1,0:T(8,128)S(1)}, f32[2,1536,128]{2,1,0:T(8,128)}, u32[]{:S(2)}) copy-start(f32[2,1536,128]{2,1,0:T(8,128)} %all-gather.11.cloned.1.call-done) | copy-start | bytes 4718596
  248.7 21.9 %collective-permute-start.4 = (f32[2,6,128,128]{3,2,0,1:T(8,128)}, f32[2,6,128,128]{3,2,0,1:T(8,128)}, u32[]{:S(2)}, u32[]{:S(2)}) collective-permute-start(f32[2,6,128,128]{3,2,0,1:T(8,128)} %copy_multiply_fusion.1), channel_id=1, source_target_pairs={{0,8},{8,16},{16,24},{1,9},{9,17},{17,25},{2,10},{10,18},{18,26},{... | collective-permute-start | bytes 2359304 | tf_op jit(solution)/shard_map/ppermute | solution.py:29
  252.1 21.4 %collective-permute-start.5 = (f32[2,6,128,128]{3,2,0,1:T(8,128)S(1)}, f32[2,6,128,128]{3,2,0,1:T(8,128)}, u32[]{:S(2)}, u32[]{:S(2)}) collective-permute-start(f32[2,6,128,128]{3,2,0,1:T(8,128)S(1)} %copy_multiply_fusion), channel_id=1, source_target_pairs={{8,0},{16,8},{24,16},{9,1},{17,9},{25,17},{10,2},{18,10},{26,18},{... | collective-permute-start | bytes 2359304 | tf_op jit(solution)/shard_map/ppermute | solution.py:29
Sparse Core Ops, SparseCore 0:
  11.1 20.5 reduce-scatter.2
  33.2 20.7 all-gather.4
  62.8 21.8 all-gather.6
  168.4 18.6 reduce-scatter.4
  188.4 20.7 all-gather.8
  218.4 21.8 all-gather.10
where the time goes:
time: 331 us; the launch traced here: 328 us
  waiting for transfers between devices  106 us (32%)
  matrix products  58.5 us (18%)
  other arithmetic  54 us (16%)
  blocking collectives  44.9 us (14%)
  local copies, waits for them, and re-layouts  22.1 us (7%)
  starting transfers between devices  17.7 us (5%)
  between operations  14.5 us (4%)
  loops' own time  10.3 us (3%)
    all_gather x2, waiting for transfers between devices, per_device(): full_corr = lax.all_gather(correction, 'crow', axis=1, tiled=True)  43.3 us
    scatter-add x12, other arithmetic, add_slot(): return inflow.at[target_rows].add(slot_terms * active_flag[:, None, None])  34.4 us
    all_gather x2, blocking collectives, per_device(): lax.all_gather(group_share, ('sub', 'crow'), axis=0, tiled=True)  34.2 us
    ppermute x4, waiting for transfers between devices, from_behind(): return lax.ppermute(block, axis, route)  32.3 us
    reduce_scatter x2, waiting for transfers between devices, per_device(): lax.psum_scatter(restricted, 'crow', scatter_dimension=0, tiled=True)  29.3 us
    dot_general x12, matrix products, add_slot(): jnp.einsum('snm,smc->snc', coupling[:, slot_index], sources, precision=hi...  22.7 us
    gather x6, local copies, waits for them, and re-layouts, take_requested(): jnp.take(full_corr.reshape(-1, case_count), flat_rows.reshape(-1), axis=0)  18.6 us
    dot_general x2, matrix products, per_device(): jnp.einsum('slm,smc->slc', stiffness, full_corr, precision=highest_mode)  14.4 us
  transfers between devices with their start and end apart: 12, of which 8 were waited for; matrix products, arithmetic and copies ran while one was open for 6% of the time, Pallas kernels for 0%

commit v1 on v0

v1 whole, which is shorter than its diff:
```python
import jax
import jax.numpy as jnp
from jax import lax
from jax.experimental import pallas as pl
from jax.experimental.pallas import tpu as pltpu
from jax.sharding import PartitionSpec as P

ITERS = 2
damping = 0.7
f32 = jnp.float32
bf16 = jnp.bfloat16
MIB = 2**20
IN_VMEM = pl.BlockSpec(memory_space=pltpu.VMEM)
IN_SMEM = pl.BlockSpec(memory_space=pltpu.SMEM)


def call(kernel, name, operands, outputs, micros, scalars=0, scratch=(), limit=8):
    return pl.pallas_call(
        kernel,
        in_specs=[IN_SMEM] * scalars + [IN_VMEM] * (len(operands) - scalars),
        out_specs=[IN_VMEM] * len(outputs),
        out_shape=[jax.ShapeDtypeStruct(shape, kind) for shape, kind in outputs],
        scratch_shapes=list(scratch),
        compiler_params=pltpu.CompilerParams(vmem_limit_bytes=limit * MIB),
        cost_estimate=pl.CostEstimate(
            flops=0, bytes_accessed=int(micros * 3.6e6), transcendentals=0
        ),
        name=name,
    )(*operands)


def parts(x):
    hi = x.astype(bf16)
    return hi, (x - hi.astype(f32)).astype(bf16)


def beside(x):
    hi, lo = parts(x)
    return jnp.concatenate([hi, lo], axis=1)


def stacked(x):
    hi, lo = parts(x)
    return jnp.concatenate([hi, lo], axis=0)


def dot(a, b):
    return jnp.dot(a, b, preferred_element_type=f32)


def sides(product):
    columns = product.shape[1] // 2
    return product[:, :columns] + product[:, columns:]


def folded(product):
    rows = product.shape[0] // 2
    return sides(product[:rows] + product[rows:])


def exchange(x, axis, bit):
    size = lax.axis_size(axis)
    return lax.ppermute(x, axis, [(i, i ^ bit) for i in range(size) if (i ^ bit) < size])


def split_matrix(matrix, crow_index, name):
    subs, rows, order = matrix.shape

    def kernel(index, m, o):
        s, q = pl.program_id(0), pl.program_id(1)
        o[s, :, pl.ds(pl.multiple_of(q * rows, rows), rows)] = stacked(m[0])

    return pl.pallas_call(
        kernel,
        grid_spec=pltpu.PrefetchScalarGridSpec(
            num_scalar_prefetch=1,
            grid=(subs, order // rows),
            in_specs=[pl.BlockSpec((1, rows, rows), lambda s, q, index: (s, 0, index[0] ^ q))],
            out_specs=IN_VMEM,
        ),
        out_shape=jax.ShapeDtypeStruct((subs, 2 * rows, order), bf16),
        compiler_params=pltpu.CompilerParams(vmem_limit_bytes=8 * MIB),
        cost_estimate=pl.CostEstimate(
            flops=0, bytes_accessed=int(2.5 * 3.6e6), transcendentals=0
        ),
        name=name,
    )(crow_index.reshape(1), matrix)


def place_coarse(pieces, y_index, crow_index):
    basis_pieces = [p[0] for p in pieces]
    inverse_pieces = [p[1] for p in pieces]
    subs, modes, rows = basis_pieces[0].shape
    own_rows, columns = inverse_pieces[0].shape
    blocks = [p[2] for p in pieces]
    halves = [p[3] for p in pieces]
    count = max(blocks) + 1
    order = rows * count
    place = jnp.stack([y_index, crow_index])

    def kernel(at, *refs):
        basis_refs = refs[: len(pieces)]
        inverse_refs = refs[len(pieces) : 2 * len(pieces)]
        down, up, inverse = refs[2 * len(pieces) :]
        for b_ref, i_ref, q, half in zip(basis_refs, inverse_refs, blocks, halves):
            here = slice(q * rows, (q + 1) * rows)
            held = b_ref.shape[0]
            first = 0 if half is None else (at[0] if half == 0 else 1 - at[0]) * held
            for i in range(held):
                value = b_ref[i]
                down[first + i, :, here] = stacked(value)
                up[first + i, here] = beside(value.T)
            height = i_ref.shape[0]
            start = 0 if half is None else (at[0] if half == 0 else 1 - at[0]) * height
            inverse[at[1] ^ q, pl.ds(start, height)] = i_ref[...]

    return call(
        kernel,
        "place_coarse",
        [place] + basis_pieces + inverse_pieces,
        [
            ((subs, 2 * modes, order), bf16),
            ((subs, order, 2 * modes), bf16),
            ((count, own_rows, columns), f32),
        ],
        1.0,
        scalars=1,
    )


def split_targets(targets, order):
    subs, slots, width = targets.shape

    def kernel(tg, o):
        line = lax.broadcasted_iota(jnp.int32, (order, width), 0)
        for s in range(subs):
            for k in range(slots):
                hit = (line == tg[s, k : k + 1, :]).astype(f32).astype(bf16)
                o[s, :, k * width : (k + 1) * width] = hit

    return call(kernel, "split_targets", [targets], [((subs, order, slots * width), bf16)], 1.3)[0]


def own_part_restricted(basis, residual):
    subs, modes, rows = basis.shape
    cases = residual.shape[2]

    def kernel(z, r, o):
        for s in range(subs):
            o[s] = folded(dot(stacked(z[s]), beside(r[s])))

    return call(kernel, "own_part_restricted", [basis, residual], [((subs, modes, cases), f32)], 0.4)[0]


def load(ref, s):
    return ref[s] if len(ref.shape) == 3 else ref[...]


def local_solve(s, split, blocks):
    rows = split.shape[1] // 2
    order = split.shape[2]
    cases = blocks[0].shape[-1]

    def kernel(m, *refs):
        o, rhs = refs[-2:]
        for q, ref in enumerate(refs[:-2]):
            rhs[q * rows : (q + 1) * rows] = beside(load(ref, s))
        o[...] = folded(dot(m[s], rhs[...]))

    return call(
        kernel,
        "local_solve",
        [split, *blocks],
        [((rows, cases), f32)],
        0.8,
        scratch=[pltpu.VMEM((order, 2 * cases), bf16)],
    )[0]


def choose_terms(flag, mine, other, terms, width):
    slots = mine.shape[0]

    @pl.when(flag == 1)
    def _():
        for k in range(slots):
            terms[k * width : (k + 1) * width] = beside(mine[k])

    @pl.when(flag == 0)
    def _():
        for k in range(slots):
            terms[k * width : (k + 1) * width] = beside(other[k])


def local_solve_inflow(s, split, basis, blocks, hits, mine, other, flag):
    rows = split.shape[1] // 2
    order = split.shape[2]
    cases = blocks[0].shape[-1]
    modes = basis.shape[1] // 2
    slots, width = mine.shape[:2]
    count = len(blocks)

    def kernel(flag_ref, m, z, tg, g_mine, g_other, *refs):
        o, restricted, own, rhs, terms = refs[count:]
        choose_terms(flag_ref[s], g_mine, g_other, terms, width)
        for q, ref in enumerate(refs[:count]):
            here = slice(q * rows, (q + 1) * rows)
            r = ref[...] + damping * sides(dot(tg[s, here], terms[...]))
            if q == 0:
                own[...] = r
            rhs[here] = beside(r)
        restricted[...] = folded(dot(z[s], rhs[...]))
        o[...] = folded(dot(m[s], rhs[...]))

    return call(
        kernel,
        "local_solve_inflow",
        [flag, split, basis, hits, mine, other, *blocks],
        [((rows, cases), f32), ((modes, cases), f32), ((rows, cases), f32)],
        1.5,
        scalars=1,
        scratch=[
            pltpu.VMEM((order, 2 * cases), bf16),
            pltpu.VMEM((slots * width, 2 * cases), bf16),
        ],
    )


def correct(s, split, lift, inverse, place, mine, other, blocks, residual, old):
    rows = split.shape[1] // 2
    order = split.shape[2]
    cases = blocks[0].shape[-1]
    modes = lift.shape[2] // 2
    groups, half = mine.shape[:2]
    per_sub = inverse.shape[0] // split.shape[0]
    count = len(blocks)
    columns = inverse.shape[2]

    def kernel(at, m, z, c, g_mine, g_other, res, *refs):
        old_refs = refs[count : len(refs) - 4]
        o, total, corr, right = refs[len(refs) - 4 :]
        for b in range(groups):
            base = (at[0] ^ b) * (2 * half)
            right[pl.ds(pl.multiple_of(base + at[1] * half, half), half)] = beside(g_mine[b])
            right[pl.ds(pl.multiple_of(base + (1 - at[1]) * half, half), half)] = beside(g_other[b])
        c_rows = c[s * per_sub : (s + 1) * per_sub].reshape(modes, columns)
        coarse = beside(folded(dot(stacked(c_rows), right[...])))
        coarse = jnp.concatenate([coarse, coarse], axis=0)
        for q, ref in enumerate(refs[:count]):
            here = slice(q * rows, (q + 1) * rows)
            value = ref[...] + sides(dot(z[s, here], coarse))
            corr[here] = beside(value)
            if q == 0:
                total[...] = damping * value + old_refs[0][...] if old_refs else damping * value
        o[...] = load(res, s) - damping * folded(dot(m[s], corr[...]))

    return call(
        kernel,
        "correct",
        [place, split, lift, inverse, mine, other, residual, *blocks] + ([] if old is None else [old]),
        [((rows, cases), f32), ((rows, cases), f32), ((order, 2 * cases), bf16)],
        1.2,
        scalars=1,
        scratch=[pltpu.VMEM((columns, 2 * cases), bf16)],
        limit=12,
    )


def select_rows(where, lists, corrs):
    ways, slots, width = lists.shape
    order, twice = corrs[0].shape
    cases = twice // 2

    def kernel(where_ref, l, *refs):
        corr_refs = refs[: len(corrs)]
        outs = refs[len(corrs) :]
        lane = lax.broadcasted_iota(jnp.int32, (width, order), 1)
        for d in range(ways):

            @pl.loop(0, slots)
            def _(k):
                place = where_ref[d * slots + k]

                @pl.when(place < 0)
                def _():
                    outs[d][k] = jnp.zeros((width, cases), f32)

                for s, ref in enumerate(corr_refs):

                    @pl.when(place == s)
                    def _():
                        rows = jnp.broadcast_to(l[d, pl.ds(k, 1), :], (width, width)).T
                        rows = jnp.concatenate([rows] * (order // width), axis=1)
                        one = (rows == lane).astype(f32).astype(bf16)
                        outs[d][k] = sides(dot(one, ref[...]))

    return call(
        kernel,
        "select_rows",
        [where, lists, *corrs],
        [((slots, width, cases), f32)] * ways,
        1.5,
        scalars=1,
    )


def couple(codes, core, coupling, sources):
    slots, width = coupling.shape[1:3]
    cases = sources[0].shape[2]

    def kernel(codes_ref, core_ref, c, *refs):
        source_refs = refs[: len(sources)]
        out = refs[len(sources)]

        @pl.loop(0, slots)
        def _(k):
            code = codes_ref[k]

            @pl.when(code < 0)
            def _():
                out[k] = jnp.zeros((width, cases), f32)

            for d, ref in enumerate(source_refs):

                @pl.when(code == d)
                def _():
                    out[k] = folded(dot(stacked(c[core_ref[0], k]), beside(ref[k])))

    return call(
        kernel,
        "couple",
        [codes, core.reshape(1), coupling, *sources],
        [((slots, width, cases), f32)],
        0.8,
        scalars=2,
    )[0]


def add_inflow(residuals, hits, mine, other, flag):
    subs = hits.shape[0]
    slots, width = mine.shape[:2]
    rows, cases = residuals[0].shape

    def kernel(flag_ref, tg, g_mine, g_other, *refs):
        out, terms = refs[subs:]
        for s in range(subs):
            choose_terms(flag_ref[s], g_mine, g_other, terms, width)
            out[s] = refs[s][...] + damping * sides(dot(tg[s, :rows], terms[...]))

    return call(
        kernel,
        "add_inflow",
        [flag, hits, mine, other, *residuals],
        [((subs, rows, cases), f32)],
        0.8,
        scalars=1,
        scratch=[pltpu.VMEM((slots * width, 2 * cases), bf16)],
    )[0]


def coarse_pieces(basis, inverse, y_index):
    copies, size = lax.axis_size("ccol"), lax.axis_size("crow")
    pieces = [(basis, inverse, 0, None)]
    bit = size // 2
    while bit >= 1:
        news = []
        for z, c, q, half in pieces:
            if bit > 1 and copies == 2 and half is None:
                zh, ch = z.shape[0] // 2, c.shape[0] // 2
                z = exchange(lax.dynamic_slice_in_dim(z, y_index * zh, zh, 0), "crow", bit)
                c = exchange(lax.dynamic_slice_in_dim(c, y_index * ch, ch, 0), "crow", bit)
                news.append((z, c, q | bit, 0))
                news.append((exchange(z, "ccol", 1), exchange(c, "ccol", 1), q | bit, 1))
            else:
                news.append((exchange(z, "crow", bit), exchange(c, "crow", bit), q | bit, half))
        pieces = pieces + news
        bit //= 2
    return pieces


def gathered(x):
    bit = lax.axis_size("crow") // 2
    blocks = {0: x}
    while bit >= 1:
        blocks.update({q | bit: exchange(b, "crow", bit) for q, b in blocks.items()})
        bit //= 2
    return [blocks[q] for q in sorted(blocks)]


def spread_over_sub(half):
    half = half[None]
    bit = 1
    while bit < lax.axis_size("sub"):
        half = jnp.concatenate([half, exchange(half, "sub", bit)], axis=0)
        bit *= 2
    return half, exchange(half, "crow", 1)


def pair_routes(size):
    low = [(i, i + 1) for i in range(0, size - 1, 2)]
    high = [(i, i + 1) for i in range(1, size - 1, 2)]
    return [[p for a, b in pairs for p in ((a, b), (b, a))] for pairs in (low, high)]


def per_device(
    load_cases,
    stiffness,
    local_inverse,
    coarse_basis,
    coarse_inverse,
    coupling,
    target_local_rows,
    neighbour_read_rows,
    neighbour,
    counts,
):
    subs, rows, cases = load_cases.shape
    modes = coarse_basis.shape[1]
    slots = neighbour.shape[1]
    width = coupling.shape[3]
    groups = lax.axis_size("sub")
    crow_size = lax.axis_size("crow")
    group = lax.axis_index("sub")
    crow_index = lax.axis_index("crow")
    core = crow_index % 2
    y_index = lax.axis_index("ccol")
    half_subs = subs // 2

    first_blocks = gathered(load_cases)

    share = own_part_restricted(coarse_basis, load_cases)
    keep = lax.dynamic_slice_in_dim(share, core * half_subs, half_subs, 0)
    give = lax.dynamic_slice_in_dim(share, (1 - core) * half_subs, half_subs, 0)
    keep = (keep + exchange(give, "crow", 1)).reshape(half_subs * modes, cases)
    bit = 2
    while bit < crow_size:
        keep = keep + exchange(keep, "crow", bit)
        bit *= 2
    mine, other = spread_over_sub(keep)

    packed = jnp.concatenate(
        [
            neighbour_read_rows.reshape(subs * slots, width),
            jnp.pad(neighbour.reshape(1, subs * slots), ((0, 0), (0, width - subs * slots))),
            jnp.pad(counts.reshape(1, subs), ((0, 0), (0, width - subs))),
        ],
        axis=0,
    )
    routes = pair_routes(groups)
    all_lists = [packed] + [lax.ppermute(packed, "sub", route) for route in routes]
    slot = jnp.arange(slots, dtype=jnp.int32)
    wheres, lists = [], []
    for held in all_lists:
        reads = lax.dynamic_slice_in_dim(
            held[: subs * slots].reshape(subs, slots, width), core * half_subs, half_subs, 0
        ).reshape(half_subs * slots, width)
        ids = held[subs * slots, : subs * slots].reshape(subs, slots)
        limits = held[subs * slots + 1, :subs]
        place = ids - group * subs
        use = (slot[None, :] < limits[:, None]) & (place >= 0) & (place < subs)
        place = lax.dynamic_slice_in_dim(jnp.where(use, place, -1), core * half_subs, half_subs, 0)
        wheres.append(place.reshape(-1))
        lists.append(((reads // rows) ^ crow_index) * rows + reads % rows)
    where = jnp.concatenate(wheres)
    lists = jnp.stack(lists)
    source_group = neighbour // subs
    code = jnp.where(source_group == group, 0, jnp.where(source_group == (group ^ 1), 1, 2))
    active = slot[None, :] < counts[:, None]
    code = jnp.where(active, code, -1)
    codes = lax.dynamic_slice_in_dim(code, core * half_subs, half_subs, 0).reshape(-1)
    targets = ((target_local_rows // rows) ^ crow_index) * rows + target_local_rows % rows
    hits = split_targets(jnp.where(active[:, :, None], targets, -1), crow_size * rows)
    flag = (jnp.arange(subs, dtype=jnp.int32) // half_subs == core).astype(jnp.int32)
    place = jnp.stack([group, core])

    inverse_split = split_matrix(local_inverse, crow_index, "split_inverse")
    stiffness_split = split_matrix(stiffness, crow_index, "split_stiffness")
    down, lift, inverse = place_coarse(
        coarse_pieces(coarse_basis, coarse_inverse, y_index), y_index, crow_index
    )

    totals, residuals = [None] * subs, [load_cases] * subs
    local = [local_solve(s, inverse_split, first_blocks) for s in range(subs)]
    for sweep_index in range(ITERS):
        local_blocks = [gathered(v) for v in local]
        steps = [
            correct(
                s, stiffness_split, lift, inverse, place, mine, other,
                local_blocks[s], residuals[s], totals[s],
            )
            for s in range(subs)
        ]
        passed, totals, corrs = zip(*steps)
        chosen = select_rows(where, lists, corrs)
        sources = [chosen[0]] + [lax.ppermute(c, "sub", route) for c, route in zip(chosen[1:], routes)]
        terms = couple(codes, core, coupling, sources)
        other_terms = exchange(terms, "crow", 1)
        if sweep_index == ITERS - 1:
            return jnp.stack(totals), add_inflow(passed, hits, terms, other_terms, flag)
        steps = [
            local_solve_inflow(
                s, inverse_split, down, gathered(passed[s]), hits, terms, other_terms, flag
            )
            for s in range(subs)
        ]
        local, restricted, residuals = zip(*steps)
        keep = lax.dynamic_slice_in_dim(jnp.stack(restricted), core * half_subs, half_subs, 0)
        mine, other = spread_over_sub(keep.reshape(half_subs * modes, cases))


def solution(mesh):
    return jax.shard_map(
        per_device,
        mesh=mesh,
        in_specs=(
            P("sub", "crow", "ccol"),
            P("sub", "crow", None),
            P("sub", "crow", None),
            P("sub", None, "crow"),
            P(("sub", "crow"), None),
            P("sub", None, None, None),
            P("sub", None, None),
            P("sub", None, None),
            P("sub", None),
            P("sub"),
        ),
        out_specs=(P("sub", "crow", "ccol"), P("sub", "crow", "ccol")),
        check_vma=False,
    )
```

time: 331 us -> 127 us (0.38)
  waiting for transfers between devices: 106 us -> 44.4 us
  matrix products: 58.5 us -> 0 us
  other arithmetic: 54 us -> 2.88 us
  blocking collectives: 44.9 us -> 0 us
  Pallas kernels: 0 us -> 31.4 us
  starting transfers between devices: 17.7 us -> 31.5 us
  between operations: 14.5 us -> 1.28 us
  loops' own time: 10.3 us -> 0 us
  local copies, waits for them, and re-layouts: 22.1 us -> 14.5 us
    dot_general x22 -> x0, matrix products: 58.5 us -> none  [the longest x12 22.7 us: add_slot(): jnp.einsum('snm,smc->snc', coupling[:, slot_index], sources, precision=hi...]
    all_gather x4 -> x0, blocking collectives: 44.9 us -> none  [the longest x2 34.2 us: per_device(): lax.all_gather(group_share, ('sub', 'crow'), axis=0, tiled=True)]
    all_gather x4 -> x0, waiting for transfers between devices: 43.3 us -> none  [the longest x2 43.3 us: per_device(): full_corr = lax.all_gather(correction, 'crow', axis=1, tiled=True)]
    scatter-add x12 -> x0, other arithmetic: 34.4 us -> none  [add_slot(): return inflow.at[target_rows].add(slot_terms * active_flag[:, None, None])]
    pallas_call x0 -> x18, Pallas kernels: none -> 31.4 us  [the longest x16 28.5 us: call(): pl.pallas_call(kernel, in_specs=[IN_SMEM] * scalars + [IN_VMEM] * (len(op...]
    reduce_scatter x2 -> x0, waiting for transfers between devices: 29.3 us -> none  [per_device(): lax.psum_scatter(restricted, 'crow', scatter_dimension=0, tiled=True)]
    gather x6 -> x0, local copies, waits for them, and re-layouts: 18.6 us -> none  [take_requested(): jnp.take(full_corr.reshape(-1, case_count), flat_rows.reshape(-1), axis=0)]
    ppermute x6 -> x47, starting transfers between devices: 17.5 us -> 31.5 us  [the longest x41 22.8 us: exchange(): lax.ppermute(x, axis, [(i, i ^ bit) for i in range(size) if i ^ bit < size])]
  transfers between devices with their start and end apart: 12 -> 47, of which waited for: 8 -> 14; matrix products, arithmetic and copies ran while one was open for 6% -> 5% of each run, Pallas kernels for 0% -> 12%
where the time goes in v1:
time: 127 us; the launch traced here: 126 us
  waiting for transfers between devices  44.4 us (35%)
  starting transfers between devices  31.5 us (25%)
  Pallas kernels  31.4 us (25%)
  local copies, waits for them, and re-layouts  14.5 us (11%)
  other arithmetic  2.88 us (2%)
  between operations  1.28 us (1%)
    pallas_call x16, Pallas kernels, call(): pl.pallas_call(kernel, in_specs=[IN_SMEM] * scalars + [IN_VMEM] * (len(op...  28.5 us
    ppermute x41, waiting for transfers between devices, exchange(): lax.ppermute(x, axis, [(i, i ^ bit) for i in range(size) if i ^ bit < size])  27.6 us
    ppermute x41, starting transfers between devices, exchange(): lax.ppermute(x, axis, [(i, i ^ bit) for i in range(size) if i ^ bit < size])  22.8 us
    ppermute x4, waiting for transfers between devices, per_device(): lax.ppermute(c, 'sub', route)  16.7 us
    unnamed x35, local copies, waits for them, and re-layouts  11.7 us
    ppermute x4, starting transfers between devices, per_device(): lax.ppermute(c, 'sub', route)  6.32 us
    pallas_call x2, Pallas kernels, split_matrix(): pl.pallas_call(kernel, grid_spec=pltpu.PrefetchScalarGridSpec(num_scalar_...  2.84 us
  transfers between devices with their start and end apart: 47, of which 14 were waited for; matrix products, arithmetic and copies ran while one was open for 5% of the time, Pallas kernels for 12%

profile of v1, /device:TPU:16, one launch (start us, length us, event | category | flops | bytes accessed | tf_op | source)
XLA Modules:
  0.0 125.9 jit_solution(7812183084053479586)
XLA Ops:
  0.6 1.6 %collective-permute-start.18 = (f32[2,384,128]{2,1,0:T(8,128)}, f32[2,384,128]{2,1,0:T(8,128)S(1)}, u32[]{:S(2)}, u32[]{:S(2)}) collective-permute-start(f32[2,384,128]{2,1,0:T(8,128)} %res.3), channel_id=1, source_target_pairs={{0,4},{2,6},{4,0},{6,2},{1,5},{3,7},{5,1},{7,3},{8,12},{10,14},{12... | collective-permute-start | bytes 1179656 | tf_op jit(solution)/shard_map/ppermute | solution.py:63
  4.3 2.3 %collective-permute-start.11 = (s32[14,128]{1,0:T(8,128)S(1)}, s32[14,128]{1,0:T(8,128)S(1)}, u32[]{:S(2)}, u32[]{:S(2)}) collective-permute-start(s32[14,128]{1,0:T(8,128)S(1)} %pad_add_fusion.1), channel_id=1, source_target_pairs={{8,16},{16,8},{9,17},{17,9},{10,18},{18,10},{11,19},{19,11},{12,20... | collective-permute-start | bytes 21512 | tf_op jit(solution)/shard_map/ppermute | solution.py:449
  6.8 1.0 copy-done.3
  7.8 1.0 copy-done.8
  9.3 0.9 constant_dynamic-slice_fusion.6
  12.1 2.3 %copy-done.5 = f32[2,384,1536]{2,1,0:T(8,128)S(1)} copy-done((f32[2,384,1536]{2,1,0:T(8,128)S(1)}, f32[2,384,1536]{2,1,0:T(8,128)}, u32[]{:S(2)}) %copy-start.5) | copy-done | bytes 4718616
  14.4 1.4 %split_inverse.1.m = bf16[2,768,1536]{2,1,0:T(8,128)(2,1)S(1)} custom-call(s32[1]{0:T(128)} %bitcast.2.index, f32[2,384,1536]{2,1,0:T(8,128)S(1)} %copy-done.5), custom_call_target="tpu_custom_call" | custom-call | bytes 9000000 | tf_op jit(solution)/shard_map/split_inverse/pallas_call | solution.py:73
  15.8 2.2 %copy-done.1 = bf16[2,768,1536]{2,1,0:T(8,128)(2,1)} copy-done((bf16[2,768,1536]{2,1,0:T(8,128)(2,1)}, bf16[2,768,1536]{2,1,0:T(8,128)(2,1)S(1)}, u32[]{:S(2)}) %copy-start.1) | copy-done | bytes 4718616
  18.0 1.4 %split_stiffness.1.m = bf16[2,768,1536]{2,1,0:T(8,128)(2,1)S(1)} custom-call(s32[1]{0:T(128)} %bitcast.2.index, f32[2,384,1536]{2,1,0:T(8,128)S(1)} %copy-done.6), custom_call_target="tpu_custom_call" | custom-call | bytes 9000000 | tf_op jit(solution)/shard_map/split_stiffness/pallas_call | solution.py:73
  19.5 2.2 %copy-done = bf16[2,768,1536]{2,1,0:T(8,128)(2,1)} copy-done((bf16[2,768,1536]{2,1,0:T(8,128)(2,1)}, bf16[2,768,1536]{2,1,0:T(8,128)(2,1)S(1)}, u32[]{:S(2)}) %copy-start) | copy-done | bytes 4718616
  22.3 1.5 %collective-permute-start = (f32[1,96,384]{2,1,0:T(8,128)S(1)}, f32[1,96,384]{2,1,0:T(8,128)S(1)}, u32[]{:S(2)}, u32[]{:S(2)}) collective-permute-start(f32[1,96,384]{2,1,0:T(8,128)S(1)} %constant_dynamic-slice_fusion.6), channel_id=1, source_target_pairs={{0,4},{2,6},{4,0},{6,2},{1,5},{3,7},{5,1},{7,3},{8,12},{10,14},{12... | collective-permute-start | bytes 442376 | tf_op jit(solution)/shard_map/ppermute | solution.py:63
  24.6 2.2 %collective-permute-done.5.refs_7_ = f32[24,768]{1,0:T(8,128)S(1)} collective-permute-done((f32[24,768]{1,0:T(8,128)S(1)}, f32[24,768]{1,0:T(8,128)S(1)}, u32[]{:S(2)}, u32[]{:S(2)}) %collective-permute-start.5) | collective-permute-done | bytes 73760 | tf_op jit(solution)/shard_map/ppermute | solution.py:63
  26.7 1.5 %collective-permute-start.6 = (f32[24,768]{1,0:T(8,128)S(1)}, f32[24,768]{1,0:T(8,128)S(1)}, u32[]{:S(2)}, u32[]{:S(2)}) collective-permute-start(f32[24,768]{1,0:T(8,128)S(1)} %collective-permute-done.5.refs_7_), channel_id=1, source_target_pairs={{0,1},{1,0},{2,3},{3,2},{4,5},{5,4},{6,7},{7,6},{8,9},{9,8},{10,11... | collective-permute-start | bytes 221192 | tf_op jit(solution)/shard_map/ppermute | solution.py:63
  28.3 2.0 %collective-permute-done.13 = f32[96,128]{1,0:T(8,128)S(1)} collective-permute-done((f32[96,128]{1,0:T(8,128)S(1)}, f32[96,128]{1,0:T(8,128)S(1)}, u32[]{:S(2)}, u32[]{:S(2)}) %collective-permute-start.13) | collective-permute-done | bytes 49184 | tf_op jit(solution)/shard_map/ppermute | solution.py:63
  30.3 2.1 %collective-permute-start.14 = (f32[1,96,128]{2,1,0:T(8,128)S(1)}, f32[1,96,128]{2,1,0:T(8,128)S(1)}, u32[]{:S(2)}, u32[]{:S(2)}) collective-permute-start(f32[1,96,128]{2,1,0:T(8,128)S(1)} %add_bitcast_fusion), channel_id=1, source_target_pairs={{0,8},{8,0},{16,24},{24,16},{1,9},{9,1},{17,25},{25,17},{2,10},{10... | collective-permute-start | bytes 147464 | tf_op jit(solution)/shard_map/ppermute | solution.py:63
  32.4 2.0 %collective-permute-done.14 = f32[1,96,128]{2,1,0:T(8,128)S(1)} collective-permute-done((f32[1,96,128]{2,1,0:T(8,128)S(1)}, f32[1,96,128]{2,1,0:T(8,128)S(1)}, u32[]{:S(2)}, u32[]{:S(2)}) %collective-permute-start.14) | collective-permute-done | bytes 49184 | tf_op jit(solution)/shard_map/ppermute | solution.py:63
  35.0 1.5 %collective-permute-start.1 = (f32[1,96,384]{2,1,0:T(8,128)S(1)}, f32[1,96,384]{2,1,0:T(8,128)S(1)}, u32[]{:S(2)}, u32[]{:S(2)}) collective-permute-start(f32[1,96,384]{2,1,0:T(8,128)S(1)} %collective-permute-done.refs_1_), channel_id=1, source_target_pairs={{0,1},{1,0},{2,3},{3,2},{4,5},{5,4},{6,7},{7,6},{8,9},{9,8},{10,11... | collective-permute-start | bytes 442376 | tf_op jit(solution)/shard_map/ppermute | solution.py:63
  36.6 3.1 %collective-permute-start.15 = (f32[2,96,128]{2,1,0:T(8,128)S(1)}, f32[2,96,128]{2,1,0:T(8,128)S(1)}, u32[]{:S(2)}, u32[]{:S(2)}) collective-permute-start(f32[2,96,128]{2,1,0:T(8,128)S(1)} %pad_maximum_fusion.3), channel_id=1, source_target_pairs={{0,16},{8,24},{16,0},{24,8},{1,17},{9,25},{17,1},{25,9},{2,18},{10... | collective-permute-start | bytes 294920 | tf_op jit(solution)/shard_map/ppermute | solution.py:63
  39.9 2.3 %copy-done.2 = bf16[2,768,1536]{2,1,0:T(8,128)(2,1)S(1)} copy-done((bf16[2,768,1536]{2,1,0:T(8,128)(2,1)S(1)}, bf16[2,768,1536]{2,1,0:T(8,128)(2,1)}, u32[]{:S(2)}) %copy-start.2) | copy-done | bytes 4718616
  44.9 1.5 %collective-permute-start.21 = (f32[384,128]{1,0:T(8,128)S(1)}, f32[384,128]{1,0:T(8,128)S(1)}, u32[]{:S(2)}, u32[]{:S(2)}) collective-permute-start(f32[384,128]{1,0:T(8,128)S(1)} %local_solve.2.refs_0_), channel_id=1, source_target_pairs={{0,4},{2,6},{4,0},{6,2},{1,5},{3,7},{5,1},{7,3},{8,12},{10,14},{12... | collective-permute-start | bytes 589832 | tf_op jit(solution)/shard_map/ppermute | solution.py:63
  47.1 5.0 %collective-permute-done.24.refs_2_ = f32[384,128]{1,0:T(8,128)S(1)} collective-permute-done((f32[384,128]{1,0:T(8,128)S(1)}, f32[384,128]{1,0:T(8,128)S(1)}, u32[]{:S(2)}, u32[]{:S(2)}) %collective-permute-start.24) | collective-permute-done | bytes 196640 | tf_op jit(solution)/shard_map/ppermute | solution.py:63
  52.1 3.6 %collective-permute-done.21.refs_2_ = f32[384,128]{1,0:T(8,128)S(1)} collective-permute-done((f32[384,128]{1,0:T(8,128)S(1)}, f32[384,128]{1,0:T(8,128)S(1)}, u32[]{:S(2)}, u32[]{:S(2)}) %collective-permute-start.21) | collective-permute-done | bytes 196640 | tf_op jit(solution)/shard_map/ppermute | solution.py:63
  55.8 1.3 %place_coarse.1 = (bf16[2,192,1536]{2,1,0:T(8,128)(2,1)S(1)}, bf16[2,1536,192]{2,1,0:T(8,128)(2,1)S(1)}, f32[4,48,768]{2,1,0:T(8,128)S(1)}) custom-call(s32[2]{0:T(128)S(1)} %pad_add_fusion.4.at, f32[2,96,384]{2,1,0:T(8,128)S(1)} %copy-done.9, f32[1,96,384]{2,1,0:T(8,128)S(1)} %collective-permute-done.refs_1_, ...), custom_call_target="tpu_custom_call" | custom-call | bytes 3600000 | tf_op jit(solution)/shard_map/place_coarse/pallas_call | solution.py:18
  57.2 2.0 %correct.5 = (f32[384,128]{1,0:T(8,128)S(1)}, f32[384,128]{1,0:T(8,128)S(1)}, bf16[1536,256]{1,0:T(8,128)(2,1)S(1)}) custom-call(s32[2]{0:T(128)S(1)} %pad_add_fusion.3.at, bf16[2,768,1536]{2,1,0:T(8,128)(2,1)S(1)} %bitcast.28, bf16[2,1536,192]{2,1,0:T(8,128)(2,1)S(1)} %get-tuple-element.29.z, f32[4,48,768]{2,1,0:T(8,128)S(1)} %get-tuple-element.30.c, ...), custom_call_target="tpu_custom_call" | custom-call | bytes 4320000 | tf_op jit(solution)/shard_map/correct/pallas_call | solution.py:18
  59.3 2.0 %correct.4 = (f32[384,128]{1,0:T(8,128)S(1)}, f32[384,128]{1,0:T(8,128)S(1)}, bf16[1536,256]{1,0:T(8,128)(2,1)S(1)}) custom-call(s32[2]{0:T(128)S(1)} %pad_add_fusion.3.at, bf16[2,768,1536]{2,1,0:T(8,128)(2,1)S(1)} %bitcast.28, bf16[2,1536,192]{2,1,0:T(8,128)(2,1)S(1)} %get-tuple-element.29.z, f32[4,48,768]{2,1,0:T(8,128)S(1)} %get-tuple-element.30.c, ...), custom_call_target="tpu_custom_call" | custom-call | bytes 4320000 | tf_op jit(solution)/shard_map/correct/pallas_call | solution.py:18
  61.3 2.9 %select_rows.2 = (f32[6,128,128]{2,1,0:T(8,128)S(1)}, f32[6,128,128]{2,1,0:T(8,128)S(1)}, f32[6,128,128]{2,1,0:T(8,128)S(1)}) custom-call(s32[18]{0:T(128)S(1)} %pad_add_fusion.5.where_ref, s32[3,6,128]{2,1,0:T(8,128)S(1)} %pad_add_fusion.l, bf16[1536,256]{1,0:T(8,128)(2,1)S(1)} %get-tuple-element.32.refs_0_, bf16[1536,256]{1,0:T(8,128)(2,1)S(1)} %get-tuple-element.33.refs_1_), custom_call_target="tpu_custom_call" | custom-call | bytes 5400000 | tf_op jit(solution)/shard_map/select_rows/pallas_call | solution.py:18
  64.3 2.4 %collective-permute-start.27 = (f32[6,128,128]{2,1,0:T(8,128)S(1)}, f32[6,128,128]{2,1,0:T(8,128)S(1)}, u32[]{:S(2)}, u32[]{:S(2)}) collective-permute-start(f32[6,128,128]{2,1,0:T(8,128)S(1)} %get-tuple-element.36), channel_id=1, source_target_pairs={{8,16},{16,8},{9,17},{17,9},{10,18},{18,10},{11,19},{19,11},{12,20... | collective-permute-start | bytes 1179656 | tf_op jit(solution)/shard_map/ppermute | solution.py:494
  67.3 1.5 %collective-permute-start.30 = (f32[384,128]{1,0:T(8,128)S(1)}, f32[384,128]{1,0:T(8,128)S(1)}, u32[]{:S(2)}, u32[]{:S(2)}) collective-permute-start(f32[384,128]{1,0:T(8,128)S(1)} %get-tuple-element.37.refs_0_), channel_id=1, source_target_pairs={{0,4},{2,6},{4,0},{6,2},{1,5},{3,7},{5,1},{7,3},{8,12},{10,14},{12... | collective-permute-start | bytes 589832 | tf_op jit(solution)/shard_map/ppermute | solution.py:63
  68.8 5.7 %collective-permute-done.26.refs_1_ = f32[6,128,128]{2,1,0:T(8,128)S(1)} collective-permute-done((f32[6,128,128]{2,1,0:T(8,128)S(1)}, f32[6,128,128]{2,1,0:T(8,128)S(1)}, u32[]{:S(2)}, u32[]{:S(2)}) %collective-permute-start.26) | collective-permute-done | bytes 393248 | tf_op jit(solution)/shard_map/ppermute | solution.py:494
  74.5 1.9 %collective-permute-done.27.refs_2_ = f32[6,128,128]{2,1,0:T(8,128)S(1)} collective-permute-done((f32[6,128,128]{2,1,0:T(8,128)S(1)}, f32[6,128,128]{2,1,0:T(8,128)S(1)}, u32[]{:S(2)}, u32[]{:S(2)}) %collective-permute-start.27) | collective-permute-done | bytes 393248 | tf_op jit(solution)/shard_map/ppermute | solution.py:494
  76.4 1.7 %couple.2.g_mine = f32[6,128,128]{2,1,0:T(8,128)S(1)} custom-call(s32[6]{0:T(128)S(1)} %fusion.23.codes_ref, s32[1]{0:T(128)} %bitcast.1.core_ref, f32[2,6,128,128]{3,2,1,0:T(8,128)S(1)} %copy-done.7, f32[6,128,128]{2,1,0:T(8,128)S(1)} %get-tuple-element.34.refs_0_, f32[6,128,128]{2,1,0:T(8,128)S(1)} %collective-permute-done.26.refs_1_, ...), custom_call_target="tpu_custom_call" | custom-call | bytes 2880000 | tf_op jit(solution)/shard_map/couple/pallas_call | solution.py:18
  79.5 1.3 %split_targets.1.tg = bf16[2,1536,768]{2,1,0:T(8,128)(2,1)S(1)} custom-call(s32[2,6,128]{2,1,0:T(8,128)S(1)} %fusion.7.tg), custom_call_target="tpu_custom_call" | custom-call | bytes 4680000 | tf_op jit(solution)/shard_map/split_targets/pallas_call | solution.py:18
  80.9 2.2 %local_solve_inflow.3 = (f32[384,128]{1,0:T(8,128)S(1)}, f32[96,128]{1,0:T(8,128)S(1)}, f32[384,128]{1,0:T(8,128)S(1)}) custom-call(s32[2]{0:T(128)S(1)} %compare_convert_fusion.flag_ref, bf16[2,768,1536]{2,1,0:T(8,128)(2,1)S(1)} %bitcast.30, bf16[2,192,1536]{2,1,0:T(8,128)(2,1)S(1)} %get-tuple-element.31.z, bf16[2,1536,768]{2,1,0:T(8,128)(2,1)S(1)} %split_targets.1.tg, ...), custom_call_target="tpu_custom_call" | custom-call | bytes 5400000 | tf_op jit(solution)/shard_map/local_solve_inflow/pallas_call | solution.py:18
  83.1 2.3 %local_solve_inflow.2 = (f32[384,128]{1,0:T(8,128)S(1)}, f32[96,128]{1,0:T(8,128)S(1)}, f32[384,128]{1,0:T(8,128)S(1)}) custom-call(s32[2]{0:T(128)S(1)} %compare_convert_fusion.flag_ref, bf16[2,768,1536]{2,1,0:T(8,128)(2,1)S(1)} %bitcast.30, bf16[2,192,1536]{2,1,0:T(8,128)(2,1)S(1)} %get-tuple-element.31.z, bf16[2,1536,768]{2,1,0:T(8,128)(2,1)S(1)} %split_targets.1.tg, ...), custom_call_target="tpu_custom_call" | custom-call | bytes 5400000 | tf_op jit(solution)/shard_map/local_solve_inflow/pallas_call | solution.py:18
  85.5 4.1 %collective-permute-done.35 = f32[1,96,128]{2,1,0:T(8,128)S(1)} collective-permute-done((f32[1,96,128]{2,1,0:T(8,128)S(1)}, f32[1,96,128]{2,1,0:T(8,128)S(1)}, u32[]{:S(2)}, u32[]{:S(2)}) %collective-permute-start.35) | collective-permute-done | bytes 49184 | tf_op jit(solution)/shard_map/ppermute | solution.py:63
  90.3 1.5 %collective-permute-start.42 = (f32[384,128]{1,0:T(8,128)S(1)}, f32[384,128]{1,0:T(8,128)S(1)}, u32[]{:S(2)}, u32[]{:S(2)}) collective-permute-start(f32[384,128]{1,0:T(8,128)S(1)} %get-tuple-element.46.refs_0_), channel_id=1, source_target_pairs={{0,4},{2,6},{4,0},{6,2},{1,5},{3,7},{5,1},{7,3},{8,12},{10,14},{12... | collective-permute-start | bytes 589832 | tf_op jit(solution)/shard_map/ppermute | solution.py:63
  91.8 3.5 %collective-permute-done.36 = f32[2,96,128]{2,1,0:T(8,128)S(1)} collective-permute-done((f32[2,96,128]{2,1,0:T(8,128)S(1)}, f32[2,96,128]{2,1,0:T(8,128)S(1)}, u32[]{:S(2)}, u32[]{:S(2)}) %collective-permute-start.36) | collective-permute-done | bytes 98336 | tf_op jit(solution)/shard_map/ppermute | solution.py:63
  95.4 2.2 %collective-permute-done.39.refs_2_ = f32[384,128]{1,0:T(8,128)S(1)} collective-permute-done((f32[384,128]{1,0:T(8,128)S(1)}, f32[384,128]{1,0:T(8,128)S(1)}, u32[]{:S(2)}, u32[]{:S(2)}) %collective-permute-start.39) | collective-permute-done | bytes 196640 | tf_op jit(solution)/shard_map/ppermute | solution.py:63
  98.1 2.0 %collective-permute-done.42.refs_2_ = f32[384,128]{1,0:T(8,128)S(1)} collective-permute-done((f32[384,128]{1,0:T(8,128)S(1)}, f32[384,128]{1,0:T(8,128)S(1)}, u32[]{:S(2)}, u32[]{:S(2)}) %collective-permute-start.42) | collective-permute-done | bytes 196640 | tf_op jit(solution)/shard_map/ppermute | solution.py:63
  100.1 2.0 %correct.6 = (f32[384,128]{1,0:T(8,128)S(1)}, f32[384,128]{1,0:T(8,128)S(1)}, bf16[1536,256]{1,0:T(8,128)(2,1)S(1)}) custom-call(s32[2]{0:T(128)S(1)} %pad_add_fusion.3.at, bf16[2,768,1536]{2,1,0:T(8,128)(2,1)S(1)} %bitcast.28, bf16[2,1536,192]{2,1,0:T(8,128)(2,1)S(1)} %get-tuple-element.29.z, f32[4,48,768]{2,1,0:T(8,128)S(1)} %get-tuple-element.30.c, ...), custom_call_target="tpu_custom_call" | custom-call | bytes 4320000 | tf_op jit(solution)/shard_map/correct/pallas_call | solution.py:18
  102.2 2.0 %correct.7 = (f32[384,128]{1,0:T(8,128)S(1)}, f32[384,128]{1,0:T(8,128)S(1)}, bf16[1536,256]{1,0:T(8,128)(2,1)S(1)}) custom-call(s32[2]{0:T(128)S(1)} %pad_add_fusion.3.at, bf16[2,768,1536]{2,1,0:T(8,128)(2,1)S(1)} %bitcast.28, bf16[2,1536,192]{2,1,0:T(8,128)(2,1)S(1)} %get-tuple-element.29.z, f32[4,48,768]{2,1,0:T(8,128)S(1)} %get-tuple-element.30.c, ...), custom_call_target="tpu_custom_call" | custom-call | bytes 4320000 | tf_op jit(solution)/shard_map/correct/pallas_call | solution.py:18
  104.2 2.9 %select_rows.3 = (f32[6,128,128]{2,1,0:T(8,128)S(1)}, f32[6,128,128]{2,1,0:T(8,128)S(1)}, f32[6,128,128]{2,1,0:T(8,128)S(1)}) custom-call(s32[18]{0:T(128)S(1)} %pad_add_fusion.5.where_ref, s32[3,6,128]{2,1,0:T(8,128)S(1)} %pad_add_fusion.l, bf16[1536,256]{1,0:T(8,128)(2,1)S(1)} %get-tuple-element.49.refs_0_, bf16[1536,256]{1,0:T(8,128)(2,1)S(1)} %get-tuple-element.50.refs_1_), custom_call_target="tpu_custom_call" | custom-call | bytes 5400000 | tf_op jit(solution)/shard_map/select_rows/pallas_call | solution.py:18
  107.2 3.8 %collective-permute-start.45 = (f32[6,128,128]{2,1,0:T(8,128)S(1)}, f32[6,128,128]{2,1,0:T(8,128)S(1)}, u32[]{:S(2)}, u32[]{:S(2)}) collective-permute-start(f32[6,128,128]{2,1,0:T(8,128)S(1)} %get-tuple-element.53), channel_id=1, source_target_pairs={{8,16},{16,8},{9,17},{17,9},{10,18},{18,10},{11,19},{19,11},{12,20... | collective-permute-start | bytes 1179656 | tf_op jit(solution)/shard_map/ppermute | solution.py:494
  111.0 6.4 %collective-permute-done.44.refs_1_ = f32[6,128,128]{2,1,0:T(8,128)S(1)} collective-permute-done((f32[6,128,128]{2,1,0:T(8,128)S(1)}, f32[6,128,128]{2,1,0:T(8,128)S(1)}, u32[]{:S(2)}, u32[]{:S(2)}) %collective-permute-start.44) | collective-permute-done | bytes 393248 | tf_op jit(solution)/shard_map/ppermute | solution.py:494
  117.4 2.7 %collective-permute-done.45.refs_2_ = f32[6,128,128]{2,1,0:T(8,128)S(1)} collective-permute-done((f32[6,128,128]{2,1,0:T(8,128)S(1)}, f32[6,128,128]{2,1,0:T(8,128)S(1)}, u32[]{:S(2)}, u32[]{:S(2)}) %collective-permute-start.45) | collective-permute-done | bytes 393248 | tf_op jit(solution)/shard_map/ppermute | solution.py:494
  120.0 1.7 %couple.3.g_mine = f32[6,128,128]{2,1,0:T(8,128)S(1)} custom-call(s32[6]{0:T(128)S(1)} %fusion.23.codes_ref, s32[1]{0:T(128)} %bitcast.1.core_ref, f32[2,6,128,128]{3,2,1,0:T(8,128)S(1)} %copy-done.7, f32[6,128,128]{2,1,0:T(8,128)S(1)} %get-tuple-element.51.refs_0_, f32[6,128,128]{2,1,0:T(8,128)S(1)} %collective-permute-done.44.refs_1_, ...), custom_call_target="tpu_custom_call" | custom-call | bytes 2880000 | tf_op jit(solution)/shard_map/couple/pallas_call | solution.py:18
  122.6 0.9 collective-permute-done.46.g_other
  123.6 2.3 %add_inflow.1 = f32[2,384,128]{2,1,0:T(8,128)} custom-call(s32[2]{0:T(128)S(1)} %compare_convert_fusion.flag_ref, bf16[2,1536,768]{2,1,0:T(8,128)(2,1)S(1)} %split_targets.1.tg, f32[6,128,128]{2,1,0:T(8,128)S(1)} %couple.3.g_mine, f32[6,128,128]{2,1,0:T(8,128)S(1)} %collective-permute-done.46.g_other, f32[384,128]{1,0:T(8,128)S(1)} %get-tuple-element.54.refs_0_, ...), custom_call_target="tpu_custom_call" | custom-call | bytes 2880000 | tf_op jit(solution)/shard_map/add_inflow/pallas_call | solution.py:18
  (138 shorter events, 14.7 us)
Async XLA Ops:
  0.6 27.6 %collective-permute-start.18 = (f32[2,384,128]{2,1,0:T(8,128)}, f32[2,384,128]{2,1,0:T(8,128)S(1)}, u32[]{:S(2)}, u32[]{:S(2)}) collective-permute-start(f32[2,384,128]{2,1,0:T(8,128)} %res.3), channel_id=1, source_target_pairs={{0,4},{2,6},{4,0},{6,2},{1,5},{3,7},{5,1},{7,3},{8,12},{10,14},{12... | collective-permute-start | bytes 1179656 | tf_op jit(solution)/shard_map/ppermute | solution.py:63
  2.2 34.4 %collective-permute-start.17 = (f32[2,384,128]{2,1,0:T(8,128)}, f32[2,384,128]{2,1,0:T(8,128)S(1)}, u32[]{:S(2)}, u32[]{:S(2)}) collective-permute-start(f32[2,384,128]{2,1,0:T(8,128)} %res.3), channel_id=1, source_target_pairs={{0,2},{2,0},{4,6},{6,4},{1,3},{3,1},{5,7},{7,5},{8,10},{10,8},{12,... | collective-permute-start | bytes 1179656 | tf_op jit(solution)/shard_map/ppermute | solution.py:63
  4.3 17.3 %collective-permute-start.11 = (s32[14,128]{1,0:T(8,128)S(1)}, s32[14,128]{1,0:T(8,128)S(1)}, u32[]{:S(2)}, u32[]{:S(2)}) collective-permute-start(s32[14,128]{1,0:T(8,128)S(1)} %pad_add_fusion.1), channel_id=1, source_target_pairs={{8,16},{16,8},{9,17},{17,9},{10,18},{18,10},{11,19},{19,11},{12,20... | collective-permute-start | bytes 21512 | tf_op jit(solution)/shard_map/ppermute | solution.py:449
  6.7 15.6 %collective-permute-start.10 = (s32[14,128]{1,0:T(8,128)S(1)}, s32[14,128]{1,0:T(8,128)S(1)}, u32[]{:S(2)}, u32[]{:S(2)}) collective-permute-start(s32[14,128]{1,0:T(8,128)S(1)} %pad_add_fusion.1), channel_id=1, source_target_pairs={{0,8},{8,0},{16,24},{24,16},{1,9},{9,1},{17,25},{25,17},{2,10},{10... | collective-permute-start | bytes 21512 | tf_op jit(solution)/shard_map/ppermute | solution.py:449
  9.0 14.8 %collective-permute-start.12 = (f32[1,96,128]{2,1,0:T(8,128)S(1)}, f32[1,96,128]{2,1,0:T(8,128)S(1)}, u32[]{:S(2)}, u32[]{:S(2)}) collective-permute-start(f32[1,96,128]{2,1,0:T(8,128)S(1)} %constant_dynamic-slice_fusion), channel_id=1, source_target_pairs={{0,2},{2,0},{4,6},{6,4},{1,3},{3,1},{5,7},{7,5},{8,10},{10,8},{12,... | collective-permute-start | bytes 147464 | tf_op jit(solution)/shard_map/ppermute | solution.py:63
  18.0 21.9 %copy-start.4 = (f32[2,384,128]{2,1,0:T(8,128)S(1)}, f32[2,384,128]{2,1,0:T(8,128)}, u32[]{:S(2)}) copy-start(f32[2,384,128]{2,1,0:T(8,128)} %res.3) | copy-start | bytes 1179652
  21.6 5.1 %collective-permute-start.5 = (f32[24,768]{1,0:T(8,128)S(1)}, f32[24,768]{1,0:T(8,128)S(1)}, u32[]{:S(2)}, u32[]{:S(2)}) collective-permute-start(f32[24,768]{1,0:T(8,128)S(1)} %constant_dynamic-slice_fusion.5), channel_id=1, source_target_pairs={{0,4},{2,6},{4,0},{6,2},{1,5},{3,7},{5,1},{7,3},{8,12},{10,14},{12... | collective-permute-start | bytes 221192 | tf_op jit(solution)/shard_map/ppermute | solution.py:63
  22.3 12.7 %collective-permute-start = (f32[1,96,384]{2,1,0:T(8,128)S(1)}, f32[1,96,384]{2,1,0:T(8,128)S(1)}, u32[]{:S(2)}, u32[]{:S(2)}) collective-permute-start(f32[1,96,384]{2,1,0:T(8,128)S(1)} %constant_dynamic-slice_fusion.6), channel_id=1, source_target_pairs={{0,4},{2,6},{4,0},{6,2},{1,5},{3,7},{5,1},{7,3},{8,12},{10,14},{12... | collective-permute-start | bytes 442376 | tf_op jit(solution)/shard_map/ppermute | solution.py:63
  23.9 6.4 %collective-permute-start.13 = (f32[96,128]{1,0:T(8,128)S(1)}, f32[96,128]{1,0:T(8,128)S(1)}, u32[]{:S(2)}, u32[]{:S(2)}) collective-permute-start(f32[96,128]{1,0:T(8,128)S(1)} %add_bitcast_fusion.1), channel_id=1, source_target_pairs={{0,4},{2,6},{4,0},{6,2},{1,5},{3,7},{5,1},{7,3},{8,12},{10,14},{12... | collective-permute-start | bytes 147464 | tf_op jit(solution)/shard_map/ppermute | solution.py:63
  26.7 7.7 %collective-permute-start.6 = (f32[24,768]{1,0:T(8,128)S(1)}, f32[24,768]{1,0:T(8,128)S(1)}, u32[]{:S(2)}, u32[]{:S(2)}) collective-permute-start(f32[24,768]{1,0:T(8,128)S(1)} %collective-permute-done.5.refs_7_), channel_id=1, source_target_pairs={{0,1},{1,0},{2,3},{3,2},{4,5},{5,4},{6,7},{7,6},{8,9},{9,8},{10,11... | collective-permute-start | bytes 221192 | tf_op jit(solution)/shard_map/ppermute | solution.py:63
  28.3 11.4 %collective-permute-start.19 = (f32[2,384,128]{2,1,0:T(8,128)S(1)}, f32[2,384,128]{2,1,0:T(8,128)S(1)}, u32[]{:S(2)}, u32[]{:S(2)}) collective-permute-start(f32[2,384,128]{2,1,0:T(8,128)S(1)} %collective-permute-done.18.refs_2_), channel_id=1, source_target_pairs={{0,2},{2,0},{4,6},{6,4},{1,3},{3,1},{5,7},{7,5},{8,10},{10,8},{12,... | collective-permute-start | bytes 1179656 | tf_op jit(solution)/shard_map/ppermute | solution.py:63
  30.3 4.2 %collective-permute-start.14 = (f32[1,96,128]{2,1,0:T(8,128)S(1)}, f32[1,96,128]{2,1,0:T(8,128)S(1)}, u32[]{:S(2)}, u32[]{:S(2)}) collective-permute-start(f32[1,96,128]{2,1,0:T(8,128)S(1)} %add_bitcast_fusion), channel_id=1, source_target_pairs={{0,8},{8,0},{16,24},{24,16},{1,9},{9,1},{17,25},{25,17},{2,10},{10... | collective-permute-start | bytes 147464 | tf_op jit(solution)/shard_map/ppermute | solution.py:63
  34.5 9.3 %collective-permute-start.7 = (f32[48,768]{1,0:T(8,128)S(1)}, f32[48,768]{1,0:T(8,128)S(1)}, u32[]{:S(2)}, u32[]{:S(2)}) collective-permute-start(f32[48,768]{1,0:T(8,128)S(1)} %copy-done.10), channel_id=1, source_target_pairs={{0,2},{2,0},{4,6},{6,4},{1,3},{3,1},{5,7},{7,5},{8,10},{10,8},{12,... | collective-permute-start | bytes 442376 | tf_op jit(solution)/shard_map/ppermute | solution.py:63
  34.5 2.0 %collective-permute-start.8 = (f32[24,768]{1,0:T(8,128)S(1)}, f32[24,768]{1,0:T(8,128)S(1)}, u32[]{:S(2)}, u32[]{:S(2)}) collective-permute-start(f32[24,768]{1,0:T(8,128)S(1)} %collective-permute-done.5.refs_7_), channel_id=1, source_target_pairs={{0,2},{2,0},{4,6},{6,4},{1,3},{3,1},{5,7},{7,5},{8,10},{10,8},{12,... | collective-permute-start | bytes 221192 | tf_op jit(solution)/shard_map/ppermute | solution.py:63
  35.0 9.2 %collective-permute-start.1 = (f32[1,96,384]{2,1,0:T(8,128)S(1)}, f32[1,96,384]{2,1,0:T(8,128)S(1)}, u32[]{:S(2)}, u32[]{:S(2)}) collective-permute-start(f32[1,96,384]{2,1,0:T(8,128)S(1)} %collective-permute-done.refs_1_), channel_id=1, source_target_pairs={{0,1},{1,0},{2,3},{3,2},{4,5},{5,4},{6,7},{7,6},{8,9},{9,8},{10,11... | collective-permute-start | bytes 442376 | tf_op jit(solution)/shard_map/ppermute | solution.py:63
  36.5 10.0 %collective-permute-start.2 = (f32[2,96,384]{2,1,0:T(8,128)S(1)}, f32[2,96,384]{2,1,0:T(8,128)S(1)}, u32[]{:S(2)}, u32[]{:S(2)}) collective-permute-start(f32[2,96,384]{2,1,0:T(8,128)S(1)} %copy-done.9), channel_id=1, source_target_pairs={{0,2},{2,0},{4,6},{6,4},{1,3},{3,1},{5,7},{7,5},{8,10},{10,8},{12,... | collective-permute-start | bytes 884744 | tf_op jit(solution)/shard_map/ppermute | solution.py:63
  36.6 8.3 %collective-permute-start.15 = (f32[2,96,128]{2,1,0:T(8,128)S(1)}, f32[2,96,128]{2,1,0:T(8,128)S(1)}, u32[]{:S(2)}, u32[]{:S(2)}) collective-permute-start(f32[2,96,128]{2,1,0:T(8,128)S(1)} %pad_maximum_fusion.3), channel_id=1, source_target_pairs={{0,16},{8,24},{16,0},{24,8},{1,17},{9,25},{17,1},{25,9},{2,18},{10... | collective-permute-start | bytes 294920 | tf_op jit(solution)/shard_map/ppermute | solution.py:63
  39.7 4.7 %collective-permute-start.9 = (f32[24,768]{1,0:T(8,128)S(1)}, f32[24,768]{1,0:T(8,128)S(1)}, u32[]{:S(2)}, u32[]{:S(2)}) collective-permute-start(f32[24,768]{1,0:T(8,128)S(1)} %collective-permute-done.6.refs_8_), channel_id=1, source_target_pairs={{0,2},{2,0},{4,6},{6,4},{1,3},{3,1},{5,7},{7,5},{8,10},{10,8},{12,... | collective-permute-start | bytes 221192 | tf_op jit(solution)/shard_map/ppermute | solution.py:63
  43.8 2.6 %collective-permute-start.3 = (f32[1,96,384]{2,1,0:T(8,128)S(1)}, f32[1,96,384]{2,1,0:T(8,128)S(1)}, u32[]{:S(2)}, u32[]{:S(2)}) collective-permute-start(f32[1,96,384]{2,1,0:T(8,128)S(1)} %collective-permute-done.refs_1_), channel_id=1, source_target_pairs={{0,2},{2,0},{4,6},{6,4},{1,3},{3,1},{5,7},{7,5},{8,10},{10,8},{12,... | collective-permute-start | bytes 442376 | tf_op jit(solution)/shard_map/ppermute | solution.py:63
  44.2 2.8 %collective-permute-start.4 = (f32[1,96,384]{2,1,0:T(8,128)S(1)}, f32[1,96,384]{2,1,0:T(8,128)S(1)}, u32[]{:S(2)}, u32[]{:S(2)}) collective-permute-start(f32[1,96,384]{2,1,0:T(8,128)S(1)} %collective-permute-done.1.refs_2_), channel_id=1, source_target_pairs={{0,2},{2,0},{4,6},{6,4},{1,3},{3,1},{5,7},{7,5},{8,10},{10,8},{12,... | collective-permute-start | bytes 442376 | tf_op jit(solution)/shard_map/ppermute | solution.py:63
  44.4 7.7 %collective-permute-start.24 = (f32[384,128]{1,0:T(8,128)S(1)}, f32[384,128]{1,0:T(8,128)S(1)}, u32[]{:S(2)}, u32[]{:S(2)}) collective-permute-start(f32[384,128]{1,0:T(8,128)S(1)} %local_solve.3.refs_0_), channel_id=1, source_target_pairs={{0,4},{2,6},{4,0},{6,2},{1,5},{3,7},{5,1},{7,3},{8,12},{10,14},{12... | collective-permute-start | bytes 589832 | tf_op jit(solution)/shard_map/ppermute | solution.py:63
  44.9 10.8 %collective-permute-start.21 = (f32[384,128]{1,0:T(8,128)S(1)}, f32[384,128]{1,0:T(8,128)S(1)}, u32[]{:S(2)}, u32[]{:S(2)}) collective-permute-start(f32[384,128]{1,0:T(8,128)S(1)} %local_solve.2.refs_0_), channel_id=1, source_target_pairs={{0,4},{2,6},{4,0},{6,2},{1,5},{3,7},{5,1},{7,3},{8,12},{10,14},{12... | collective-permute-start | bytes 589832 | tf_op jit(solution)/shard_map/ppermute | solution.py:63
  46.5 10.7 %collective-permute-start.16 = (f32[4,96,128]{2,1,0:T(8,128)S(1)}, f32[4,96,128]{2,1,0:T(8,128)S(1)}, u32[]{:S(2)}, u32[]{:S(2)}) collective-permute-start(f32[4,96,128]{2,1,0:T(8,128)S(1)} %pad_maximum_fusion.1.g_mine), channel_id=1, source_target_pairs={{0,2},{2,0},{4,6},{6,4},{1,3},{3,1},{5,7},{7,5},{8,10},{10,8},{12,... | collective-permute-start | bytes 589832 | tf_op jit(solution)/shard_map/ppermute | solution.py:63
  46.5 10.6 %collective-permute-start.23 = (f32[384,128]{1,0:T(8,128)S(1)}, f32[384,128]{1,0:T(8,128)S(1)}, u32[]{:S(2)}, u32[]{:S(2)}) collective-permute-start(f32[384,128]{1,0:T(8,128)S(1)} %local_solve.3.refs_0_), channel_id=1, source_target_pairs={{0,2},{2,0},{4,6},{6,4},{1,3},{3,1},{5,7},{7,5},{8,10},{10,8},{12,... | collective-permute-start | bytes 589832 | tf_op jit(solution)/shard_map/ppermute | solution.py:63
  47.0 12.2 %collective-permute-start.20 = (f32[384,128]{1,0:T(8,128)S(1)}, f32[384,128]{1,0:T(8,128)S(1)}, u32[]{:S(2)}, u32[]{:S(2)}) collective-permute-start(f32[384,128]{1,0:T(8,128)S(1)} %local_solve.2.refs_0_), channel_id=1, source_target_pairs={{0,2},{2,0},{4,6},{6,4},{1,3},{3,1},{5,7},{7,5},{8,10},{10,8},{12,... | collective-permute-start | bytes 589832 | tf_op jit(solution)/shard_map/ppermute | solution.py:63
  52.1 5.1 %collective-permute-start.25 = (f32[384,128]{1,0:T(8,128)S(1)}, f32[384,128]{1,0:T(8,128)S(1)}, u32[]{:S(2)}, u32[]{:S(2)}) collective-permute-start(f32[384,128]{1,0:T(8,128)S(1)} %collective-permute-done.24.refs_2_), channel_id=1, source_target_pairs={{0,2},{2,0},{4,6},{6,4},{1,3},{3,1},{5,7},{7,5},{8,10},{10,8},{12,... | collective-permute-start | bytes 589832 | tf_op jit(solution)/shard_map/ppermute | solution.py:63
  55.8 3.5 %collective-permute-start.22 = (f32[384,128]{1,0:T(8,128)S(1)}, f32[384,128]{1,0:T(8,128)S(1)}, u32[]{:S(2)}, u32[]{:S(2)}) collective-permute-start(f32[384,128]{1,0:T(8,128)S(1)} %collective-permute-done.21.refs_2_), channel_id=1, source_target_pairs={{0,2},{2,0},{4,6},{6,4},{1,3},{3,1},{5,7},{7,5},{8,10},{10,8},{12,... | collective-permute-start | bytes 589832 | tf_op jit(solution)/shard_map/ppermute | solution.py:63
  64.2 10.3 %collective-permute-start.26 = (f32[6,128,128]{2,1,0:T(8,128)S(1)}, f32[6,128,128]{2,1,0:T(8,128)S(1)}, u32[]{:S(2)}, u32[]{:S(2)}) collective-permute-start(f32[6,128,128]{2,1,0:T(8,128)S(1)} %get-tuple-element.35), channel_id=1, source_target_pairs={{0,8},{8,0},{16,24},{24,16},{1,9},{9,1},{17,25},{25,17},{2,10},{10... | collective-permute-start | bytes 1179656 | tf_op jit(solution)/shard_map/ppermute | solution.py:494
  64.3 12.1 %collective-permute-start.27 = (f32[6,128,128]{2,1,0:T(8,128)S(1)}, f32[6,128,128]{2,1,0:T(8,128)S(1)}, u32[]{:S(2)}, u32[]{:S(2)}) collective-permute-start(f32[6,128,128]{2,1,0:T(8,128)S(1)} %get-tuple-element.36), channel_id=1, source_target_pairs={{8,16},{16,8},{9,17},{17,9},{10,18},{18,10},{11,19},{19,11},{12,20... | collective-permute-start | bytes 1179656 | tf_op jit(solution)/shard_map/ppermute | solution.py:494
  66.7 12.2 %collective-permute-start.33 = (f32[384,128]{1,0:T(8,128)S(1)}, f32[384,128]{1,0:T(8,128)S(1)}, u32[]{:S(2)}, u32[]{:S(2)}) collective-permute-start(f32[384,128]{1,0:T(8,128)S(1)} %get-tuple-element.39.refs_0_), channel_id=1, source_target_pairs={{0,4},{2,6},{4,0},{6,2},{1,5},{3,7},{5,1},{7,3},{8,12},{10,14},{12... | collective-permute-start | bytes 589832 | tf_op jit(solution)/shard_map/ppermute | solution.py:63
  67.3 12.1 %collective-permute-start.30 = (f32[384,128]{1,0:T(8,128)S(1)}, f32[384,128]{1,0:T(8,128)S(1)}, u32[]{:S(2)}, u32[]{:S(2)}) collective-permute-start(f32[384,128]{1,0:T(8,128)S(1)} %get-tuple-element.37.refs_0_), channel_id=1, source_target_pairs={{0,4},{2,6},{4,0},{6,2},{1,5},{3,7},{5,1},{7,3},{8,12},{10,14},{12... | collective-permute-start | bytes 589832 | tf_op jit(solution)/shard_map/ppermute | solution.py:63
  78.2 2.7 %collective-permute-start.28 = (f32[6,128,128]{2,1,0:T(8,128)S(1)}, f32[6,128,128]{2,1,0:T(8,128)S(1)}, u32[]{:S(2)}, u32[]{:S(2)}) collective-permute-start(f32[6,128,128]{2,1,0:T(8,128)S(1)} %couple.2.g_mine), channel_id=1, source_target_pairs={{0,2},{2,0},{4,6},{6,4},{1,3},{3,1},{5,7},{7,5},{8,10},{10,8},{12,... | collective-permute-start | bytes 1179656 | tf_op jit(solution)/shard_map/ppermute | solution.py:63
  78.3 2.5 %collective-permute-start.32 = (f32[384,128]{1,0:T(8,128)S(1)}, f32[384,128]{1,0:T(8,128)S(1)}, u32[]{:S(2)}, u32[]{:S(2)}) collective-permute-start(f32[384,128]{1,0:T(8,128)S(1)} %get-tuple-element.39.refs_0_), channel_id=1, source_target_pairs={{0,2},{2,0},{4,6},{6,4},{1,3},{3,1},{5,7},{7,5},{8,10},{10,8},{12,... | collective-permute-start | bytes 589832 | tf_op jit(solution)/shard_map/ppermute | solution.py:63
  78.8 4.2 %collective-permute-start.29 = (f32[384,128]{1,0:T(8,128)S(1)}, f32[384,128]{1,0:T(8,128)S(1)}, u32[]{:S(2)}, u32[]{:S(2)}) collective-permute-start(f32[384,128]{1,0:T(8,128)S(1)} %get-tuple-element.37.refs_0_), channel_id=1, source_target_pairs={{0,2},{2,0},{4,6},{6,4},{1,3},{3,1},{5,7},{7,5},{8,10},{10,8},{12,... | collective-permute-start | bytes 589832 | tf_op jit(solution)/shard_map/ppermute | solution.py:63
  78.9 1.9 %collective-permute-start.34 = (f32[384,128]{1,0:T(8,128)S(1)}, f32[384,128]{1,0:T(8,128)S(1)}, u32[]{:S(2)}, u32[]{:S(2)}) collective-permute-start(f32[384,128]{1,0:T(8,128)S(1)} %collective-permute-done.33.refs_2_), channel_id=1, source_target_pairs={{0,2},{2,0},{4,6},{6,4},{1,3},{3,1},{5,7},{7,5},{8,10},{10,8},{12,... | collective-permute-start | bytes 589832 | tf_op jit(solution)/shard_map/ppermute | solution.py:63
  79.4 3.7 %collective-permute-start.31 = (f32[384,128]{1,0:T(8,128)S(1)}, f32[384,128]{1,0:T(8,128)S(1)}, u32[]{:S(2)}, u32[]{:S(2)}) collective-permute-start(f32[384,128]{1,0:T(8,128)S(1)} %collective-permute-done.30.refs_2_), channel_id=1, source_target_pairs={{0,2},{2,0},{4,6},{6,4},{1,3},{3,1},{5,7},{7,5},{8,10},{10,8},{12,... | collective-permute-start | bytes 589832 | tf_op jit(solution)/shard_map/ppermute | solution.py:63
  85.5 4.2 %collective-permute-start.35 = (f32[1,96,128]{2,1,0:T(8,128)S(1)}, f32[1,96,128]{2,1,0:T(8,128)S(1)}, u32[]{:S(2)}, u32[]{:S(2)}) collective-permute-start(f32[1,96,128]{2,1,0:T(8,128)S(1)} %fusion), channel_id=1, source_target_pairs={{0,8},{8,0},{16,24},{24,16},{1,9},{9,1},{17,25},{25,17},{2,10},{10... | collective-permute-start | bytes 147464 | tf_op jit(solution)/shard_map/ppermute | solution.py:63
  89.6 5.7 %collective-permute-start.36 = (f32[2,96,128]{2,1,0:T(8,128)S(1)}, f32[2,96,128]{2,1,0:T(8,128)S(1)}, u32[]{:S(2)}, u32[]{:S(2)}) collective-permute-start(f32[2,96,128]{2,1,0:T(8,128)S(1)} %pad_maximum_fusion.4), channel_id=1, source_target_pairs={{0,16},{8,24},{16,0},{24,8},{1,17},{9,25},{17,1},{25,9},{2,18},{10... | collective-permute-start | bytes 294920 | tf_op jit(solution)/shard_map/ppermute | solution.py:63
  89.7 7.9 %collective-permute-start.39 = (f32[384,128]{1,0:T(8,128)S(1)}, f32[384,128]{1,0:T(8,128)S(1)}, u32[]{:S(2)}, u32[]{:S(2)}) collective-permute-start(f32[384,128]{1,0:T(8,128)S(1)} %get-tuple-element.42.refs_0_), channel_id=1, source_target_pairs={{0,4},{2,6},{4,0},{6,2},{1,5},{3,7},{5,1},{7,3},{8,12},{10,14},{12... | collective-permute-start | bytes 589832 | tf_op jit(solution)/shard_map/ppermute | solution.py:63
  90.3 9.8 %collective-permute-start.42 = (f32[384,128]{1,0:T(8,128)S(1)}, f32[384,128]{1,0:T(8,128)S(1)}, u32[]{:S(2)}, u32[]{:S(2)}) collective-permute-start(f32[384,128]{1,0:T(8,128)S(1)} %get-tuple-element.46.refs_0_), channel_id=1, source_target_pairs={{0,4},{2,6},{4,0},{6,2},{1,5},{3,7},{5,1},{7,3},{8,12},{10,14},{12... | collective-permute-start | bytes 589832 | tf_op jit(solution)/shard_map/ppermute | solution.py:63
  91.8 8.3 %collective-permute-start.38 = (f32[384,128]{1,0:T(8,128)S(1)}, f32[384,128]{1,0:T(8,128)S(1)}, u32[]{:S(2)}, u32[]{:S(2)}) collective-permute-start(f32[384,128]{1,0:T(8,128)S(1)} %get-tuple-element.42.refs_0_), channel_id=1, source_target_pairs={{0,2},{2,0},{4,6},{6,4},{1,3},{3,1},{5,7},{7,5},{8,10},{10,8},{12,... | collective-permute-start | bytes 589832 | tf_op jit(solution)/shard_map/ppermute | solution.py:63
  95.3 4.8 %collective-permute-start.37 = (f32[4,96,128]{2,1,0:T(8,128)S(1)}, f32[4,96,128]{2,1,0:T(8,128)S(1)}, u32[]{:S(2)}, u32[]{:S(2)}) collective-permute-start(f32[4,96,128]{2,1,0:T(8,128)S(1)} %pad_maximum_fusion.2.g_mine), channel_id=1, source_target_pairs={{0,2},{2,0},{4,6},{6,4},{1,3},{3,1},{5,7},{7,5},{8,10},{10,8},{12,... | collective-permute-start | bytes 589832 | tf_op jit(solution)/shard_map/ppermute | solution.py:63
  97.6 2.5 %collective-permute-start.40 = (f32[384,128]{1,0:T(8,128)S(1)}, f32[384,128]{1,0:T(8,128)S(1)}, u32[]{:S(2)}, u32[]{:S(2)}) collective-permute-start(f32[384,128]{1,0:T(8,128)S(1)} %collective-permute-done.39.refs_2_), channel_id=1, source_target_pairs={{0,2},{2,0},{4,6},{6,4},{1,3},{3,1},{5,7},{7,5},{8,10},{10,8},{12,... | collective-permute-start | bytes 589832 | tf_op jit(solution)/shard_map/ppermute | solution.py:63
  97.6 4.5 %collective-permute-start.41 = (f32[384,128]{1,0:T(8,128)S(1)}, f32[384,128]{1,0:T(8,128)S(1)}, u32[]{:S(2)}, u32[]{:S(2)}) collective-permute-start(f32[384,128]{1,0:T(8,128)S(1)} %get-tuple-element.46.refs_0_), channel_id=1, source_target_pairs={{0,2},{2,0},{4,6},{6,4},{1,3},{3,1},{5,7},{7,5},{8,10},{10,8},{12,... | collective-permute-start | bytes 589832 | tf_op jit(solution)/shard_map/ppermute | solution.py:63
  100.1 2.0 %collective-permute-start.43 = (f32[384,128]{1,0:T(8,128)S(1)}, f32[384,128]{1,0:T(8,128)S(1)}, u32[]{:S(2)}, u32[]{:S(2)}) collective-permute-start(f32[384,128]{1,0:T(8,128)S(1)} %collective-permute-done.42.refs_2_), channel_id=1, source_target_pairs={{0,2},{2,0},{4,6},{6,4},{1,3},{3,1},{5,7},{7,5},{8,10},{10,8},{12,... | collective-permute-start | bytes 589832 | tf_op jit(solution)/shard_map/ppermute | solution.py:63
  107.1 10.3 %collective-permute-start.44 = (f32[6,128,128]{2,1,0:T(8,128)S(1)}, f32[6,128,128]{2,1,0:T(8,128)S(1)}, u32[]{:S(2)}, u32[]{:S(2)}) collective-permute-start(f32[6,128,128]{2,1,0:T(8,128)S(1)} %get-tuple-element.52), channel_id=1, source_target_pairs={{0,8},{8,0},{16,24},{24,16},{1,9},{9,1},{17,25},{25,17},{2,10},{10... | collective-permute-start | bytes 1179656 | tf_op jit(solution)/shard_map/ppermute | solution.py:494
  107.2 12.9 %collective-permute-start.45 = (f32[6,128,128]{2,1,0:T(8,128)S(1)}, f32[6,128,128]{2,1,0:T(8,128)S(1)}, u32[]{:S(2)}, u32[]{:S(2)}) collective-permute-start(f32[6,128,128]{2,1,0:T(8,128)S(1)} %get-tuple-element.53), channel_id=1, source_target_pairs={{8,16},{16,8},{9,17},{17,9},{10,18},{18,10},{11,19},{19,11},{12,20... | collective-permute-start | bytes 1179656 | tf_op jit(solution)/shard_map/ppermute | solution.py:494
  121.8 1.8 %collective-permute-start.46 = (f32[6,128,128]{2,1,0:T(8,128)S(1)}, f32[6,128,128]{2,1,0:T(8,128)S(1)}, u32[]{:S(2)}, u32[]{:S(2)}) collective-permute-start(f32[6,128,128]{2,1,0:T(8,128)S(1)} %couple.3.g_mine), channel_id=1, source_target_pairs={{0,2},{2,0},{4,6},{6,4},{1,3},{3,1},{5,7},{7,5},{8,10},{10,8},{12,... | collective-permute-start | bytes 1179656 | tf_op jit(solution)/shard_map/ppermute | solution.py:63
  (16 other events, 176.3 us)

commit v2 on v1

v2 whole, which is shorter than its diff:
```python
import jax
import jax.numpy as jnp
from jax import lax
from jax.experimental import pallas as pl
from jax.experimental.pallas import tpu as pltpu
from jax.sharding import PartitionSpec as P

ITERS = 2
damping = 0.7
f32 = jnp.float32
bf16 = jnp.bfloat16
MIB = 2**20
COST = 1000.0
IN_VMEM = pl.BlockSpec(memory_space=pltpu.VMEM)
IN_SMEM = pl.BlockSpec(memory_space=pltpu.SMEM)
IN_HBM = pl.BlockSpec(memory_space=pltpu.HBM)


def call(kernel, name, operands, outputs, micros, scalars=0, scratch=(), limit=8, far=0, after=()):
    used = len(operands)

    def body(*refs):
        kernel(*refs[:used], *refs[used + len(after) :])

    operands = list(operands[: used - far]) + [
        pltpu.with_memory_space_constraint(x, pltpu.HBM) for x in operands[used - far :]
    ]
    return pl.pallas_call(
        body,
        in_specs=[IN_SMEM] * scalars
        + [IN_VMEM] * (used - scalars - far)
        + [IN_HBM] * far
        + [pl.BlockSpec(memory_space=pl.ANY)] * len(after),
        out_specs=[IN_SMEM if len(shape) == 1 else IN_VMEM for shape, _ in outputs],
        out_shape=[jax.ShapeDtypeStruct(shape, kind) for shape, kind in outputs],
        scratch_shapes=list(scratch),
        compiler_params=pltpu.CompilerParams(vmem_limit_bytes=limit * MIB),
        cost_estimate=pl.CostEstimate(flops=0, bytes_accessed=int(micros * COST), transcendentals=0),
        name=name,
    )(*operands, *after)


def position():
    crow = lax.axis_index("crow")
    return lax.axis_index("sub"), lax.rem(crow, 2), crow


def parts(x):
    hi = x.astype(bf16)
    return hi, (x - hi.astype(f32)).astype(bf16)


def beside(x):
    hi, lo = parts(x)
    return jnp.concatenate([hi, lo], axis=1)


def stacked(x):
    hi, lo = parts(x)
    return jnp.concatenate([hi, lo], axis=0)


def dot(a, b):
    return jnp.dot(a, b, preferred_element_type=f32)


def sides(product):
    columns = product.shape[1] // 2
    return product[:, :columns] + product[:, columns:]


def folded(product):
    rows = product.shape[0] // 2
    return sides(product[:rows] + product[rows:])


def exchange(x, axis, bit):
    size = lax.axis_size(axis)
    return lax.ppermute(x, axis, [(i, i ^ bit) for i in range(size) if (i ^ bit) < size])


def split_matrix(matrix, name, after=()):
    subs, rows, order = matrix.shape
    tile = 96 if rows % 96 == 0 else rows
    tiles = rows // tile

    def kernel(m, o, held, sems):
        crow = lax.axis_index("crow")
        copies = [
            pltpu.make_async_copy(
                m.at[i // tiles, pl.ds((i % tiles) * tile, tile)], held.at[i], sems.at[i]
            )
            for i in range(subs * tiles)
        ]
        for copy in copies:
            copy.start()
        for i, copy in enumerate(copies):
            copy.wait()
            first = (i % tiles) * tile
            for q in range(order // rows):
                column = pl.multiple_of((crow ^ q) * rows, 128)
                hi, lo = parts(held[i, :, pl.ds(column, rows)])
                o[i // tiles, first : first + tile, q * rows : (q + 1) * rows] = hi
                o[i // tiles, rows + first : rows + first + tile, q * rows : (q + 1) * rows] = lo

    return call(
        kernel,
        name,
        [matrix],
        [((subs, 2 * rows, order), bf16)],
        2.0,
        far=1,
        scratch=[
            pltpu.VMEM((subs * tiles, tile, order), f32),
            pltpu.SemaphoreType.DMA((subs * tiles,)),
        ],
        after=after,
    )[0]


def place_coarse(pieces, subs, modes, own_rows, after=()):
    height, rows = pieces[0][0].shape
    count = max(q for _, q, _ in pieces) + 1
    order = rows * count
    spans = (height - subs * modes) // own_rows

    def kernel(*refs):
        down, up, inverse, held = refs[len(pieces) :]
        crow, ccol = lax.axis_index("crow"), lax.axis_index("ccol")
        for ref, (_, q, half) in zip(refs, pieces):
            if half is None:
                held[q] = ref[...]
            else:
                size = ref.shape[0]
                which = ccol if half == 0 else 1 - ccol
                held[q, pl.ds(pl.multiple_of(which * size, 8), size)] = ref[...]
        for q in range(count):
            here = slice(q * rows, (q + 1) * rows)
            for s in range(subs):
                value = held[q, s * modes : (s + 1) * modes]
                down[s, :, here] = stacked(value)
                up[s, here] = beside(value.T)
            for i in range(spans):
                first = subs * modes + i * own_rows
                inverse[crow ^ q, :, i * rows : (i + 1) * rows] = held[q, first : first + own_rows]

    return call(
        kernel,
        "place_coarse",
        [p[0] for p in pieces],
        [
            ((subs, 2 * modes, order), bf16),
            ((subs, order, 2 * modes), bf16),
            ((count, own_rows, spans * rows), f32),
        ],
        1.2,
        scratch=[pltpu.VMEM((count, height, rows), f32)],
        limit=16,
        after=after,
    )


def fold_targets(counts, targets, split, basis, after=()):
    slots, subs, width = targets.shape
    rows = split.shape[1] // 2
    order = split.shape[2]
    modes = basis.shape[1] // 2
    half = subs // 2

    def kernel(n, tg, m, z, own, folds, z_folds):
        at = position()
        line = lax.broadcasted_iota(jnp.int32, (order, width), 0)
        for s in range(subs):
            for k in range(0, slots, 2):
                pair = []
                for kk in (k, k + 1):
                    aim = in_xor_order(tg[kk, s : s + 1, :], rows, order // rows, at[2])
                    aim = jnp.where(kk < n[s], aim, -1)
                    pair.append((line == aim).astype(f32).astype(bf16))
                hit = jnp.concatenate(pair, axis=1)
                here = slice(k * width, (k + 2) * width)
                own[s, :, here] = hit[:rows]
                folds[s, :, here] = dot(m[s], hit).astype(bf16)

                @pl.when(at[1] == s // half)
                def _():
                    z_folds[s % half, :, here] = dot(z[s], hit).astype(bf16)

    return call(
        kernel,
        "fold_targets",
        [counts, targets, split, basis],
        [
            ((subs, rows, slots * width), bf16),
            ((subs, 2 * rows, slots * width), bf16),
            ((half, 2 * modes, slots * width), bf16),
        ],
        4.5,
        scalars=1,
        limit=8,
        after=after,
    )


def begin(neighbour, counts, reads, basis, residual, inverse):
    subs, modes, rows = basis.shape
    cases = residual.shape[2]
    half = subs // 2
    slots, _, width = reads.shape
    used = subs * slots
    listed = -(-(used + 2) // 8) * 8
    own_rows, columns = inverse.shape
    height = subs * modes + own_rows * (columns // rows)

    def kernel(n, c, rd, z_far, r_far, c_far, keep, give, r, packed, both, part, sems):
        at = position()
        pairs = [(z_far.at[s], both.at[s * modes : (s + 1) * modes]) for s in range(subs)]
        pairs.append((r_far, r))
        for i in range(columns // rows):
            first = subs * modes + i * own_rows
            pairs.append((c_far.at[:, i * rows : (i + 1) * rows], both.at[first : first + own_rows]))
        moves = [pltpu.make_async_copy(a, b, sems.at[i]) for i, (a, b) in enumerate(pairs)]
        for move in moves:
            move.start()
        lane = lax.broadcasted_iota(jnp.int32, (1, width), 1)
        ids = jnp.zeros((1, width), jnp.int32)
        limits = jnp.zeros((1, width), jnp.int32)
        packed[...] = jnp.zeros((listed, width), f32)
        for s in range(subs):
            for k in range(slots):
                block = s * slots + k
                packed[block : block + 1] = rd[k, s : s + 1].astype(f32)
                ids = jnp.where(lane == block, n[s, k], ids)
                limits = jnp.where(lane == block, jnp.where(k < c[s], 1, 0), limits)
        packed[used : used + 1] = ids.astype(f32)
        packed[used + 1 : used + 2] = limits.astype(f32)
        for move in moves:
            move.wait()
        start = pl.multiple_of(lax.axis_index("ccol") * (height // 2), 8)
        part[...] = both[pl.ds(start, height // 2)]
        for i in range(half):
            for out, first in ((keep, at[1] * half), (give, (1 - at[1]) * half)):
                s = first + i
                z = both[pl.ds(pl.multiple_of(s * modes, modes), modes)]
                out[i * modes : (i + 1) * modes] = folded(dot(stacked(z), beside(r[s])))

    return call(
        kernel,
        "begin",
        [neighbour, counts, reads, basis, residual, inverse],
        [
            ((half * modes, cases), f32),
            ((half * modes, cases), f32),
            (residual.shape, f32),
            ((listed, width), f32),
            ((height, rows), f32),
            ((height // 2, rows), f32),
        ],
        2.0,
        scalars=2,
        far=3,
        scratch=[pltpu.SemaphoreType.DMA((subs + 1 + columns // rows,))],
    )


def relay(x, after):
    def kernel(a, b):
        b[...] = a[...]

    return call(kernel, "relay", [x], [(x.shape, x.dtype)], 0.3, after=after)[0]


def in_xor_order(rows_listed, rows, blocks, crow_index):
    block = jnp.zeros_like(rows_listed)
    for q in range(1, blocks):
        block = block + (rows_listed >= q * rows).astype(jnp.int32)
    return rows_listed + ((block ^ crow_index) - block) * rows


def prepare(held, subs, slots, rows, blocks, after=()):
    ways = len(held)
    width = held[0].shape[1]
    used = subs * slots
    half = used // 2
    listed = -(-(used + 2) // 8) * 8
    starts = [h.shape[0] - listed for h in held]

    def kernel(*refs):
        at = position()
        lists, info, rows_v, sem = refs[ways:]
        for d in range(ways):
            table = refs[d][starts[d] : starts[d] + listed].astype(jnp.int32)
            picked = jnp.where(at[1] == 0, table[:half], table[half:used])
            lists[d] = in_xor_order(picked, rows, blocks, at[2])
            ids, limits = table[used : used + 1], table[used + 1 : used + 2]
            place = ids - at[0] * subs
            use = (limits > 0) & (place >= 0) & (place < subs)
            rows_v[d : d + 1] = jnp.where(use, place, -1)
        table = refs[0][starts[0] : starts[0] + listed].astype(jnp.int32)
        ids, limits = table[used : used + 1], table[used + 1 : used + 2]
        twin = at[0] ^ 1
        inside = (ids >= at[0] * subs) & (ids < (at[0] + 1) * subs)
        paired = (ids >= twin * subs) & (ids < (twin + 1) * subs)
        theirs = jnp.where(inside, 0, jnp.where(paired, 1, 2))
        rows_v[ways : ways + 1] = jnp.where(limits > 0, theirs, -1)
        move = pltpu.make_async_copy(rows_v, info, sem)
        move.start()
        move.wait()

    return pl.pallas_call(
        lambda *refs: kernel(*refs[:ways], *refs[ways + len(after) :]),
        in_specs=[IN_VMEM] * ways + [pl.BlockSpec(memory_space=pl.ANY)] * len(after),
        out_specs=[IN_VMEM, IN_SMEM],
        out_shape=[
            jax.ShapeDtypeStruct((ways, half, width), jnp.int32),
            jax.ShapeDtypeStruct((8, width), jnp.int32),
        ],
        scratch_shapes=[pltpu.VMEM((8, width), jnp.int32), pltpu.SemaphoreType.DMA(())],
        compiler_params=pltpu.CompilerParams(vmem_limit_bytes=8 * MIB),
        cost_estimate=pl.CostEstimate(flops=0, bytes_accessed=int(COST), transcendentals=0),
        name="prepare",
    )(*held, *after)


def add_up(a, b, below=None, after=()):
    rows = a.shape[0]
    more = 0 if below is None else below.shape[0]

    def kernel(x, y, *refs):
        o = refs[-1]
        o[:rows] = x[...] + y[...]
        if more:
            o[rows:] = refs[0][...]

    operands = [a, b] + ([] if below is None else [below])
    return call(kernel, "add_up", operands, [((rows + more, a.shape[1]), f32)], 0.2, after=after)[0]


def load(ref, s):
    return ref[s] if len(ref.shape) == 3 else ref[...]


def local_solve(s, split, blocks, after=()):
    rows = split.shape[1] // 2
    order = split.shape[2]
    cases = blocks[0].shape[-1]

    def kernel(m, *refs):
        o, rhs = refs[-2:]
        for q, ref in enumerate(refs[:-2]):
            rhs[q * rows : (q + 1) * rows] = beside(load(ref, s))
        o[...] = folded(dot(m[s], rhs[...]))

    return call(
        kernel,
        "local_solve",
        [split, *blocks],
        [((rows, cases), f32)],
        0.8,
        scratch=[pltpu.VMEM((order, 2 * cases), bf16)],
        after=after,
    )[0]


def choose_terms(here, mine, other, terms):
    slots, width = mine.shape[:2]

    @pl.when(here)
    def _():
        for k in range(slots):
            terms[k * width : (k + 1) * width] = beside(mine[k])

    @pl.when(jnp.logical_not(here))
    def _():
        for k in range(slots):
            terms[k * width : (k + 1) * width] = beside(other[k])


def local_solve_inflow(s, split, folds, blocks, mine, other, after=()):
    rows = split.shape[1] // 2
    order = split.shape[2]
    subs = split.shape[0]
    cases = blocks[0].shape[-1]
    slots, width = mine.shape[:2]
    count = len(blocks)

    def kernel(m, f, g_mine, g_other, *refs):
        at = position()
        o, rhs, terms = refs[count:]
        for q, ref in enumerate(refs[:count]):
            rhs[q * rows : (q + 1) * rows] = beside(ref[...])
        choose_terms(at[1] == s // (subs // 2), g_mine, g_other, terms)
        o[...] = folded(dot(m[s], rhs[...])) + damping * folded(dot(f[s], terms[...]))

    return call(
        kernel,
        "local_solve_inflow",
        [split, folds, mine, other, *blocks],
        [((rows, cases), f32), ((order, 2 * cases), bf16)],
        1.2,
        scratch=[pltpu.VMEM((slots * width, 2 * cases), bf16)],
        after=after,
    )


def restrict(basis, z_folds, residual_parts, terms, after=()):
    subs = basis.shape[0]
    modes = basis.shape[1] // 2
    cases = residual_parts[0].shape[1] // 2
    half = subs // 2
    slots, width = terms.shape[0] // half, terms.shape[1]

    def kernel(z, zf, g, *refs):
        at = position()
        out, rhs = refs[subs:]
        for i in range(half):
            for k in range(slots):
                rhs[k * width : (k + 1) * width] = beside(g[i * slots + k])
            inflow = damping * folded(dot(zf[i], rhs[...]))
            for s in range(i, subs, half):

                @pl.when(at[1] == s // half)
                def _():
                    out[i * modes : (i + 1) * modes] = folded(dot(z[s], refs[s][...])) + inflow

    return call(
        kernel,
        "restrict",
        [basis, z_folds, terms, *residual_parts],
        [((half * modes, cases), f32)],
        0.4,
        scratch=[pltpu.VMEM((slots * width, 2 * cases), bf16)],
        after=after,
    )[0]


def lift_coarse(inverse, lift, mine, other, after=()):
    subs, order, twice = lift.shape
    modes = twice // 2
    half, cases = subs // 2, mine[0].shape[1]
    per_sub = inverse.shape[0] // subs
    columns = inverse.shape[2]
    groups = len(mine)

    def kernel(c, z, *refs):
        at = position()
        o, right = refs[2 * groups :]
        for b in range(groups):
            base = (at[0] ^ b) * (2 * half * modes)
            for h, ref in ((at[1], refs[b]), (1 - at[1], refs[groups + b])):
                for i in range(half):
                    row = pl.multiple_of(base + h * (half * modes) + i * modes, 16)
                    right[pl.ds(row, modes)] = beside(ref[i * modes : (i + 1) * modes])
        for s in range(subs):
            c_rows = c[s * per_sub : (s + 1) * per_sub].reshape(modes, columns)
            coarse = beside(folded(dot(stacked(c_rows), right[...])))
            o[s] = sides(dot(z[s], jnp.concatenate([coarse, coarse], axis=0)))

    return call(
        kernel,
        "lift_coarse",
        [inverse, lift, *mine, *other],
        [((subs, order, cases), f32)],
        1.2,
        scratch=[pltpu.VMEM((columns, 2 * cases), bf16)],
        limit=16,
        after=after,
    )[0]


def correct(s, split, lifted, blocks, residual, old, after=()):
    rows = split.shape[1] // 2
    order = split.shape[2]
    cases = blocks[0].shape[-1]
    count = len(blocks)

    def kernel(m, up, res, *refs):
        old_refs = refs[count : len(refs) - 3]
        o, total, corr = refs[len(refs) - 3 :]
        for q, ref in enumerate(refs[:count]):
            here = slice(q * rows, (q + 1) * rows)
            value = ref[...] + up[s, here]
            corr[here] = beside(value)
            if q == 0:
                total[...] = damping * value + old_refs[0][...] if old_refs else damping * value
        o[...] = load(res, s) - damping * folded(dot(m[s], corr[...]))

    return call(
        kernel,
        "correct",
        [split, lifted, residual, *blocks] + ([] if old is None else [old]),
        [((rows, cases), f32), ((rows, cases), f32), ((order, 2 * cases), bf16)],
        1.0,
        after=after,
    )


def select_rows(info, lists, corrs, after=()):
    ways, slots, width = lists.shape
    order, twice = corrs[0].shape
    cases = twice // 2

    def kernel(where, l, *refs):
        at = position()
        corr_refs = refs[: len(corrs)]
        outs = refs[len(corrs) :]
        lane = lax.broadcasted_iota(jnp.int32, (width, order), 1)
        for d in range(ways):

            @pl.loop(0, slots)
            def _(k):
                place = where[d, at[1] * slots + k]

                @pl.when(place < 0)
                def _():
                    outs[d][k] = jnp.zeros((width, cases), f32)

                for s, ref in enumerate(corr_refs):

                    @pl.when(place == s)
                    def _():
                        rows = jnp.broadcast_to(l[d, pl.ds(k, 1), :], (width, width)).T
                        rows = jnp.concatenate([rows] * (order // width), axis=1)
                        one = (rows == lane).astype(f32).astype(bf16)
                        outs[d][k] = sides(dot(one, ref[...]))

    return call(
        kernel,
        "select_rows",
        [info, lists, *corrs],
        [((slots, width, cases), f32)] * ways,
        1.5,
        scalars=1,
        after=after,
    )


def couple(info, coupling, sources, after=()):
    subs, per_sub, width, _ = coupling.shape
    slots, _, cases = sources[0].shape
    ways = len(sources)

    def kernel(where, c, *refs):
        at = position()
        out = refs[ways]

        @pl.loop(0, slots)
        def _(k):
            block = at[1] * slots + k
            code = where[ways, block]

            @pl.when(code < 0)
            def _():
                out[k] = jnp.zeros((width, cases), f32)

            for d, ref in enumerate(refs[:ways]):

                @pl.when(code == d)
                def _():
                    out[k] = folded(dot(stacked(c[block // per_sub, block % per_sub]), beside(ref[k])))

    return call(
        kernel,
        "couple",
        [info, coupling, *sources],
        [((slots, width, cases), f32)],
        0.8,
        scalars=1,
        after=after,
    )[0]


def add_inflow(residuals, hits, mine, other):
    subs = hits.shape[0]
    slots, width, cases = mine[0].shape
    rows = residuals[0].shape[0]
    sweeps = len(mine)

    def kernel(tg, *refs):
        at = position()
        groups = (refs[:sweeps], refs[sweeps : 2 * sweeps])
        res = refs[2 * sweeps : 2 * sweeps + subs]
        out, terms = refs[2 * sweeps + subs :]
        for s in range(subs):
            here = at[1] == s // (subs // 2)
            for flag, terms_of in ((here, groups[0]), (jnp.logical_not(here), groups[1])):

                @pl.when(flag)
                def _():
                    for k in range(slots):
                        value = terms_of[0][k]
                        for more in terms_of[1:]:
                            value = value + more[k]
                        terms[k * width : (k + 1) * width] = beside(value)

            out[s] = res[s][...] + damping * sides(dot(tg[s], terms[...]))

    return call(
        kernel,
        "add_inflow",
        [hits, *mine, *other, *residuals],
        [((subs, rows, cases), f32)],
        0.8,
        scratch=[pltpu.VMEM((slots * width, 2 * cases), bf16)],
    )[0]


def gathered(x, hold=()):
    bit = lax.axis_size("crow") // 2
    blocks = {0: x}
    while bit >= 1:
        news = {q | bit: exchange(b, "crow", bit) for q, b in blocks.items()}
        if bit > 1 and hold:
            news = {q: relay(b, hold) for q, b in news.items()}
        blocks.update(news)
        bit //= 2
    return [blocks[q] for q in sorted(blocks)]


def coarse_pieces(x, part, hold):
    bit = lax.axis_size("crow") // 2
    if lax.axis_size("ccol") == 2:
        part = relay(exchange(part, "crow", bit), hold)
        pieces = [(x, 0, None), (part, bit, 0), (exchange(part, "ccol", 1), bit, 1)]
    else:
        pieces = [(x, 0, None), (exchange(x, "crow", bit), bit, None)]
    while bit > 1:
        bit //= 2
        pieces = pieces + [(exchange(p, "crow", bit), q | bit, half) for p, q, half in pieces]
    return pieces


def spread_over_sub(half):
    halves = [half] + [exchange(half, "sub", b) for b in range(1, lax.axis_size("sub"))]
    return halves, [exchange(h, "crow", 1) for h in halves]


def pair_routes(size):
    low = [(i, i + 1) for i in range(0, size - 1, 2)]
    high = [(i, i + 1) for i in range(1, size - 1, 2)]
    return [[p for a, b in pairs for p in ((a, b), (b, a))] for pairs in (low, high)]


def per_device(
    load_cases,
    stiffness,
    local_inverse,
    coarse_basis,
    coarse_inverse,
    coupling,
    target_local_rows,
    neighbour_read_rows,
    neighbour,
    counts,
):
    subs, rows, cases = load_cases.shape
    slots = neighbour.shape[1]
    groups = lax.axis_size("sub")
    crow_size = lax.axis_size("crow")
    targets = target_local_rows.transpose(1, 0, 2)
    routes = pair_routes(groups)

    keep, give, residual, packed, both, part = begin(
        neighbour, counts, neighbour_read_rows.transpose(1, 0, 2), coarse_basis, load_cases,
        coarse_inverse,
    )
    keep = add_up(keep, exchange(give, "crow", 1), None, [keep])
    inverse_split = split_matrix(local_inverse, "split_inverse", [keep])
    first_blocks = gathered(load_cases, [inverse_split])
    bits = [bit for bit in (2, 4, 8) if bit < crow_size]
    for bit in bits[:-1]:
        keep = add_up(keep, exchange(keep, "crow", bit), None, [inverse_split])
    more = relay(exchange(keep, "crow", bits[-1]), [inverse_split])
    local = []
    for s in range(subs):
        local.append(local_solve(s, inverse_split, first_blocks, [more] if s == 0 else [local[-1]]))
    keep = add_up(keep, more, packed, [local[-1]])
    mine, other = spread_over_sub(keep)

    if groups == 4:
        held = [packed, mine[1], mine[3]]
    else:
        held = [packed] + [lax.ppermute(packed, "sub", route) for route in routes]

    down, lift, inverse = place_coarse(
        coarse_pieces(both, part, [keep]), subs, coarse_basis.shape[1], coarse_inverse.shape[0],
        [keep],
    )
    lists, info = prepare(held, subs, slots, rows, crow_size, [down])
    stiffness_split = split_matrix(stiffness, "split_stiffness", [info])

    totals, residuals, last = [None] * subs, [residual] * subs, stiffness_split
    all_terms, all_others = [], []
    for sweep_index in range(ITERS):
        local_blocks = [gathered(v) for v in local]
        lifted = lift_coarse(inverse, lift, mine, other, [last])
        steps, last = [], lifted
        for s in range(subs):
            steps.append(
                correct(s, stiffness_split, lifted, local_blocks[s], residuals[s], totals[s], [last])
            )
            last = steps[-1][0]
        residuals, totals, corrs = zip(*steps)
        chosen = select_rows(info, lists, corrs)
        sources = [chosen[0]] + [lax.ppermute(c, "sub", route) for c, route in zip(chosen[1:], routes)]
        if sweep_index == 0:
            own_hits, folds, z_folds = fold_targets(
                counts, targets, inverse_split, down, [chosen[0]]
            )
            wholes = [gathered(r, [folds]) for r in residuals]
            ready = [w[crow_size // 2] for w in wholes]
        terms = couple(info, coupling, sources, ready if sweep_index == 0 else [])
        other_terms = exchange(terms, "crow", 1)
        all_terms.append(terms)
        all_others.append(other_terms)
        if sweep_index == ITERS - 1:
            return jnp.stack(totals), add_inflow(residuals, own_hits, all_terms, all_others)
        steps, last = [], terms
        for s in range(subs):
            steps.append(
                local_solve_inflow(
                    s, inverse_split, folds, wholes[s], terms, other_terms, [last]
                )
            )
            last = steps[-1][0]
        local, residual_parts = zip(*steps)
        half = restrict(down, z_folds, residual_parts, terms, [last])
        last = half
        mine, other = spread_over_sub(half)


def solution(mesh):
    return jax.shard_map(
        per_device,
        mesh=mesh,
        in_specs=(
            P("sub", "crow", "ccol"),
            P("sub", "crow", None),
            P("sub", "crow", None),
            P("sub", None, "crow"),
            P(("sub", "crow"), None),
            P("sub", None, None, None),
            P("sub", None, None),
            P("sub", None, None),
            P("sub", None),
            P("sub"),
        ),
        out_specs=(P("sub", "crow", "ccol"), P("sub", "crow", "ccol")),
        check_vma=False,
    )
```

time: 127 us -> 111 us (0.87)
  local copies, waits for them, and re-layouts: 14.5 us -> 2.05 us
  waiting for transfers between devices: 44.4 us -> 36.8 us
  Pallas kernels: 31.4 us -> 36.8 us
  other arithmetic: 2.88 us -> 0.77 us
  starting transfers between devices: 31.5 us -> 33.2 us
    unnamed x35 -> x14, local copies, waits for them, and re-layouts: 11.7 us -> 2.05 us
    ppermute x4, waiting for transfers between devices: 16.7 us -> 10 us  [per_device(): lax.ppermute(c, 'sub', route)]
    pallas_call x18 -> x29, Pallas kernels: 31.4 us -> 36.8 us  [the longest x28 35.5 us: call(): pl.pallas_call(body, in_specs=[IN_SMEM] * scalars + [IN_VMEM] * (used - s...]
    ppermute x41 -> x44, starting transfers between devices: 22.8 us -> 26.6 us  [exchange(): lax.ppermute(x, axis, [(i, i ^ bit) for i in range(size) if i ^ bit < size])]
    ppermute x2 -> x0, starting transfers between devices: 2.42 us -> none  [per_device(): lax.ppermute(packed, 'sub', route)]
    dynamic_slice x3 -> x0, local copies, waits for them, and re-layouts: 1.82 us -> none  [the longest x1 0.92 us: coarse_pieces(): z = exchange(lax.dynamic_slice_in_dim(z, y_index * zh, zh, 0), 'crow', bit)]
    ppermute x41 -> x44, waiting for transfers between devices: 27.6 us -> 26.8 us  [exchange(): lax.ppermute(x, axis, [(i, i ^ bit) for i in range(size) if i ^ bit < size])]
  transfers between devices with their start and end apart: 47 -> 48, of which waited for: 14 -> 20; matrix products, arithmetic and copies ran while one was open for 5% -> 1% of each run, Pallas kernels for 12% -> 22%
where the time goes in v2:
time: 111 us
  Pallas kernels  36.8 us (33%)
  waiting for transfers between devices  36.8 us (33%)
  starting transfers between devices  33.2 us (30%)
  local copies, waits for them, and re-layouts  2.05 us (2%)
    pallas_call x28, Pallas kernels, call(): pl.pallas_call(body, in_specs=[IN_SMEM] * scalars + [IN_VMEM] * (used - s...  35.5 us
    ppermute x44, waiting for transfers between devices, exchange(): lax.ppermute(x, axis, [(i, i ^ bit) for i in range(size) if i ^ bit < size])  26.8 us
    ppermute x44, starting transfers between devices, exchange(): lax.ppermute(x, axis, [(i, i ^ bit) for i in range(size) if i ^ bit < size])  26.6 us
    ppermute x4, waiting for transfers between devices, per_device(): lax.ppermute(c, 'sub', route)  10 us
    ppermute x4, starting transfers between devices, per_device(): lax.ppermute(c, 'sub', route)  6.62 us
  transfers between devices with their start and end apart: 48, of which 20 were waited for; matrix products, arithmetic and copies ran while one was open for 1% of the time, Pallas kernels for 22%

profile of v2, /device:TPU:16, one launch (start us, length us, event | category | flops | bytes accessed | tf_op | source)
XLA Modules:
  0.0 110.7 jit_solution(3536104462910282213)
XLA Ops:
  0.6 1.6 %collective-permute-start.3 = (f32[2,384,128]{2,1,0:T(8,128)}, f32[2,384,128]{2,1,0:T(8,128)S(1)}, u32[]{:S(2)}, u32[]{:S(2)}) collective-permute-start(f32[2,384,128]{2,1,0:T(8,128)} %refs_1_.7), channel_id=1, source_target_pairs={{0,4},{2,6},{4,0},{6,2},{1,5},{3,7},{5,1},{7,3},{8,12},{10,14},{12... | collective-permute-start | bytes 1179656 | tf_op jit(solution)/shard_map/ppermute | solution.py:79
  4.2 2.1 %begin.1 = (f32[96,128]{1,0:T(8,128)S(1)}, f32[96,128]{1,0:T(8,128)S(1)}, f32[2,384,128]{2,1,0:T(8,128)S(1)}, f32[16,128]{1,0:T(8,128)S(1)}, f32[288,384]{1,0:T(8,128)S(1)}, /*index=5*/f32[144,384]{1,0:T(8,128)S(1)}) custom-call(s32[2,6]{1,0:T(2,128)S(1)} %copy-done.6, s32[2]{0:T(128)S(1)} %copy-done.4, s32[6,2,128]{2,1,0:T(2,128)S(1)} %bitcast.6, ...), custom_call_target="tpu_custom_call" | custom-call | bytes 2000 | tf_op jit(solution)/shard_map/begin/pallas_call | solution.py:28
  7.6 2.5 %split_inverse.1.refs_1_.refs_0_.refs_2_ = bf16[2,768,1536]{2,1,0:T(8,128)(2,1)S(1)} custom-call(f32[2,384,1536]{2,1,0:T(8,128)} %refs_0_.5, f32[96,128]{1,0:T(8,128)S(1)} %add_up.2.refs_1_.refs_0_), custom_call_target="tpu_custom_call" | custom-call | bytes 2000 | tf_op jit(solution)/shard_map/split_inverse/pallas_call | solution.py:28
  10.1 1.7 %collective-permute-done.3.refs_0_ = f32[2,384,128]{2,1,0:T(8,128)S(1)} collective-permute-done((f32[2,384,128]{2,1,0:T(8,128)}, f32[2,384,128]{2,1,0:T(8,128)S(1)}, u32[]{:S(2)}, u32[]{:S(2)}) %collective-permute-start.3) | collective-permute-done | bytes 393248 | tf_op jit(solution)/shard_map/ppermute | solution.py:79
  12.4 1.5 %collective-permute-start.7 = (f32[144,384]{1,0:T(8,128)S(1)}, f32[144,384]{1,0:T(8,128)S(1)}, u32[]{:S(2)}, u32[]{:S(2)}) collective-permute-start(f32[144,384]{1,0:T(8,128)S(1)} %get-tuple-element.42), channel_id=1, source_target_pairs={{0,4},{2,6},{4,0},{6,2},{1,5},{3,7},{5,1},{7,3},{8,12},{10,14},{12... | collective-permute-start | bytes 663560 | tf_op jit(solution)/shard_map/ppermute | solution.py:79
  14.4 6.4 %collective-permute-done.1.refs_0_ = f32[96,128]{1,0:T(8,128)S(1)} collective-permute-done((f32[96,128]{1,0:T(8,128)S(1)}, f32[96,128]{1,0:T(8,128)S(1)}, u32[]{:S(2)}, u32[]{:S(2)}) %collective-permute-start.1) | collective-permute-done | bytes 49184 | tf_op jit(solution)/shard_map/ppermute | solution.py:79
  22.5 1.6 %collective-permute-start.8 = (f32[144,384]{1,0:T(8,128)S(1)}, f32[144,384]{1,0:T(8,128)S(1)}, u32[]{:S(2)}, u32[]{:S(2)}) collective-permute-start(f32[144,384]{1,0:T(8,128)S(1)} %relay.7.refs_1_), channel_id=1, source_target_pairs={{0,1},{1,0},{2,3},{3,2},{4,5},{5,4},{6,7},{7,6},{8,9},{9,8},{10,11... | collective-permute-start | bytes 663560 | tf_op jit(solution)/shard_map/ppermute | solution.py:79
  24.4 2.7 %collective-permute-start.6 = (f32[112,128]{1,0:T(8,128)S(1)}, f32[112,128]{1,0:T(8,128)S(1)}, u32[]{:S(2)}, u32[]{:S(2)}) collective-permute-start(f32[112,128]{1,0:T(8,128)S(1)} %add_up.3.refs_1_.refs_6_.refs_2_), channel_id=1, source_target_pairs={{0,24},{8,16},{16,8},{24,0},{1,25},{9,17},{17,9},{25,1},{2,26},{10... | collective-permute-start | bytes 172040 | tf_op jit(solution)/shard_map/ppermute | solution.py:79
  27.1 1.6 %collective-permute-start.18 = (f32[384,128]{1,0:T(8,128)S(1)}, f32[384,128]{1,0:T(8,128)S(1)}, u32[]{:S(2)}, u32[]{:S(2)}) collective-permute-start(f32[384,128]{1,0:T(8,128)S(1)} %local_solve.2.refs_5_.refs_3_), channel_id=1, source_target_pairs={{0,4},{2,6},{4,0},{6,2},{1,5},{3,7},{5,1},{7,3},{8,12},{10,14},{12... | collective-permute-start | bytes 589832 | tf_op jit(solution)/shard_map/ppermute | solution.py:79
  28.7 0.9 collective-permute-done.12.refs_4_
  29.6 1.5 %collective-permute-start.21 = (f32[384,128]{1,0:T(8,128)S(1)}, f32[384,128]{1,0:T(8,128)S(1)}, u32[]{:S(2)}, u32[]{:S(2)}) collective-permute-start(f32[384,128]{1,0:T(8,128)S(1)} %local_solve.3.refs_3_), channel_id=1, source_target_pairs={{0,4},{2,6},{4,0},{6,2},{1,5},{3,7},{5,1},{7,3},{8,12},{10,14},{12... | collective-permute-start | bytes 589832 | tf_op jit(solution)/shard_map/ppermute | solution.py:79
  31.1 1.9 %collective-permute-done.6.refs_2_.refs_5_ = f32[112,128]{1,0:T(8,128)S(1)} collective-permute-done((f32[112,128]{1,0:T(8,128)S(1)}, f32[112,128]{1,0:T(8,128)S(1)}, u32[]{:S(2)}, u32[]{:S(2)}) %collective-permute-start.6) | collective-permute-done | bytes 57376 | tf_op jit(solution)/shard_map/ppermute | solution.py:79
  33.0 1.8 %collective-permute-start.5 = (f32[112,128]{1,0:T(8,128)S(1)}, f32[112,128]{1,0:T(8,128)S(1)}, u32[]{:S(2)}, u32[]{:S(2)}) collective-permute-start(f32[112,128]{1,0:T(8,128)S(1)} %add_up.3.refs_1_.refs_6_.refs_2_), channel_id=1, source_target_pairs={{0,8},{8,0},{16,24},{24,16},{1,9},{9,1},{17,25},{25,17},{2,10},{10... | collective-permute-start | bytes 172040 | tf_op jit(solution)/shard_map/ppermute | solution.py:79
  34.8 2.4 %collective-permute-done.5.refs_1_.refs_3_ = f32[112,128]{1,0:T(8,128)S(1)} collective-permute-done((f32[112,128]{1,0:T(8,128)S(1)}, f32[112,128]{1,0:T(8,128)S(1)}, u32[]{:S(2)}, u32[]{:S(2)}) %collective-permute-start.5) | collective-permute-done | bytes 57376 | tf_op jit(solution)/shard_map/ppermute | solution.py:79
  38.6 1.1 collective-permute-done.16.refs_9_
  40.9 1.0 place_coarse.1
  41.8 1.3 %prepare.1 = (s32[3,6,128]{2,1,0:T(8,128)S(1)}, s32[8,128]{1,0:T(8,128)S(1)}) custom-call(f32[16,128]{1,0:T(8,128)S(1)} %get-tuple-element.38.refs_2_.refs_0_, f32[112,128]{1,0:T(8,128)S(1)} %collective-permute-done.5.refs_1_.refs_3_, f32[112,128]{1,0:T(8,128)S(1)} %collective-permute-done.6.refs_2_.refs_5_, ...), custom_call_target="tpu_custom_call" | custom-call | bytes 1000 | tf_op jit(solution)/shard_map/prepare/pallas_call | solution.py:310
  43.1 2.5 %split_stiffness.1.refs_10_.refs_0_ = bf16[2,768,1536]{2,1,0:T(8,128)(2,1)S(1)} custom-call(f32[2,384,1536]{2,1,0:T(8,128)} %refs_0_.6, s32[8,128]{1,0:T(8,128)S(1)} %get-tuple-element.44.refs_1_.refs_0_), custom_call_target="tpu_custom_call" | custom-call | bytes 2000 | tf_op jit(solution)/shard_map/split_stiffness/pallas_call | solution.py:28
  45.6 1.1 lift_coarse.2.refs_1_.refs_7_
  47.5 0.8 correct.5
  48.3 3.0 %select_rows.2 = (f32[6,128,128]{2,1,0:T(8,128)S(1)}, f32[6,128,128]{2,1,0:T(8,128)S(1)}, f32[6,128,128]{2,1,0:T(8,128)S(1)}) custom-call(s32[8,128]{1,0:T(8,128)S(1)} %get-tuple-element.44.refs_1_.refs_0_, s32[3,6,128]{2,1,0:T(8,128)S(1)} %get-tuple-element.47.refs_1_, bf16[1536,256]{1,0:T(8,128)(2,1)S(1)} %get-tuple-element.49.refs_2_, ...), custom_call_target="tpu_custom_call" | custom-call | bytes 1500 | tf_op jit(solution)/shard_map/select_rows/pallas_call | solution.py:28
  51.4 0.9 collective-permute-start.23
  52.2 1.9 %collective-permute-start.24 = (f32[6,128,128]{2,1,0:T(8,128)S(1)}, f32[6,128,128]{2,1,0:T(8,128)S(1)}, u32[]{:S(2)}, u32[]{:S(2)}) collective-permute-start(f32[6,128,128]{2,1,0:T(8,128)S(1)} %get-tuple-element.55), channel_id=1, source_target_pairs={{8,16},{16,8},{9,17},{17,9},{10,18},{18,10},{11,19},{19,11},{12,20... | collective-permute-start | bytes 1179656 | tf_op jit(solution)/shard_map/ppermute | solution.py:705
  54.9 1.3 %collective-permute-start.25 = (f32[384,128]{1,0:T(8,128)S(1)}, f32[384,128]{1,0:T(8,128)S(1)}, u32[]{:S(2)}, u32[]{:S(2)}) collective-permute-start(f32[384,128]{1,0:T(8,128)S(1)} %get-tuple-element.50.refs_7_.refs_4_.refs_2_), channel_id=1, source_target_pairs={{0,4},{2,6},{4,0},{6,2},{1,5},{3,7},{5,1},{7,3},{8,12},{10,14},{12... | collective-permute-start | bytes 589832 | tf_op jit(solution)/shard_map/ppermute | solution.py:79
  56.3 6.7 %fold_targets.1 = (bf16[2,384,768]{2,1,0:T(8,128)(2,1)S(1)}, bf16[2,768,768]{2,1,0:T(8,128)(2,1)S(1)}, bf16[1,192,768]{2,1,0:T(8,128)(2,1)S(1)}) custom-call(s32[2]{0:T(128)S(1)} %copy-done.5, s32[6,2,128]{2,1,0:T(2,128)S(1)} %bitcast.7, bf16[2,768,1536]{2,1,0:T(8,128)(2,1)S(1)} %split_inverse.1.refs_1_.refs_0_.refs_2_, ...), custom_call_target="tpu_custom_call" | custom-call | bytes 4500 | tf_op jit(solution)/shard_map/fold_targets/pallas_call | solution.py:28
  63.0 2.6 %collective-permute-done.25.refs_0_ = f32[384,128]{1,0:T(8,128)S(1)} collective-permute-done((f32[384,128]{1,0:T(8,128)S(1)}, f32[384,128]{1,0:T(8,128)S(1)}, u32[]{:S(2)}, u32[]{:S(2)}) %collective-permute-start.25) | collective-permute-done | bytes 196640 | tf_op jit(solution)/shard_map/ppermute | solution.py:79
  65.7 1.5 %couple.2.refs_2_.refs_8_.refs_1_ = f32[6,128,128]{2,1,0:T(8,128)S(1)} custom-call(s32[8,128]{1,0:T(8,128)S(1)} %get-tuple-element.44.refs_1_.refs_0_, f32[2,6,128,128]{3,2,1,0:T(8,128)S(1)} %copy-done.1, f32[6,128,128]{2,1,0:T(8,128)S(1)} %get-tuple-element.52.refs_4_.refs_2_, f32[6,128,128]{2,1,0:T(8,128)S(1)} %collective-permute-done.23.refs_3_, ...), custom_call_target="tpu_custom_call" | custom-call | bytes 800 | tf_op jit(solution)/shard_map/couple/pallas_call | solution.py:28
  68.4 0.9 collective-permute-done.28.refs_5_
  69.6 1.2 %local_solve_inflow.2 = (f32[384,128]{1,0:T(8,128)S(1)}, bf16[1536,256]{1,0:T(8,128)(2,1)S(1)}) custom-call(bf16[2,768,1536]{2,1,0:T(8,128)(2,1)S(1)} %split_inverse.1.refs_1_.refs_0_.refs_2_, bf16[2,768,768]{2,1,0:T(8,128)(2,1)S(1)} %get-tuple-element.56.refs_1_, f32[6,128,128]{2,1,0:T(8,128)S(1)} %couple.2.refs_2_.refs_8_.refs_1_, ...), custom_call_target="tpu_custom_call" | custom-call | bytes 1200 | tf_op jit(solution)/shard_map/local_solve_inflow/pallas_call | solution.py:28
  71.4 1.2 %local_solve_inflow.3 = (f32[384,128]{1,0:T(8,128)S(1)}, bf16[1536,256]{1,0:T(8,128)(2,1)S(1)}) custom-call(bf16[2,768,1536]{2,1,0:T(8,128)(2,1)S(1)} %split_inverse.1.refs_1_.refs_0_.refs_2_, bf16[2,768,768]{2,1,0:T(8,128)(2,1)S(1)} %get-tuple-element.56.refs_1_, f32[6,128,128]{2,1,0:T(8,128)S(1)} %couple.2.refs_2_.refs_8_.refs_1_, ...), custom_call_target="tpu_custom_call" | custom-call | bytes 1200 | tf_op jit(solution)/shard_map/local_solve_inflow/pallas_call | solution.py:28
  72.6 1.6 %collective-permute-start.43 = (f32[384,128]{1,0:T(8,128)S(1)}, f32[384,128]{1,0:T(8,128)S(1)}, u32[]{:S(2)}, u32[]{:S(2)}) collective-permute-start(f32[384,128]{1,0:T(8,128)S(1)} %get-tuple-element.61.refs_5_.refs_3_), channel_id=1, source_target_pairs={{0,4},{2,6},{4,0},{6,2},{1,5},{3,7},{5,1},{7,3},{8,12},{10,14},{12... | collective-permute-start | bytes 589832 | tf_op jit(solution)/shard_map/ppermute | solution.py:79
  74.9 1.6 %collective-permute-start.34 = (f32[96,128]{1,0:T(8,128)S(1)}, f32[96,128]{1,0:T(8,128)S(1)}, u32[]{:S(2)}, u32[]{:S(2)}) collective-permute-start(f32[96,128]{1,0:T(8,128)S(1)} %restrict.1.refs_2_.refs_10_), channel_id=1, source_target_pairs={{0,24},{8,16},{16,8},{24,0},{1,25},{9,17},{17,9},{25,1},{2,26},{10... | collective-permute-start | bytes 147464 | tf_op jit(solution)/shard_map/ppermute | solution.py:79
  76.7 1.8 %collective-permute-start.32 = (f32[96,128]{1,0:T(8,128)S(1)}, f32[96,128]{1,0:T(8,128)S(1)}, u32[]{:S(2)}, u32[]{:S(2)}) collective-permute-start(f32[96,128]{1,0:T(8,128)S(1)} %restrict.1.refs_2_.refs_10_), channel_id=1, source_target_pairs={{0,8},{8,0},{16,24},{24,16},{1,9},{9,1},{17,25},{25,17},{2,10},{10... | collective-permute-start | bytes 147464 | tf_op jit(solution)/shard_map/ppermute | solution.py:79
  78.4 1.4 %collective-permute-done.34.refs_5_ = f32[96,128]{1,0:T(8,128)S(1)} collective-permute-done((f32[96,128]{1,0:T(8,128)S(1)}, f32[96,128]{1,0:T(8,128)S(1)}, u32[]{:S(2)}, u32[]{:S(2)}) %collective-permute-start.34) | collective-permute-done | bytes 49184 | tf_op jit(solution)/shard_map/ppermute | solution.py:79
  80.3 1.4 %collective-permute-done.33.refs_4_ = f32[96,128]{1,0:T(8,128)S(1)} collective-permute-done((f32[96,128]{1,0:T(8,128)S(1)}, f32[96,128]{1,0:T(8,128)S(1)}, u32[]{:S(2)}, u32[]{:S(2)}) %collective-permute-start.33) | collective-permute-done | bytes 49184 | tf_op jit(solution)/shard_map/ppermute | solution.py:79
  82.5 1.0 collective-permute-done.38.refs_9_
  83.8 1.0 collective-permute-done.37.refs_8_
  85.0 1.0 collective-permute-done.36.refs_7_
  86.0 1.1 lift_coarse.3.refs_1_.refs_8_
  87.1 0.8 correct.6
  87.9 0.8 correct.7
  88.7 3.0 %select_rows.3 = (f32[6,128,128]{2,1,0:T(8,128)S(1)}, f32[6,128,128]{2,1,0:T(8,128)S(1)}, f32[6,128,128]{2,1,0:T(8,128)S(1)}) custom-call(s32[8,128]{1,0:T(8,128)S(1)} %get-tuple-element.44.refs_1_.refs_0_, s32[3,6,128]{2,1,0:T(8,128)S(1)} %get-tuple-element.47.refs_1_, bf16[1536,256]{1,0:T(8,128)(2,1)S(1)} %get-tuple-element.68.refs_2_, ...), custom_call_target="tpu_custom_call" | custom-call | bytes 1500 | tf_op jit(solution)/shard_map/select_rows/pallas_call | solution.py:28
  92.5 3.1 %collective-permute-start.46 = (f32[6,128,128]{2,1,0:T(8,128)S(1)}, f32[6,128,128]{2,1,0:T(8,128)S(1)}, u32[]{:S(2)}, u32[]{:S(2)}) collective-permute-start(f32[6,128,128]{2,1,0:T(8,128)S(1)} %get-tuple-element.72), channel_id=1, source_target_pairs={{8,16},{16,8},{9,17},{17,9},{10,18},{18,10},{11,19},{19,11},{12,20... | collective-permute-start | bytes 1179656 | tf_op jit(solution)/shard_map/ppermute | solution.py:705
  95.6 6.7 %collective-permute-done.45.refs_3_ = f32[6,128,128]{2,1,0:T(8,128)S(1)} collective-permute-done((f32[6,128,128]{2,1,0:T(8,128)S(1)}, f32[6,128,128]{2,1,0:T(8,128)S(1)}, u32[]{:S(2)}, u32[]{:S(2)}) %collective-permute-start.45) | collective-permute-done | bytes 393248 | tf_op jit(solution)/shard_map/ppermute | solution.py:705
  102.3 3.3 %collective-permute-done.46.refs_4_ = f32[6,128,128]{2,1,0:T(8,128)S(1)} collective-permute-done((f32[6,128,128]{2,1,0:T(8,128)S(1)}, f32[6,128,128]{2,1,0:T(8,128)S(1)}, u32[]{:S(2)}, u32[]{:S(2)}) %collective-permute-start.46) | collective-permute-done | bytes 393248 | tf_op jit(solution)/shard_map/ppermute | solution.py:705
  105.6 1.5 %couple.3.refs_2_ = f32[6,128,128]{2,1,0:T(8,128)S(1)} custom-call(s32[8,128]{1,0:T(8,128)S(1)} %get-tuple-element.44.refs_1_.refs_0_, f32[2,6,128,128]{3,2,1,0:T(8,128)S(1)} %copy-done.1, f32[6,128,128]{2,1,0:T(8,128)S(1)} %get-tuple-element.70.refs_2_, f32[6,128,128]{2,1,0:T(8,128)S(1)} %collective-permute-done.45.refs_3_, ...), custom_call_target="tpu_custom_call" | custom-call | bytes 800 | tf_op jit(solution)/shard_map/couple/pallas_call | solution.py:28
  108.0 0.9 collective-permute-done.47.refs_4_
  108.9 1.8 %add_inflow.1 = f32[2,384,128]{2,1,0:T(8,128)} custom-call(bf16[2,384,768]{2,1,0:T(8,128)(2,1)S(1)} %get-tuple-element.67.refs_0_, f32[6,128,128]{2,1,0:T(8,128)S(1)} %couple.2.refs_2_.refs_8_.refs_1_, f32[6,128,128]{2,1,0:T(8,128)S(1)} %couple.3.refs_2_, f32[6,128,128]{2,1,0:T(8,128)S(1)} %collective-permute-done.27.refs_3_, ...), custom_call_target="tpu_custom_call" | custom-call | bytes 800 | tf_op jit(solution)/shard_map/add_inflow/pallas_call | solution.py:28
  (92 shorter events, 16.8 us)
Async XLA Ops:
  0.6 11.1 %collective-permute-start.3 = (f32[2,384,128]{2,1,0:T(8,128)}, f32[2,384,128]{2,1,0:T(8,128)S(1)}, u32[]{:S(2)}, u32[]{:S(2)}) collective-permute-start(f32[2,384,128]{2,1,0:T(8,128)} %refs_1_.7), channel_id=1, source_target_pairs={{0,4},{2,6},{4,0},{6,2},{1,5},{3,7},{5,1},{7,3},{8,12},{10,14},{12... | collective-permute-start | bytes 1179656 | tf_op jit(solution)/shard_map/ppermute | solution.py:79
  6.3 1.3 %collective-permute-start = (f32[96,128]{1,0:T(8,128)S(1)}, f32[96,128]{1,0:T(8,128)S(1)}, u32[]{:S(2)}, u32[]{:S(2)}) collective-permute-start(f32[96,128]{1,0:T(8,128)S(1)} %get-tuple-element.40), channel_id=1, source_target_pairs={{0,2},{2,0},{4,6},{6,4},{1,3},{3,1},{5,7},{7,5},{8,10},{10,8},{12,... | collective-permute-start | bytes 147464 | tf_op jit(solution)/shard_map/ppermute | solution.py:79
  6.4 14.5 %collective-permute-start.2 = (f32[2,384,128]{2,1,0:T(8,128)}, f32[2,384,128]{2,1,0:T(8,128)S(1)}, u32[]{:S(2)}, u32[]{:S(2)}) collective-permute-start(f32[2,384,128]{2,1,0:T(8,128)} %refs_1_.7), channel_id=1, source_target_pairs={{0,2},{2,0},{4,6},{6,4},{1,3},{3,1},{5,7},{7,5},{8,10},{10,8},{12,... | collective-permute-start | bytes 1179656 | tf_op jit(solution)/shard_map/ppermute | solution.py:79
  11.8 9.1 %collective-permute-start.4 = (f32[2,384,128]{2,1,0:T(8,128)S(1)}, f32[2,384,128]{2,1,0:T(8,128)S(1)}, u32[]{:S(2)}, u32[]{:S(2)}) collective-permute-start(f32[2,384,128]{2,1,0:T(8,128)S(1)} %relay.6.refs_3_), channel_id=1, source_target_pairs={{0,2},{2,0},{4,6},{6,4},{1,3},{3,1},{5,7},{7,5},{8,10},{10,8},{12,... | collective-permute-start | bytes 1179656 | tf_op jit(solution)/shard_map/ppermute | solution.py:79
  11.9 15.2 %collective-permute-start.9 = (f32[288,384]{1,0:T(8,128)S(1)}, f32[288,384]{1,0:T(8,128)S(1)}, u32[]{:S(2)}, u32[]{:S(2)}) collective-permute-start(f32[288,384]{1,0:T(8,128)S(1)} %get-tuple-element.41.refs_0_), channel_id=1, source_target_pairs={{0,2},{2,0},{4,6},{6,4},{1,3},{3,1},{5,7},{7,5},{8,10},{10,8},{12,... | collective-permute-start | bytes 1327112 | tf_op jit(solution)/shard_map/ppermute | solution.py:79
  12.4 10.1 %collective-permute-start.7 = (f32[144,384]{1,0:T(8,128)S(1)}, f32[144,384]{1,0:T(8,128)S(1)}, u32[]{:S(2)}, u32[]{:S(2)}) collective-permute-start(f32[144,384]{1,0:T(8,128)S(1)} %get-tuple-element.42), channel_id=1, source_target_pairs={{0,4},{2,6},{4,0},{6,2},{1,5},{3,7},{5,1},{7,3},{8,12},{10,14},{12... | collective-permute-start | bytes 663560 | tf_op jit(solution)/shard_map/ppermute | solution.py:79
  13.9 7.0 %collective-permute-start.1 = (f32[96,128]{1,0:T(8,128)S(1)}, f32[96,128]{1,0:T(8,128)S(1)}, u32[]{:S(2)}, u32[]{:S(2)}) collective-permute-start(f32[96,128]{1,0:T(8,128)S(1)} %add_up.2.refs_1_.refs_0_), channel_id=1, source_target_pairs={{0,4},{2,6},{4,0},{6,2},{1,5},{3,7},{5,1},{7,3},{8,12},{10,14},{12... | collective-permute-start | bytes 147464 | tf_op jit(solution)/shard_map/ppermute | solution.py:79
  22.5 14.7 %collective-permute-start.8 = (f32[144,384]{1,0:T(8,128)S(1)}, f32[144,384]{1,0:T(8,128)S(1)}, u32[]{:S(2)}, u32[]{:S(2)}) collective-permute-start(f32[144,384]{1,0:T(8,128)S(1)} %relay.7.refs_1_), channel_id=1, source_target_pairs={{0,1},{1,0},{2,3},{3,2},{4,5},{5,4},{6,7},{7,6},{8,9},{9,8},{10,11... | collective-permute-start | bytes 663560 | tf_op jit(solution)/shard_map/ppermute | solution.py:79
  24.1 3.0 %collective-permute-start.13 = (f32[112,128]{1,0:T(8,128)S(1)}, f32[112,128]{1,0:T(8,128)S(1)}, u32[]{:S(2)}, u32[]{:S(2)}) collective-permute-start(f32[112,128]{1,0:T(8,128)S(1)} %add_up.3.refs_1_.refs_6_.refs_2_), channel_id=1, source_target_pairs={{0,2},{2,0},{4,6},{6,4},{1,3},{3,1},{5,7},{7,5},{8,10},{10,8},{12,... | collective-permute-start | bytes 172040 | tf_op jit(solution)/shard_map/ppermute | solution.py:79
  24.1 5.5 %collective-permute-start.12 = (f32[112,128]{1,0:T(8,128)S(1)}, f32[112,128]{1,0:T(8,128)S(1)}, u32[]{:S(2)}, u32[]{:S(2)}) collective-permute-start(f32[112,128]{1,0:T(8,128)S(1)} %add_up.3.refs_1_.refs_6_.refs_2_), channel_id=1, source_target_pairs={{0,16},{8,24},{16,0},{24,8},{1,17},{9,25},{17,1},{25,9},{2,18},{10... | collective-permute-start | bytes 172040 | tf_op jit(solution)/shard_map/ppermute | solution.py:79
  24.4 8.6 %collective-permute-start.6 = (f32[112,128]{1,0:T(8,128)S(1)}, f32[112,128]{1,0:T(8,128)S(1)}, u32[]{:S(2)}, u32[]{:S(2)}) collective-permute-start(f32[112,128]{1,0:T(8,128)S(1)} %add_up.3.refs_1_.refs_6_.refs_2_), channel_id=1, source_target_pairs={{0,24},{8,16},{16,8},{24,0},{1,25},{9,17},{17,9},{25,1},{2,26},{10... | collective-permute-start | bytes 172040 | tf_op jit(solution)/shard_map/ppermute | solution.py:79
  27.1 13.2 %collective-permute-start.10 = (f32[144,384]{1,0:T(8,128)S(1)}, f32[144,384]{1,0:T(8,128)S(1)}, u32[]{:S(2)}, u32[]{:S(2)}) collective-permute-start(f32[144,384]{1,0:T(8,128)S(1)} %relay.7.refs_1_), channel_id=1, source_target_pairs={{0,2},{2,0},{4,6},{6,4},{1,3},{3,1},{5,7},{7,5},{8,10},{10,8},{12,... | collective-permute-start | bytes 663560 | tf_op jit(solution)/shard_map/ppermute | solution.py:79
  27.1 12.7 %collective-permute-start.18 = (f32[384,128]{1,0:T(8,128)S(1)}, f32[384,128]{1,0:T(8,128)S(1)}, u32[]{:S(2)}, u32[]{:S(2)}) collective-permute-start(f32[384,128]{1,0:T(8,128)S(1)} %local_solve.2.refs_5_.refs_3_), channel_id=1, source_target_pairs={{0,4},{2,6},{4,0},{6,2},{1,5},{3,7},{5,1},{7,3},{8,12},{10,14},{12... | collective-permute-start | bytes 589832 | tf_op jit(solution)/shard_map/ppermute | solution.py:79
  29.6 10.6 %collective-permute-start.21 = (f32[384,128]{1,0:T(8,128)S(1)}, f32[384,128]{1,0:T(8,128)S(1)}, u32[]{:S(2)}, u32[]{:S(2)}) collective-permute-start(f32[384,128]{1,0:T(8,128)S(1)} %local_solve.3.refs_3_), channel_id=1, source_target_pairs={{0,4},{2,6},{4,0},{6,2},{1,5},{3,7},{5,1},{7,3},{8,12},{10,14},{12... | collective-permute-start | bytes 589832 | tf_op jit(solution)/shard_map/ppermute | solution.py:79
  33.0 4.2 %collective-permute-start.5 = (f32[112,128]{1,0:T(8,128)S(1)}, f32[112,128]{1,0:T(8,128)S(1)}, u32[]{:S(2)}, u32[]{:S(2)}) collective-permute-start(f32[112,128]{1,0:T(8,128)S(1)} %add_up.3.refs_1_.refs_6_.refs_2_), channel_id=1, source_target_pairs={{0,8},{8,0},{16,24},{24,16},{1,9},{9,1},{17,25},{25,17},{2,10},{10... | collective-permute-start | bytes 172040 | tf_op jit(solution)/shard_map/ppermute | solution.py:79
  37.2 1.2 %collective-permute-start.15 = (f32[112,128]{1,0:T(8,128)S(1)}, f32[112,128]{1,0:T(8,128)S(1)}, u32[]{:S(2)}, u32[]{:S(2)}) collective-permute-start(f32[112,128]{1,0:T(8,128)S(1)} %collective-permute-done.12.refs_4_), channel_id=1, source_target_pairs={{0,2},{2,0},{4,6},{6,4},{1,3},{3,1},{5,7},{7,5},{8,10},{10,8},{12,... | collective-permute-start | bytes 172040 | tf_op jit(solution)/shard_map/ppermute | solution.py:79
  37.2 3.5 %collective-permute-start.11 = (f32[144,384]{1,0:T(8,128)S(1)}, f32[144,384]{1,0:T(8,128)S(1)}, u32[]{:S(2)}, u32[]{:S(2)}) collective-permute-start(f32[144,384]{1,0:T(8,128)S(1)} %collective-permute-done.8.refs_2_), channel_id=1, source_target_pairs={{0,2},{2,0},{4,6},{6,4},{1,3},{3,1},{5,7},{7,5},{8,10},{10,8},{12,... | collective-permute-start | bytes 663560 | tf_op jit(solution)/shard_map/ppermute | solution.py:79
  38.4 1.2 %collective-permute-start.16 = (f32[112,128]{1,0:T(8,128)S(1)}, f32[112,128]{1,0:T(8,128)S(1)}, u32[]{:S(2)}, u32[]{:S(2)}) collective-permute-start(f32[112,128]{1,0:T(8,128)S(1)} %collective-permute-done.6.refs_2_.refs_5_), channel_id=1, source_target_pairs={{0,2},{2,0},{4,6},{6,4},{1,3},{3,1},{5,7},{7,5},{8,10},{10,8},{12,... | collective-permute-start | bytes 172040 | tf_op jit(solution)/shard_map/ppermute | solution.py:79
  39.7 7.0 %collective-permute-start.17 = (f32[384,128]{1,0:T(8,128)S(1)}, f32[384,128]{1,0:T(8,128)S(1)}, u32[]{:S(2)}, u32[]{:S(2)}) collective-permute-start(f32[384,128]{1,0:T(8,128)S(1)} %local_solve.2.refs_5_.refs_3_), channel_id=1, source_target_pairs={{0,2},{2,0},{4,6},{6,4},{1,3},{3,1},{5,7},{7,5},{8,10},{10,8},{12,... | collective-permute-start | bytes 589832 | tf_op jit(solution)/shard_map/ppermute | solution.py:79
  39.8 6.8 %collective-permute-start.19 = (f32[384,128]{1,0:T(8,128)S(1)}, f32[384,128]{1,0:T(8,128)S(1)}, u32[]{:S(2)}, u32[]{:S(2)}) collective-permute-start(f32[384,128]{1,0:T(8,128)S(1)} %collective-permute-done.18.refs_5_), channel_id=1, source_target_pairs={{0,2},{2,0},{4,6},{6,4},{1,3},{3,1},{5,7},{7,5},{8,10},{10,8},{12,... | collective-permute-start | bytes 589832 | tf_op jit(solution)/shard_map/ppermute | solution.py:79
  40.2 7.3 %collective-permute-start.20 = (f32[384,128]{1,0:T(8,128)S(1)}, f32[384,128]{1,0:T(8,128)S(1)}, u32[]{:S(2)}, u32[]{:S(2)}) collective-permute-start(f32[384,128]{1,0:T(8,128)S(1)} %local_solve.3.refs_3_), channel_id=1, source_target_pairs={{0,2},{2,0},{4,6},{6,4},{1,3},{3,1},{5,7},{7,5},{8,10},{10,8},{12,... | collective-permute-start | bytes 589832 | tf_op jit(solution)/shard_map/ppermute | solution.py:79
  40.3 7.2 %collective-permute-start.22 = (f32[384,128]{1,0:T(8,128)S(1)}, f32[384,128]{1,0:T(8,128)S(1)}, u32[]{:S(2)}, u32[]{:S(2)}) collective-permute-start(f32[384,128]{1,0:T(8,128)S(1)} %collective-permute-done.21.refs_5_), channel_id=1, source_target_pairs={{0,2},{2,0},{4,6},{6,4},{1,3},{3,1},{5,7},{7,5},{8,10},{10,8},{12,... | collective-permute-start | bytes 589832 | tf_op jit(solution)/shard_map/ppermute | solution.py:79
  40.7 4.9 %collective-permute-start.14 = (f32[112,128]{1,0:T(8,128)S(1)}, f32[112,128]{1,0:T(8,128)S(1)}, u32[]{:S(2)}, u32[]{:S(2)}) collective-permute-start(f32[112,128]{1,0:T(8,128)S(1)} %collective-permute-done.5.refs_1_.refs_3_), channel_id=1, source_target_pairs={{0,2},{2,0},{4,6},{6,4},{1,3},{3,1},{5,7},{7,5},{8,10},{10,8},{12,... | collective-permute-start | bytes 172040 | tf_op jit(solution)/shard_map/ppermute | solution.py:79
  51.4 14.3 %collective-permute-start.23 = (f32[6,128,128]{2,1,0:T(8,128)S(1)}, f32[6,128,128]{2,1,0:T(8,128)S(1)}, u32[]{:S(2)}, u32[]{:S(2)}) collective-permute-start(f32[6,128,128]{2,1,0:T(8,128)S(1)} %get-tuple-element.54), channel_id=1, source_target_pairs={{0,8},{8,0},{16,24},{24,16},{1,9},{9,1},{17,25},{25,17},{2,10},{10... | collective-permute-start | bytes 1179656 | tf_op jit(solution)/shard_map/ppermute | solution.py:705
  52.2 13.5 %collective-permute-start.24 = (f32[6,128,128]{2,1,0:T(8,128)S(1)}, f32[6,128,128]{2,1,0:T(8,128)S(1)}, u32[]{:S(2)}, u32[]{:S(2)}) collective-permute-start(f32[6,128,128]{2,1,0:T(8,128)S(1)} %get-tuple-element.55), channel_id=1, source_target_pairs={{8,16},{16,8},{9,17},{17,9},{10,18},{18,10},{11,19},{19,11},{12,20... | collective-permute-start | bytes 1179656 | tf_op jit(solution)/shard_map/ppermute | solution.py:705
  54.2 8.8 %collective-permute-start.26 = (f32[384,128]{1,0:T(8,128)S(1)}, f32[384,128]{1,0:T(8,128)S(1)}, u32[]{:S(2)}, u32[]{:S(2)}) collective-permute-start(f32[384,128]{1,0:T(8,128)S(1)} %get-tuple-element.57.refs_4_.refs_2_), channel_id=1, source_target_pairs={{0,4},{2,6},{4,0},{6,2},{1,5},{3,7},{5,1},{7,3},{8,12},{10,14},{12... | collective-permute-start | bytes 589832 | tf_op jit(solution)/shard_map/ppermute | solution.py:79
  54.9 10.7 %collective-permute-start.25 = (f32[384,128]{1,0:T(8,128)S(1)}, f32[384,128]{1,0:T(8,128)S(1)}, u32[]{:S(2)}, u32[]{:S(2)}) collective-permute-start(f32[384,128]{1,0:T(8,128)S(1)} %get-tuple-element.50.refs_7_.refs_4_.refs_2_), channel_id=1, source_target_pairs={{0,4},{2,6},{4,0},{6,2},{1,5},{3,7},{5,1},{7,3},{8,12},{10,14},{12... | collective-permute-start | bytes 589832 | tf_op jit(solution)/shard_map/ppermute | solution.py:79
  67.2 2.4 %collective-permute-start.27 = (f32[6,128,128]{2,1,0:T(8,128)S(1)}, f32[6,128,128]{2,1,0:T(8,128)S(1)}, u32[]{:S(2)}, u32[]{:S(2)}) collective-permute-start(f32[6,128,128]{2,1,0:T(8,128)S(1)} %couple.2.refs_2_.refs_8_.refs_1_), channel_id=1, source_target_pairs={{0,2},{2,0},{4,6},{6,4},{1,3},{3,1},{5,7},{7,5},{8,10},{10,8},{12,... | collective-permute-start | bytes 1179656 | tf_op jit(solution)/shard_map/ppermute | solution.py:79
  67.3 2.0 %collective-permute-start.28 = (f32[384,128]{1,0:T(8,128)S(1)}, f32[384,128]{1,0:T(8,128)S(1)}, u32[]{:S(2)}, u32[]{:S(2)}) collective-permute-start(f32[384,128]{1,0:T(8,128)S(1)} %get-tuple-element.50.refs_7_.refs_4_.refs_2_), channel_id=1, source_target_pairs={{0,2},{2,0},{4,6},{6,4},{1,3},{3,1},{5,7},{7,5},{8,10},{10,8},{12,... | collective-permute-start | bytes 589832 | tf_op jit(solution)/shard_map/ppermute | solution.py:79
  67.8 1.8 %collective-permute-start.29 = (f32[384,128]{1,0:T(8,128)S(1)}, f32[384,128]{1,0:T(8,128)S(1)}, u32[]{:S(2)}, u32[]{:S(2)}) collective-permute-start(f32[384,128]{1,0:T(8,128)S(1)} %relay.8.refs_5_.refs_6_), channel_id=1, source_target_pairs={{0,2},{2,0},{4,6},{6,4},{1,3},{3,1},{5,7},{7,5},{8,10},{10,8},{12,... | collective-permute-start | bytes 589832 | tf_op jit(solution)/shard_map/ppermute | solution.py:79
  67.9 3.5 %collective-permute-start.30 = (f32[384,128]{1,0:T(8,128)S(1)}, f32[384,128]{1,0:T(8,128)S(1)}, u32[]{:S(2)}, u32[]{:S(2)}) collective-permute-start(f32[384,128]{1,0:T(8,128)S(1)} %get-tuple-element.57.refs_4_.refs_2_), channel_id=1, source_target_pairs={{0,2},{2,0},{4,6},{6,4},{1,3},{3,1},{5,7},{7,5},{8,10},{10,8},{12,... | collective-permute-start | bytes 589832 | tf_op jit(solution)/shard_map/ppermute | solution.py:79
  68.3 3.1 %collective-permute-start.31 = (f32[384,128]{1,0:T(8,128)S(1)}, f32[384,128]{1,0:T(8,128)S(1)}, u32[]{:S(2)}, u32[]{:S(2)}) collective-permute-start(f32[384,128]{1,0:T(8,128)S(1)} %relay.9.refs_6_), channel_id=1, source_target_pairs={{0,2},{2,0},{4,6},{6,4},{1,3},{3,1},{5,7},{7,5},{8,10},{10,8},{12,... | collective-permute-start | bytes 589832 | tf_op jit(solution)/shard_map/ppermute | solution.py:79
  70.8 9.1 %collective-permute-start.40 = (f32[384,128]{1,0:T(8,128)S(1)}, f32[384,128]{1,0:T(8,128)S(1)}, u32[]{:S(2)}, u32[]{:S(2)}) collective-permute-start(f32[384,128]{1,0:T(8,128)S(1)} %get-tuple-element.59.refs_8_.refs_3_), channel_id=1, source_target_pairs={{0,4},{2,6},{4,0},{6,2},{1,5},{3,7},{5,1},{7,3},{8,12},{10,14},{12... | collective-permute-start | bytes 589832 | tf_op jit(solution)/shard_map/ppermute | solution.py:79
  72.6 9.4 %collective-permute-start.43 = (f32[384,128]{1,0:T(8,128)S(1)}, f32[384,128]{1,0:T(8,128)S(1)}, u32[]{:S(2)}, u32[]{:S(2)}) collective-permute-start(f32[384,128]{1,0:T(8,128)S(1)} %get-tuple-element.61.refs_5_.refs_3_), channel_id=1, source_target_pairs={{0,4},{2,6},{4,0},{6,2},{1,5},{3,7},{5,1},{7,3},{8,12},{10,14},{12... | collective-permute-start | bytes 589832 | tf_op jit(solution)/shard_map/ppermute | solution.py:79
  74.8 1.9 %collective-permute-start.35 = (f32[96,128]{1,0:T(8,128)S(1)}, f32[96,128]{1,0:T(8,128)S(1)}, u32[]{:S(2)}, u32[]{:S(2)}) collective-permute-start(f32[96,128]{1,0:T(8,128)S(1)} %restrict.1.refs_2_.refs_10_), channel_id=1, source_target_pairs={{0,2},{2,0},{4,6},{6,4},{1,3},{3,1},{5,7},{7,5},{8,10},{10,8},{12,... | collective-permute-start | bytes 147464 | tf_op jit(solution)/shard_map/ppermute | solution.py:79
  74.9 5.0 %collective-permute-start.34 = (f32[96,128]{1,0:T(8,128)S(1)}, f32[96,128]{1,0:T(8,128)S(1)}, u32[]{:S(2)}, u32[]{:S(2)}) collective-permute-start(f32[96,128]{1,0:T(8,128)S(1)} %restrict.1.refs_2_.refs_10_), channel_id=1, source_target_pairs={{0,24},{8,16},{16,8},{24,0},{1,25},{9,17},{17,9},{25,1},{2,26},{10... | collective-permute-start | bytes 147464 | tf_op jit(solution)/shard_map/ppermute | solution.py:79
  76.5 5.2 %collective-permute-start.33 = (f32[96,128]{1,0:T(8,128)S(1)}, f32[96,128]{1,0:T(8,128)S(1)}, u32[]{:S(2)}, u32[]{:S(2)}) collective-permute-start(f32[96,128]{1,0:T(8,128)S(1)} %restrict.1.refs_2_.refs_10_), channel_id=1, source_target_pairs={{0,16},{8,24},{16,0},{24,8},{1,17},{9,25},{17,1},{25,9},{2,18},{10... | collective-permute-start | bytes 147464 | tf_op jit(solution)/shard_map/ppermute | solution.py:79
  76.7 5.6 %collective-permute-start.32 = (f32[96,128]{1,0:T(8,128)S(1)}, f32[96,128]{1,0:T(8,128)S(1)}, u32[]{:S(2)}, u32[]{:S(2)}) collective-permute-start(f32[96,128]{1,0:T(8,128)S(1)} %restrict.1.refs_2_.refs_10_), channel_id=1, source_target_pairs={{0,8},{8,0},{16,24},{24,16},{1,9},{9,1},{17,25},{25,17},{2,10},{10... | collective-permute-start | bytes 147464 | tf_op jit(solution)/shard_map/ppermute | solution.py:79
  79.8 7.2 %collective-permute-start.39 = (f32[384,128]{1,0:T(8,128)S(1)}, f32[384,128]{1,0:T(8,128)S(1)}, u32[]{:S(2)}, u32[]{:S(2)}) collective-permute-start(f32[384,128]{1,0:T(8,128)S(1)} %get-tuple-element.59.refs_8_.refs_3_), channel_id=1, source_target_pairs={{0,2},{2,0},{4,6},{6,4},{1,3},{3,1},{5,7},{7,5},{8,10},{10,8},{12,... | collective-permute-start | bytes 589832 | tf_op jit(solution)/shard_map/ppermute | solution.py:79
  79.8 7.2 %collective-permute-start.41 = (f32[384,128]{1,0:T(8,128)S(1)}, f32[384,128]{1,0:T(8,128)S(1)}, u32[]{:S(2)}, u32[]{:S(2)}) collective-permute-start(f32[384,128]{1,0:T(8,128)S(1)} %collective-permute-done.40.refs_5_), channel_id=1, source_target_pairs={{0,2},{2,0},{4,6},{6,4},{1,3},{3,1},{5,7},{7,5},{8,10},{10,8},{12,... | collective-permute-start | bytes 589832 | tf_op jit(solution)/shard_map/ppermute | solution.py:79
  81.7 6.2 %collective-permute-start.42 = (f32[384,128]{1,0:T(8,128)S(1)}, f32[384,128]{1,0:T(8,128)S(1)}, u32[]{:S(2)}, u32[]{:S(2)}) collective-permute-start(f32[384,128]{1,0:T(8,128)S(1)} %get-tuple-element.61.refs_5_.refs_3_), channel_id=1, source_target_pairs={{0,2},{2,0},{4,6},{6,4},{1,3},{3,1},{5,7},{7,5},{8,10},{10,8},{12,... | collective-permute-start | bytes 589832 | tf_op jit(solution)/shard_map/ppermute | solution.py:79
  82.0 5.9 %collective-permute-start.44 = (f32[384,128]{1,0:T(8,128)S(1)}, f32[384,128]{1,0:T(8,128)S(1)}, u32[]{:S(2)}, u32[]{:S(2)}) collective-permute-start(f32[384,128]{1,0:T(8,128)S(1)} %collective-permute-done.43.refs_5_), channel_id=1, source_target_pairs={{0,2},{2,0},{4,6},{6,4},{1,3},{3,1},{5,7},{7,5},{8,10},{10,8},{12,... | collective-permute-start | bytes 589832 | tf_op jit(solution)/shard_map/ppermute | solution.py:79
  82.3 1.3 %collective-permute-start.38 = (f32[96,128]{1,0:T(8,128)S(1)}, f32[96,128]{1,0:T(8,128)S(1)}, u32[]{:S(2)}, u32[]{:S(2)}) collective-permute-start(f32[96,128]{1,0:T(8,128)S(1)} %collective-permute-done.34.refs_5_), channel_id=1, source_target_pairs={{0,2},{2,0},{4,6},{6,4},{1,3},{3,1},{5,7},{7,5},{8,10},{10,8},{12,... | collective-permute-start | bytes 147464 | tf_op jit(solution)/shard_map/ppermute | solution.py:79
  83.5 1.2 %collective-permute-start.37 = (f32[96,128]{1,0:T(8,128)S(1)}, f32[96,128]{1,0:T(8,128)S(1)}, u32[]{:S(2)}, u32[]{:S(2)}) collective-permute-start(f32[96,128]{1,0:T(8,128)S(1)} %collective-permute-done.33.refs_4_), channel_id=1, source_target_pairs={{0,2},{2,0},{4,6},{6,4},{1,3},{3,1},{5,7},{7,5},{8,10},{10,8},{12,... | collective-permute-start | bytes 147464 | tf_op jit(solution)/shard_map/ppermute | solution.py:79
  84.8 1.2 %collective-permute-start.36 = (f32[96,128]{1,0:T(8,128)S(1)}, f32[96,128]{1,0:T(8,128)S(1)}, u32[]{:S(2)}, u32[]{:S(2)}) collective-permute-start(f32[96,128]{1,0:T(8,128)S(1)} %collective-permute-done.32.refs_3_), channel_id=1, source_target_pairs={{0,2},{2,0},{4,6},{6,4},{1,3},{3,1},{5,7},{7,5},{8,10},{10,8},{12,... | collective-permute-start | bytes 147464 | tf_op jit(solution)/shard_map/ppermute | solution.py:79
  91.8 10.5 %collective-permute-start.45 = (f32[6,128,128]{2,1,0:T(8,128)S(1)}, f32[6,128,128]{2,1,0:T(8,128)S(1)}, u32[]{:S(2)}, u32[]{:S(2)}) collective-permute-start(f32[6,128,128]{2,1,0:T(8,128)S(1)} %get-tuple-element.71), channel_id=1, source_target_pairs={{0,8},{8,0},{16,24},{24,16},{1,9},{9,1},{17,25},{25,17},{2,10},{10... | collective-permute-start | bytes 1179656 | tf_op jit(solution)/shard_map/ppermute | solution.py:705
  92.5 13.2 %collective-permute-start.46 = (f32[6,128,128]{2,1,0:T(8,128)S(1)}, f32[6,128,128]{2,1,0:T(8,128)S(1)}, u32[]{:S(2)}, u32[]{:S(2)}) collective-permute-start(f32[6,128,128]{2,1,0:T(8,128)S(1)} %get-tuple-element.72), channel_id=1, source_target_pairs={{8,16},{16,8},{9,17},{17,9},{10,18},{18,10},{11,19},{19,11},{12,20... | collective-permute-start | bytes 1179656 | tf_op jit(solution)/shard_map/ppermute | solution.py:705
  107.1 1.8 %collective-permute-start.47 = (f32[6,128,128]{2,1,0:T(8,128)S(1)}, f32[6,128,128]{2,1,0:T(8,128)S(1)}, u32[]{:S(2)}, u32[]{:S(2)}) collective-permute-start(f32[6,128,128]{2,1,0:T(8,128)S(1)} %couple.3.refs_2_), channel_id=1, source_target_pairs={{0,2},{2,0},{4,6},{6,4},{1,3},{3,1},{5,7},{7,5},{8,10},{10,8},{12,... | collective-permute-start | bytes 1179656 | tf_op jit(solution)/shard_map/ppermute | solution.py:79
  (7 other events, 30.7 us)

commit v3 on v2

--- a/solution.py
+++ b/solution.py
@@ -79,7 +79,7 @@
     return lax.ppermute(x, axis, [(i, i ^ bit) for i in range(size) if (i ^ bit) < size])
 
 
-def split_matrix(matrix, name, after=()):
+def split_matrix(matrix, name, micros, after=()):
     subs, rows, order = matrix.shape
     tile = 96 if rows % 96 == 0 else rows
     tiles = rows // tile
@@ -108,7 +108,7 @@
         name,
         [matrix],
         [((subs, 2 * rows, order), bf16)],
-        2.0,
+        micros,
         far=1,
         scratch=[
             pltpu.VMEM((subs * tiles, tile, order), f32),
@@ -119,43 +119,34 @@
 
 
 def place_coarse(pieces, subs, modes, own_rows, after=()):
-    height, rows = pieces[0][0].shape
-    count = max(q for _, q, _ in pieces) + 1
+    height, rows = pieces[0].shape
+    count = len(pieces)
     order = rows * count
     spans = (height - subs * modes) // own_rows
 
     def kernel(*refs):
-        down, up, inverse, held = refs[len(pieces) :]
-        crow, ccol = lax.axis_index("crow"), lax.axis_index("ccol")
-        for ref, (_, q, half) in zip(refs, pieces):
-            if half is None:
-                held[q] = ref[...]
-            else:
-                size = ref.shape[0]
-                which = ccol if half == 0 else 1 - ccol
-                held[q, pl.ds(pl.multiple_of(which * size, 8), size)] = ref[...]
-        for q in range(count):
+        down, up, inverse = refs[count:]
+        crow = lax.axis_index("crow")
+        for q, ref in enumerate(refs[:count]):
             here = slice(q * rows, (q + 1) * rows)
             for s in range(subs):
-                value = held[q, s * modes : (s + 1) * modes]
+                value = ref[s * modes : (s + 1) * modes]
                 down[s, :, here] = stacked(value)
                 up[s, here] = beside(value.T)
             for i in range(spans):
                 first = subs * modes + i * own_rows
-                inverse[crow ^ q, :, i * rows : (i + 1) * rows] = held[q, first : first + own_rows]
+                inverse[crow ^ q, :, i * rows : (i + 1) * rows] = ref[first : first + own_rows]
 
     return call(
         kernel,
         "place_coarse",
-        [p[0] for p in pieces],
+        pieces,
         [
             ((subs, 2 * modes, order), bf16),
             ((subs, order, 2 * modes), bf16),
             ((count, own_rows, spans * rows), f32),
         ],
         1.2,
-        scratch=[pltpu.VMEM((count, height, rows), f32)],
-        limit=16,
         after=after,
     )
 
@@ -212,16 +203,19 @@
     own_rows, columns = inverse.shape
     height = subs * modes + own_rows * (columns // rows)
 
-    def kernel(n, c, rd, z_far, r_far, c_far, keep, give, r, packed, both, part, sems):
+    def kernel(n_far, l_far, rd_far, z_far, r_far, c_far, keep, give, r, packed, both, n, c, rd, sems):
         at = position()
         pairs = [(z_far.at[s], both.at[s * modes : (s + 1) * modes]) for s in range(subs)]
         pairs.append((r_far, r))
         for i in range(columns // rows):
             first = subs * modes + i * own_rows
             pairs.append((c_far.at[:, i * rows : (i + 1) * rows], both.at[first : first + own_rows]))
-        moves = [pltpu.make_async_copy(a, b, sems.at[i]) for i, (a, b) in enumerate(pairs)]
+        small = [(n_far, n), (l_far, c), (rd_far, rd)]
+        moves = [pltpu.make_async_copy(a, b, sems.at[i]) for i, (a, b) in enumerate(small + pairs)]
         for move in moves:
             move.start()
+        for move in moves[:3]:
+            move.wait()
         lane = lax.broadcasted_iota(jnp.int32, (1, width), 1)
         ids = jnp.zeros((1, width), jnp.int32)
         limits = jnp.zeros((1, width), jnp.int32)
@@ -234,10 +228,8 @@
                 limits = jnp.where(lane == block, jnp.where(k < c[s], 1, 0), limits)
         packed[used : used + 1] = ids.astype(f32)
         packed[used + 1 : used + 2] = limits.astype(f32)
-        for move in moves:
+        for move in moves[3:]:
             move.wait()
-        start = pl.multiple_of(lax.axis_index("ccol") * (height // 2), 8)
-        part[...] = both[pl.ds(start, height // 2)]
         for i in range(half):
             for out, first in ((keep, at[1] * half), (give, (1 - at[1]) * half)):
                 s = first + i
@@ -254,12 +246,15 @@
             (residual.shape, f32),
             ((listed, width), f32),
             ((height, rows), f32),
-            ((height // 2, rows), f32),
         ],
         2.0,
-        scalars=2,
-        far=3,
-        scratch=[pltpu.SemaphoreType.DMA((subs + 1 + columns // rows,))],
+        far=6,
+        scratch=[
+            pltpu.SMEM(neighbour.shape, jnp.int32),
+            pltpu.SMEM(counts.shape, jnp.int32),
+            pltpu.VMEM(reads.shape, jnp.int32),
+            pltpu.SemaphoreType.DMA((subs + 4 + columns // rows,)),
+        ],
     )
 
 
@@ -287,39 +282,39 @@
 
     def kernel(*refs):
         at = position()
-        lists, info, rows_v, sem = refs[ways:]
+        columns, info = refs[ways:]
+        info[...] = jnp.full(info.shape, -1, jnp.int32)
         for d in range(ways):
             table = refs[d][starts[d] : starts[d] + listed].astype(jnp.int32)
             picked = jnp.where(at[1] == 0, table[:half], table[half:used])
-            lists[d] = in_xor_order(picked, rows, blocks, at[2])
+            aims = in_xor_order(picked, rows, blocks, at[2])
+            spans = lax.div(aims, width)
+            within = (aims - spans * width).astype(f32)
+            spans = spans.astype(f32)
+            for k in range(half):
+                for i, line in enumerate((within, spans)):
+                    tall = jnp.broadcast_to(line[k : k + 1], (width, width)).T
+                    columns[d, k, i] = tall.astype(bf16)
             ids, limits = table[used : used + 1], table[used + 1 : used + 2]
             place = ids - at[0] * subs
             use = (limits > 0) & (place >= 0) & (place < subs)
-            rows_v[d : d + 1] = jnp.where(use, place, -1)
+            info[d : d + 1] = jnp.where(use, place, -1)
         table = refs[0][starts[0] : starts[0] + listed].astype(jnp.int32)
         ids, limits = table[used : used + 1], table[used + 1 : used + 2]
         twin = at[0] ^ 1
         inside = (ids >= at[0] * subs) & (ids < (at[0] + 1) * subs)
         paired = (ids >= twin * subs) & (ids < (twin + 1) * subs)
         theirs = jnp.where(inside, 0, jnp.where(paired, 1, 2))
-        rows_v[ways : ways + 1] = jnp.where(limits > 0, theirs, -1)
-        move = pltpu.make_async_copy(rows_v, info, sem)
-        move.start()
-        move.wait()
-
-    return pl.pallas_call(
-        lambda *refs: kernel(*refs[:ways], *refs[ways + len(after) :]),
-        in_specs=[IN_VMEM] * ways + [pl.BlockSpec(memory_space=pl.ANY)] * len(after),
-        out_specs=[IN_VMEM, IN_SMEM],
-        out_shape=[
-            jax.ShapeDtypeStruct((ways, half, width), jnp.int32),
-            jax.ShapeDtypeStruct((8, width), jnp.int32),
-        ],
-        scratch_shapes=[pltpu.VMEM((8, width), jnp.int32), pltpu.SemaphoreType.DMA(())],
-        compiler_params=pltpu.CompilerParams(vmem_limit_bytes=8 * MIB),
-        cost_estimate=pl.CostEstimate(flops=0, bytes_accessed=int(COST), transcendentals=0),
-        name="prepare",
-    )(*held, *after)
+        info[ways : ways + 1] = jnp.where(limits > 0, theirs, -1)
+
+    return call(
+        kernel,
+        "prepare",
+        list(held),
+        [((ways, half, 2, width, width), bf16), ((8, width), jnp.int32)],
+        0.5,
+        after=after,
+    )
 
 
 def add_up(a, b, below=None, after=()):
@@ -334,6 +329,17 @@
 
     operands = [a, b] + ([] if below is None else [below])
     return call(kernel, "add_up", operands, [((rows + more, a.shape[1]), f32)], 0.2, after=after)[0]
+
+
+def pile(arrays, rows, after=()):
+    count = len(arrays)
+
+    def kernel(*refs):
+        for i, ref in enumerate(refs[:count]):
+            refs[count][i] = ref[:rows]
+
+    columns = arrays[0].shape[1]
+    return call(kernel, "pile", arrays, [((count, rows, columns), f32)], 0.2, after=after)[0]
 
 
 def load(ref, s):
@@ -388,7 +394,7 @@
         at = position()
         o, rhs, terms = refs[count:]
         for q, ref in enumerate(refs[:count]):
-            rhs[q * rows : (q + 1) * rows] = beside(ref[...])
+            rhs[q * rows : (q + 1) * rows] = beside(load(ref, s))
         choose_terms(at[1] == s // (subs // 2), g_mine, g_other, terms)
         o[...] = folded(dot(m[s], rhs[...])) + damping * folded(dot(f[s], terms[...]))
 
@@ -437,20 +443,18 @@
 def lift_coarse(inverse, lift, mine, other, after=()):
     subs, order, twice = lift.shape
     modes = twice // 2
-    half, cases = subs // 2, mine[0].shape[1]
+    groups, _, cases = mine.shape
+    half = subs // 2
     per_sub = inverse.shape[0] // subs
     columns = inverse.shape[2]
-    groups = len(mine)
-
-    def kernel(c, z, *refs):
+
+    def kernel(c, z, g_mine, g_other, o, right):
         at = position()
-        o, right = refs[2 * groups :]
         for b in range(groups):
             base = (at[0] ^ b) * (2 * half * modes)
-            for h, ref in ((at[1], refs[b]), (1 - at[1], refs[groups + b])):
-                for i in range(half):
-                    row = pl.multiple_of(base + h * (half * modes) + i * modes, 16)
-                    right[pl.ds(row, modes)] = beside(ref[i * modes : (i + 1) * modes])
+            for h, ref in ((at[1], g_mine), (1 - at[1], g_other)):
+                row = pl.multiple_of(base + h * (half * modes), 16)
+                right[pl.ds(row, half * modes)] = beside(ref[b])
         for s in range(subs):
             c_rows = c[s * per_sub : (s + 1) * per_sub].reshape(modes, columns)
             coarse = beside(folded(dot(stacked(c_rows), right[...])))
@@ -459,7 +463,7 @@
     return call(
         kernel,
         "lift_coarse",
-        [inverse, lift, *mine, *other],
+        [inverse, lift, mine, other],
         [((subs, order, cases), f32)],
         1.2,
         scratch=[pltpu.VMEM((columns, 2 * cases), bf16)],
@@ -468,71 +472,81 @@
     )[0]
 
 
-def correct(s, split, lifted, blocks, residual, old, after=()):
-    rows = split.shape[1] // 2
-    order = split.shape[2]
-    cases = blocks[0].shape[-1]
-    count = len(blocks)
-
-    def kernel(m, up, res, *refs):
-        old_refs = refs[count : len(refs) - 3]
-        o, total, corr = refs[len(refs) - 3 :]
-        for q, ref in enumerate(refs[:count]):
-            here = slice(q * rows, (q + 1) * rows)
-            value = ref[...] + up[s, here]
-            corr[here] = beside(value)
-            if q == 0:
-                total[...] = damping * value + old_refs[0][...] if old_refs else damping * value
-        o[...] = load(res, s) - damping * folded(dot(m[s], corr[...]))
-
-    return call(
-        kernel,
-        "correct",
-        [split, lifted, residual, *blocks] + ([] if old is None else [old]),
-        [((rows, cases), f32), ((rows, cases), f32), ((order, 2 * cases), bf16)],
-        1.0,
-        after=after,
-    )
-
-
-def select_rows(info, lists, corrs, after=()):
-    ways, slots, width = lists.shape
-    order, twice = corrs[0].shape
-    cases = twice // 2
-
-    def kernel(where, l, *refs):
-        at = position()
-        corr_refs = refs[: len(corrs)]
-        outs = refs[len(corrs) :]
-        lane = lax.broadcasted_iota(jnp.int32, (width, order), 1)
+def correct(lifted, blocks, old, info, lists, after=()):
+    subs = len(blocks)
+    count = len(blocks[0])
+    rows, cases = blocks[0][0].shape
+    order = rows * count
+    ways, slots, _, width, _ = lists.shape
+    has_old = old is not None
+
+    def kernel(up, facts, l, *refs):
+        block_refs = refs[: subs * count]
+        refs = refs[subs * count :]
+        old_ref, refs = (refs[0], refs[1:]) if has_old else (None, refs)
+        total, corrs, outs = refs[0], refs[1 : 1 + subs], refs[1 + subs : 1 + subs + ways]
+        where, sem = refs[1 + subs + ways :]
+        move = pltpu.make_async_copy(facts, where, sem)
+        move.start()
+        core = position()[1]
+        for s in range(subs):
+            for q in range(count):
+                here = slice(q * rows, (q + 1) * rows)
+                value = block_refs[s * count + q][...] + up[s, here]
+                corrs[s][here] = beside(value)
+                if q == 0:
+                    total[s] = damping * value + old_ref[s] if has_old else damping * value
+        move.wait()
+        lane = lax.broadcasted_iota(jnp.int32, (width, width), 1).astype(f32).astype(bf16)
+        none = jnp.zeros((width, width), bf16)
         for d in range(ways):
 
             @pl.loop(0, slots)
             def _(k):
-                place = where[d, at[1] * slots + k]
+                place = where[d, core * slots + k]
 
                 @pl.when(place < 0)
                 def _():
                     outs[d][k] = jnp.zeros((width, cases), f32)
 
-                for s, ref in enumerate(corr_refs):
+                for s in range(subs):
 
                     @pl.when(place == s)
                     def _():
-                        rows = jnp.broadcast_to(l[d, pl.ds(k, 1), :], (width, width)).T
-                        rows = jnp.concatenate([rows] * (order // width), axis=1)
-                        one = (rows == lane).astype(f32).astype(bf16)
-                        outs[d][k] = sides(dot(one, ref[...]))
-
-    return call(
-        kernel,
-        "select_rows",
-        [info, lists, *corrs],
-        [((slots, width, cases), f32)] * ways,
-        1.5,
-        scalars=1,
-        after=after,
-    )
+                        one = jnp.where(l[d, k, 0] == lane, jnp.ones_like(none), none)
+                        span = l[d, k, 1]
+                        ones = [jnp.where(span == t, one, none) for t in range(order // width)]
+                        outs[d][k] = sides(dot(jnp.concatenate(ones, axis=1), corrs[s][...]))
+
+    flat = [b for of_sub in blocks for b in of_sub]
+    return call(
+        kernel,
+        "correct",
+        [lifted, info, lists, *flat] + ([old] if has_old else []),
+        [((subs, rows, cases), f32)]
+        + [((order, 2 * cases), bf16)] * subs
+        + [((slots, width, cases), f32)] * ways,
+        3.0,
+        scratch=[pltpu.SMEM(info.shape, jnp.int32), pltpu.SemaphoreType.DMA(())],
+        after=after,
+    )
+
+
+def reduce_residual(split, corrs, residual, after=()):
+    subs, rows, cases = residual.shape
+
+    def kernel(m, res, *refs):
+        for s in range(subs):
+            refs[subs][s] = res[s] - damping * folded(dot(m[s], refs[s][...]))
+
+    return call(
+        kernel,
+        "reduce_residual",
+        [split, residual, *corrs],
+        [(residual.shape, f32)],
+        1.2,
+        after=after,
+    )[0]
 
 
 def couple(info, coupling, sources, after=()):
@@ -540,24 +554,30 @@
     slots, _, cases = sources[0].shape
     ways = len(sources)
 
-    def kernel(where, c, *refs):
-        at = position()
-        out = refs[ways]
-
-        @pl.loop(0, slots)
-        def _(k):
-            block = at[1] * slots + k
-            code = where[ways, block]
+    def kernel(facts, c, *refs):
+        out, left, right, where, sem = refs[ways:]
+        move = pltpu.make_async_copy(facts, where, sem)
+        move.start()
+        first = position()[1] * slots
+        for k in range(slots):
+            block = first + k
+            left[k] = stacked(c[block // per_sub, lax.rem(block, per_sub)])
+        move.wait()
+        for k in range(slots):
+            code = where[ways, first + k]
 
             @pl.when(code < 0)
             def _():
-                out[k] = jnp.zeros((width, cases), f32)
+                right[k] = jnp.zeros((width, 2 * cases), bf16)
 
             for d, ref in enumerate(refs[:ways]):
 
                 @pl.when(code == d)
                 def _():
-                    out[k] = folded(dot(stacked(c[block // per_sub, block % per_sub]), beside(ref[k])))
+                    right[k] = beside(ref[k])
+
+        for k in range(slots):
+            out[k] = folded(dot(left[k], right[k]))
 
     return call(
         kernel,
@@ -565,44 +585,51 @@
         [info, coupling, *sources],
         [((slots, width, cases), f32)],
         0.8,
-        scalars=1,
+        scratch=[
+            pltpu.VMEM((slots, 2 * width, width), bf16),
+            pltpu.VMEM((slots, width, 2 * cases), bf16),
+            pltpu.SMEM(info.shape, jnp.int32),
+            pltpu.SemaphoreType.DMA(()),
+        ],
         after=after,
     )[0]
 
 
-def add_inflow(residuals, hits, mine, other):
-    subs = hits.shape[0]
-    slots, width, cases = mine[0].shape
-    rows = residuals[0].shape[0]
-    sweeps = len(mine)
-
-    def kernel(tg, *refs):
-        at = position()
-        groups = (refs[:sweeps], refs[sweeps : 2 * sweeps])
-        res = refs[2 * sweeps : 2 * sweeps + subs]
-        out, terms = refs[2 * sweeps + subs :]
-        for s in range(subs):
-            here = at[1] == s // (subs // 2)
-            for flag, terms_of in ((here, groups[0]), (jnp.logical_not(here), groups[1])):
-
-                @pl.when(flag)
-                def _():
-                    for k in range(slots):
-                        value = terms_of[0][k]
-                        for more in terms_of[1:]:
-                            value = value + more[k]
-                        terms[k * width : (k + 1) * width] = beside(value)
-
-            out[s] = res[s][...] + damping * sides(dot(tg[s], terms[...]))
-
-    return call(
-        kernel,
-        "add_inflow",
-        [hits, *mine, *other, *residuals],
-        [((subs, rows, cases), f32)],
+def add_own_half(residual, hits, terms, old=None, after=()):
+    subs, rows, cases = residual.shape
+    slots, width, _ = terms.shape
+    half = subs // 2
+    per_sub = slots // half
+
+    def kernel(res, tg, g, *refs):
+        out, rhs = refs[-2:]
+        core = position()[1]
+        side = core if old is None else 1 - core
+        for i in range(half):
+            for k in range(per_sub):
+                rhs[k * width : (k + 1) * width] = beside(g[i * per_sub + k])
+            s = side * half + i
+            value = res[s] + damping * sides(dot(tg[s], rhs[...]))
+            if old is None:
+                out[i] = value
+            else:
+                out[s] = value
+                out[core * half + i] = refs[0][i]
+
+    return call(
+        kernel,
+        "add_own_half",
+        [residual, hits, terms] + ([] if old is None else [old]),
+        [((half if old is None else subs, rows, cases), f32)],
         0.8,
-        scratch=[pltpu.VMEM((slots * width, 2 * cases), bf16)],
+        scratch=[pltpu.VMEM((per_sub * width, 2 * cases), bf16)],
+        after=after,
     )[0]
+
+
+def add_inflow(residual, hits, terms, others, after=()):
+    own = add_own_half(residual, hits, terms, None, after)
+    return add_own_half(residual, hits, others, own)
 
 
 def gathered(x, hold=()):
@@ -617,22 +644,8 @@
     return [blocks[q] for q in sorted(blocks)]
 
 
-def coarse_pieces(x, part, hold):
-    bit = lax.axis_size("crow") // 2
-    if lax.axis_size("ccol") == 2:
-        part = relay(exchange(part, "crow", bit), hold)
-        pieces = [(x, 0, None), (part, bit, 0), (exchange(part, "ccol", 1), bit, 1)]
-    else:
-        pieces = [(x, 0, None), (exchange(x, "crow", bit), bit, None)]
-    while bit > 1:
-        bit //= 2
-        pieces = pieces + [(exchange(p, "crow", bit), q | bit, half) for p, q, half in pieces]
-    return pieces
-
-
 def spread_over_sub(half):
-    halves = [half] + [exchange(half, "sub", b) for b in range(1, lax.axis_size("sub"))]
-    return halves, [exchange(h, "crow", 1) for h in halves]
+    return [half] + [exchange(half, "sub", b) for b in range(1, lax.axis_size("sub"))]
 
 
 def pair_routes(size):
@@ -660,73 +673,72 @@
     targets = target_local_rows.transpose(1, 0, 2)
     routes = pair_routes(groups)
 
-    keep, give, residual, packed, both, part = begin(
+    keep, give, residual, packed, both = begin(
         neighbour, counts, neighbour_read_rows.transpose(1, 0, 2), coarse_basis, load_cases,
         coarse_inverse,
     )
-    keep = add_up(keep, exchange(give, "crow", 1), None, [keep])
-    inverse_split = split_matrix(local_inverse, "split_inverse", [keep])
-    first_blocks = gathered(load_cases, [inverse_split])
+    keep = add_up(keep, exchange(give, "crow", 1))
+    inverse_split = split_matrix(local_inverse, "split_inverse", 2.0, [keep])
     bits = [bit for bit in (2, 4, 8) if bit < crow_size]
     for bit in bits[:-1]:
         keep = add_up(keep, exchange(keep, "crow", bit), None, [inverse_split])
     more = relay(exchange(keep, "crow", bits[-1]), [inverse_split])
+    first_blocks = gathered(load_cases, [more])
+    both = relay(both, [more])
     local = []
     for s in range(subs):
-        local.append(local_solve(s, inverse_split, first_blocks, [more] if s == 0 else [local[-1]]))
-    keep = add_up(keep, more, packed, [local[-1]])
-    mine, other = spread_over_sub(keep)
+        local.append(local_solve(s, inverse_split, first_blocks, local[-1:]))
+    stiffness_split = split_matrix(stiffness, "split_stiffness", 9000.0, [local[-1]])
+    local_blocks = [gathered(v, [stiffness_split]) for v in local]
+    arrived = [b[crow_size // 2] for b in local_blocks]
+
+    halves = spread_over_sub(add_up(keep, more, packed, [stiffness_split]))
+    height = give.shape[0]
+    mine = pile(halves, height, arrived)
+    other = exchange(mine, "crow", 1)
+    pieces = gathered(both, [mine])
+    down, lift, inverse = place_coarse(
+        pieces, subs, coarse_basis.shape[1], coarse_inverse.shape[0], [mine]
+    )
 
     if groups == 4:
-        held = [packed, mine[1], mine[3]]
+        held = [packed, halves[1], halves[3]]
     else:
         held = [packed] + [lax.ppermute(packed, "sub", route) for route in routes]
-
-    down, lift, inverse = place_coarse(
-        coarse_pieces(both, part, [keep]), subs, coarse_basis.shape[1], coarse_inverse.shape[0],
-        [keep],
-    )
     lists, info = prepare(held, subs, slots, rows, crow_size, [down])
-    stiffness_split = split_matrix(stiffness, "split_stiffness", [info])
-
-    totals, residuals, last = [None] * subs, [residual] * subs, stiffness_split
-    all_terms, all_others = [], []
+
+    total, last = None, info
     for sweep_index in range(ITERS):
-        local_blocks = [gathered(v) for v in local]
+        if sweep_index:
+            local_blocks = [gathered(v) for v in local]
         lifted = lift_coarse(inverse, lift, mine, other, [last])
-        steps, last = [], lifted
-        for s in range(subs):
-            steps.append(
-                correct(s, stiffness_split, lifted, local_blocks[s], residuals[s], totals[s], [last])
-            )
-            last = steps[-1][0]
-        residuals, totals, corrs = zip(*steps)
-        chosen = select_rows(info, lists, corrs)
+        total, *rest = correct(lifted, local_blocks, total, info, lists)
+        corrs, chosen = rest[:subs], rest[subs:]
         sources = [chosen[0]] + [lax.ppermute(c, "sub", route) for c, route in zip(chosen[1:], routes)]
+        residual = reduce_residual(stiffness_split, corrs, residual)
         if sweep_index == 0:
             own_hits, folds, z_folds = fold_targets(
-                counts, targets, inverse_split, down, [chosen[0]]
+                counts, targets, inverse_split, down, [residual]
             )
-            wholes = [gathered(r, [folds]) for r in residuals]
-            ready = [w[crow_size // 2] for w in wholes]
-        terms = couple(info, coupling, sources, ready if sweep_index == 0 else [])
+            whole = gathered(residual, [folds])
+            ready = [folds]
+        else:
+            residual = add_inflow(residual, own_hits, *held_terms, [residual])
+            ready = [residual]
+        terms = couple(info, coupling, sources, ready)
         other_terms = exchange(terms, "crow", 1)
-        all_terms.append(terms)
-        all_others.append(other_terms)
+        held_terms = (terms, other_terms)
         if sweep_index == ITERS - 1:
-            return jnp.stack(totals), add_inflow(residuals, own_hits, all_terms, all_others)
+            return total, add_inflow(residual, own_hits, terms, other_terms)
         steps, last = [], terms
         for s in range(subs):
-            steps.append(
-                local_solve_inflow(
-                    s, inverse_split, folds, wholes[s], terms, other_terms, [last]
-                )
-            )
+            steps.append(local_solve_inflow(s, inverse_split, folds, whole, terms, other_terms, [last]))
             last = steps[-1][0]
         local, residual_parts = zip(*steps)
         half = restrict(down, z_folds, residual_parts, terms, [last])
-        last = half
-        mine, other = spread_over_sub(half)
+        mine = pile(spread_over_sub(half), height)
+        other = exchange(mine, "crow", 1)
+        last = mine
 
 
 def solution(mesh):

time: 111 us -> 96.6 us (0.87)
  starting transfers between devices: 33.2 us -> 26.7 us
  Pallas kernels: 36.8 us -> 33.9 us
  waiting for transfers between devices: 36.8 us -> 34.7 us
  local copies, waits for them, and re-layouts: 2.05 us -> 0.02 us
    ppermute x44 -> x33, starting transfers between devices: 26.6 us -> 21.5 us  [exchange(): lax.ppermute(x, axis, [(i, i ^ bit) for i in range(size) if i ^ bit < size])]
    ppermute x44 -> x33, waiting for transfers between devices: 26.8 us -> 22.6 us  [exchange(): lax.ppermute(x, axis, [(i, i ^ bit) for i in range(size) if i ^ bit < size])]
    ppermute x4, waiting for transfers between devices: 10 us -> 12.1 us  [per_device(): lax.ppermute(c, 'sub', route)]
    unnamed x14 -> x8, local copies, waits for them, and re-layouts: 2.05 us -> 0.02 us
    pallas_call x28 -> x34, Pallas kernels: 35.5 us -> 33.9 us  [call(): pl.pallas_call(body, in_specs=[IN_SMEM] * scalars + [IN_VMEM] * (used - s...]
    ppermute x4, starting transfers between devices: 6.62 us -> 5.23 us  [per_device(): lax.ppermute(c, 'sub', route)]
    pallas_call x1 -> x0, Pallas kernels: 1.28 us -> none  [prepare(): pl.pallas_call(lambda *refs: kernel(*refs[:ways], *refs[ways + len(after)...]
  transfers between devices with their start and end apart: 48 -> 37, of which waited for: 20 -> 19; matrix products, arithmetic and copies ran while one was open for 1% -> 0% of each run, Pallas kernels for 22% -> 23%
where the time goes in v3:
time: 96.6 us; the launch traced here: 96.5 us
  waiting for transfers between devices  34.7 us (36%)
  Pallas kernels  33.9 us (35%)
  starting transfers between devices  26.7 us (28%)
  between operations  1.07 us (1%)
    pallas_call x34, Pallas kernels, call(): pl.pallas_call(body, in_specs=[IN_SMEM] * scalars + [IN_VMEM] * (used - s...  33.9 us
    ppermute x33, waiting for transfers between devices, exchange(): lax.ppermute(x, axis, [(i, i ^ bit) for i in range(size) if i ^ bit < size])  22.6 us
    ppermute x33, starting transfers between devices, exchange(): lax.ppermute(x, axis, [(i, i ^ bit) for i in range(size) if i ^ bit < size])  21.5 us
    ppermute x4, waiting for transfers between devices, per_device(): lax.ppermute(c, 'sub', route)  12.1 us
    ppermute x4, starting transfers between devices, per_device(): lax.ppermute(c, 'sub', route)  5.23 us
  transfers between devices with their start and end apart: 37, of which 19 were waited for; matrix products, arithmetic and copies ran while one was open for 0% of the time, Pallas kernels for 23%

profile of v3, /device:TPU:16, one launch (start us, length us, event | category | flops | bytes accessed | tf_op | source)
XLA Modules:
  0.0 96.5 jit_solution(5198794735773668485)
XLA Ops:
  0.6 1.6 %collective-permute-start.5 = (f32[2,384,128]{2,1,0:T(8,128)}, f32[2,384,128]{2,1,0:T(8,128)S(1)}, u32[]{:S(2)}, u32[]{:S(2)}) collective-permute-start(f32[2,384,128]{2,1,0:T(8,128)} %refs_1_.7), channel_id=1, source_target_pairs={{0,4},{2,6},{4,0},{6,2},{1,5},{3,7},{5,1},{7,3},{8,12},{10,14},{12... | collective-permute-start | bytes 1179656 | tf_op jit(solution)/shard_map/ppermute | solution.py:79
  2.2 1.5 %begin.1 = (f32[96,128]{1,0:T(8,128)S(1)}, f32[96,128]{1,0:T(8,128)S(1)}, f32[2,384,128]{2,1,0:T(8,128)S(1)}, f32[16,128]{1,0:T(8,128)S(1)}, f32[288,384]{1,0:T(8,128)S(1)}) custom-call(s32[2,6]{1,0:T(2,128)} %refs_0_.4, s32[2]{0:T(128)} %refs_0_.7, s32[6,2,128]{2,1,0:T(2,128)} %bitcast.3, f32[2,96,384]{2,1,0:T(8,128)} %refs_3_.1, f32[2,384,128]{2,1,0:T(8,128)} %refs_1_.7, ...), custom_call_target="tpu_custom_call" | custom-call | bytes 2000 | tf_op jit(solution)/shard_map/begin/pallas_call | solution.py:28
  3.8 1.2 %collective-permute-done.refs_1_ = f32[96,128]{1,0:T(8,128)S(1)} collective-permute-done((f32[96,128]{1,0:T(8,128)S(1)}, f32[96,128]{1,0:T(8,128)S(1)}, u32[]{:S(2)}, u32[]{:S(2)}) %collective-permute-start) | collective-permute-done | bytes 49184 | tf_op jit(solution)/shard_map/ppermute | solution.py:79
  5.0 0.6 collective-permute-start.1
  5.6 2.5 %split_inverse.1.refs_1_.refs_0_.refs_2_ = bf16[2,768,1536]{2,1,0:T(8,128)(2,1)S(1)} custom-call(f32[2,384,1536]{2,1,0:T(8,128)} %refs_0_.5, f32[96,128]{1,0:T(8,128)S(1)} %add_up.2.refs_1_.refs_0_), custom_call_target="tpu_custom_call" | custom-call | bytes 2000 | tf_op jit(solution)/shard_map/split_inverse/pallas_call | solution.py:28
  8.1 4.7 %collective-permute-done.1.refs_0_ = f32[96,128]{1,0:T(8,128)S(1)} collective-permute-done((f32[96,128]{1,0:T(8,128)S(1)}, f32[96,128]{1,0:T(8,128)S(1)}, u32[]{:S(2)}, u32[]{:S(2)}) %collective-permute-start.1) | collective-permute-done | bytes 49184 | tf_op jit(solution)/shard_map/ppermute | solution.py:79
  13.0 1.6 %collective-permute-start.3 = (f32[288,384]{1,0:T(8,128)S(1)}, f32[288,384]{1,0:T(8,128)S(1)}, u32[]{:S(2)}, u32[]{:S(2)}) collective-permute-start(f32[288,384]{1,0:T(8,128)S(1)} %relay.8.refs_0_), channel_id=1, source_target_pairs={{0,4},{2,6},{4,0},{6,2},{1,5},{3,7},{5,1},{7,3},{8,12},{10,14},{12... | collective-permute-start | bytes 1327112 | tf_op jit(solution)/shard_map/ppermute | solution.py:79
  14.7 0.8 local_solve.2.refs_5_.refs_3_
  15.4 0.8 local_solve.3.refs_1_.refs_7_
  16.2 1.6 %collective-permute-start.11 = (f32[384,128]{1,0:T(8,128)S(1)}, f32[384,128]{1,0:T(8,128)S(1)}, u32[]{:S(2)}, u32[]{:S(2)}) collective-permute-start(f32[384,128]{1,0:T(8,128)S(1)} %local_solve.3.refs_1_.refs_7_), channel_id=1, source_target_pairs={{0,4},{2,6},{4,0},{6,2},{1,5},{3,7},{5,1},{7,3},{8,12},{10,14},{12... | collective-permute-start | bytes 589832 | tf_op jit(solution)/shard_map/ppermute | solution.py:79
  18.3 2.5 %split_stiffness.1.refs_3_.refs_1_.refs_0_ = bf16[2,768,1536]{2,1,0:T(8,128)(2,1)S(1)} custom-call(f32[2,384,1536]{2,1,0:T(8,128)} %refs_0_.6, f32[384,128]{1,0:T(8,128)S(1)} %local_solve.3.refs_1_.refs_7_), custom_call_target="tpu_custom_call" | custom-call | bytes 9000000 | tf_op jit(solution)/shard_map/split_stiffness/pallas_call | solution.py:28
  20.8 0.5 collective-permute-start.9
  21.3 3.5 %collective-permute-start.8 = (f32[112,128]{1,0:T(8,128)S(1)}, f32[112,128]{1,0:T(8,128)S(1)}, u32[]{:S(2)}, u32[]{:S(2)}) collective-permute-start(f32[112,128]{1,0:T(8,128)S(1)} %add_up.3.refs_0_), channel_id=1, source_target_pairs={{0,16},{8,24},{16,0},{24,8},{1,17},{9,25},{17,1},{25,9},{2,18},{10... | collective-permute-start | bytes 172040 | tf_op jit(solution)/shard_map/ppermute | solution.py:79
  24.8 5.4 %collective-permute-done.11.refs_0_ = f32[384,128]{1,0:T(8,128)S(1)} collective-permute-done((f32[384,128]{1,0:T(8,128)S(1)}, f32[384,128]{1,0:T(8,128)S(1)}, u32[]{:S(2)}, u32[]{:S(2)}) %collective-permute-start.11) | collective-permute-done | bytes 196640 | tf_op jit(solution)/shard_map/ppermute | solution.py:79
  30.2 1.6 %collective-permute-start.7 = (f32[112,128]{1,0:T(8,128)S(1)}, f32[112,128]{1,0:T(8,128)S(1)}, u32[]{:S(2)}, u32[]{:S(2)}) collective-permute-start(f32[112,128]{1,0:T(8,128)S(1)} %add_up.3.refs_0_), channel_id=1, source_target_pairs={{0,8},{8,0},{16,24},{24,16},{1,9},{9,1},{17,25},{25,17},{2,10},{10... | collective-permute-start | bytes 172040 | tf_op jit(solution)/shard_map/ppermute | solution.py:79
  31.8 2.2 %collective-permute-done.10.refs_0_ = f32[384,128]{1,0:T(8,128)S(1)} collective-permute-done((f32[384,128]{1,0:T(8,128)S(1)}, f32[384,128]{1,0:T(8,128)S(1)}, u32[]{:S(2)}, u32[]{:S(2)}) %collective-permute-start.10) | collective-permute-done | bytes 196640 | tf_op jit(solution)/shard_map/ppermute | solution.py:79
  36.6 0.7 place_coarse.1
  37.7 1.1 %lift_coarse.2.refs_0_ = f32[2,1536,128]{2,1,0:T(8,128)S(1)} custom-call(f32[4,48,768]{2,1,0:T(8,128)S(1)} %get-tuple-element.35.refs_0_, bf16[2,1536,192]{2,1,0:T(8,128)(2,1)S(1)} %get-tuple-element.36.refs_1_, f32[4,96,128]{2,1,0:T(8,128)S(1)} %pile.2.refs_1_.refs_4_.refs_2_, f32[4,96,128]{2,1,0:T(8,128)S(1)} %collective-permute-done.13.refs_3_, ...), custom_call_target="tpu_custom_call" | custom-call | bytes 1200 | tf_op jit(solution)/shard_map/lift_coarse/pallas_call | solution.py:28
  38.8 2.4 %correct.2 = (f32[2,384,128]{2,1,0:T(8,128)S(1)}, bf16[1536,256]{1,0:T(8,128)(2,1)S(1)}, bf16[1536,256]{1,0:T(8,128)(2,1)S(1)}, f32[6,128,128]{2,1,0:T(8,128)S(1...) custom-call(f32[2,1536,128]{2,1,0:T(8,128)S(1)} %lift_coarse.2.refs_0_, ...), custom_call_target="tpu_custom_call" | custom-call | bytes 3000 | tf_op jit(solution)/shard_map/correct/pallas_call | solution.py:28
  41.3 1.4 %reduce_residual.2.refs_4_.refs_1_ = f32[2,384,128]{2,1,0:T(8,128)S(1)} custom-call(bf16[2,768,1536]{2,1,0:T(8,128)(2,1)S(1)} %split_stiffness.1.refs_3_.refs_1_.refs_0_, f32[2,384,128]{2,1,0:T(8,128)S(1)} %get-tuple-element.38.refs_1_, bf16[1536,256]{1,0:T(8,128)(2,1)S(1)} %get-tuple-element.41.refs_2_, bf16[1536,256]{1,0:T(8,128)(2,1)S(1)} %get-tuple-element.42.refs_3_), custom_call_target="tpu_custom_call" | custom-call | bytes 1200 | tf_op jit(solution)/shard_map/reduce_residual/pallas_call | solution.py:28
  42.7 1.6 %collective-permute-start.22 = (f32[2,384,128]{2,1,0:T(8,128)S(1)}, f32[2,384,128]{2,1,0:T(8,128)S(1)}, u32[]{:S(2)}, u32[]{:S(2)}) collective-permute-start(f32[2,384,128]{2,1,0:T(8,128)S(1)} %reduce_residual.2.refs_4_.refs_1_), channel_id=1, source_target_pairs={{0,4},{2,6},{4,0},{6,2},{1,5},{3,7},{5,1},{7,3},{8,12},{10,14},{12... | collective-permute-start | bytes 1179656 | tf_op jit(solution)/shard_map/ppermute | solution.py:79
  44.3 1.1 %collective-permute-start.18 = (f32[6,128,128]{2,1,0:T(8,128)S(1)}, f32[6,128,128]{2,1,0:T(8,128)S(1)}, u32[]{:S(2)}, u32[]{:S(2)}) collective-permute-start(f32[6,128,128]{2,1,0:T(8,128)S(1)} %get-tuple-element.45), channel_id=1, source_target_pairs={{0,8},{8,0},{16,24},{24,16},{1,9},{9,1},{17,25},{25,17},{2,10},{10... | collective-permute-start | bytes 1179656 | tf_op jit(solution)/shard_map/ppermute | solution.py:717
  45.3 1.9 %collective-permute-start.19 = (f32[6,128,128]{2,1,0:T(8,128)S(1)}, f32[6,128,128]{2,1,0:T(8,128)S(1)}, u32[]{:S(2)}, u32[]{:S(2)}) collective-permute-start(f32[6,128,128]{2,1,0:T(8,128)S(1)} %get-tuple-element.46), channel_id=1, source_target_pairs={{8,16},{16,8},{9,17},{17,9},{10,18},{18,10},{11,19},{19,11},{12,20... | collective-permute-start | bytes 1179656 | tf_op jit(solution)/shard_map/ppermute | solution.py:717
  47.3 6.8 %fold_targets.1 = (bf16[2,384,768]{2,1,0:T(8,128)(2,1)S(1)}, bf16[2,768,768]{2,1,0:T(8,128)(2,1)S(1)}, bf16[1,192,768]{2,1,0:T(8,128)(2,1)S(1)}) custom-call(s32[2]{0:T(128)S(1)} %copy-done.3, s32[6,2,128]{2,1,0:T(2,128)S(1)} %bitcast.2, bf16[2,768,1536]{2,1,0:T(8,128)(2,1)S(1)} %split_inverse.1.refs_1_.refs_0_.refs_2_, ...), custom_call_target="tpu_custom_call" | custom-call | bytes 4500 | tf_op jit(solution)/shard_map/fold_targets/pallas_call | solution.py:28
  54.2 0.5 collective-permute-start.23
  54.7 0.6 collective-permute-done.18.refs_3_
  55.4 2.7 %collective-permute-done.19.refs_4_ = f32[6,128,128]{2,1,0:T(8,128)S(1)} collective-permute-done((f32[6,128,128]{2,1,0:T(8,128)S(1)}, f32[6,128,128]{2,1,0:T(8,128)S(1)}, u32[]{:S(2)}, u32[]{:S(2)}) %collective-permute-start.19) | collective-permute-done | bytes 393248 | tf_op jit(solution)/shard_map/ppermute | solution.py:717
  58.0 1.1 %couple.2.refs_2_.refs_8_ = f32[6,128,128]{2,1,0:T(8,128)S(1)} custom-call(s32[8,128]{1,0:T(8,128)S(1)} %get-tuple-element.39.refs_4_.refs_1_.refs_0_, f32[2,6,128,128]{3,2,1,0:T(8,128)S(1)} %copy-done.1, f32[6,128,128]{2,1,0:T(8,128)S(1)} %get-tuple-element.44.refs_2_, f32[6,128,128]{2,1,0:T(8,128)S(1)} %collective-permute-done.18.refs_3_, ...), custom_call_target="tpu_custom_call" | custom-call | bytes 800 | tf_op jit(solution)/shard_map/couple/pallas_call | solution.py:28
  59.3 1.7 %collective-permute-done.20.refs_3_.refs_2_ = f32[6,128,128]{2,1,0:T(8,128)S(1)} collective-permute-done((f32[6,128,128]{2,1,0:T(8,128)S(1)}, f32[6,128,128]{2,1,0:T(8,128)S(1)}, u32[]{:S(2)}, u32[]{:S(2)}) %collective-permute-start.20) | collective-permute-done | bytes 393248 | tf_op jit(solution)/shard_map/ppermute | solution.py:79
  61.0 1.2 %local_solve_inflow.2 = (f32[384,128]{1,0:T(8,128)S(1)}, bf16[1536,256]{1,0:T(8,128)(2,1)S(1)}) custom-call(bf16[2,768,1536]{2,1,0:T(8,128)(2,1)S(1)} %split_inverse.1.refs_1_.refs_0_.refs_2_, bf16[2,768,768]{2,1,0:T(8,128)(2,1)S(1)} %get-tuple-element.47.refs_5_.refs_1_, f32[6,128,128]{2,1,0:T(8,128)S(1)} %couple.2.refs_2_.refs_8_, ...), custom_call_target="tpu_custom_call" | custom-call | bytes 1200 | tf_op jit(solution)/shard_map/local_solve_inflow/pallas_call | solution.py:28
  62.2 1.2 %local_solve_inflow.3 = (f32[384,128]{1,0:T(8,128)S(1)}, bf16[1536,256]{1,0:T(8,128)(2,1)S(1)}) custom-call(bf16[2,768,1536]{2,1,0:T(8,128)(2,1)S(1)} %split_inverse.1.refs_1_.refs_0_.refs_2_, bf16[2,768,768]{2,1,0:T(8,128)(2,1)S(1)} %get-tuple-element.47.refs_5_.refs_1_, f32[6,128,128]{2,1,0:T(8,128)S(1)} %couple.2.refs_2_.refs_8_, ...), custom_call_target="tpu_custom_call" | custom-call | bytes 1200 | tf_op jit(solution)/shard_map/local_solve_inflow/pallas_call | solution.py:28
  63.4 0.6 collective-permute-start.32
  64.0 1.5 %collective-permute-start.29 = (f32[384,128]{1,0:T(8,128)S(1)}, f32[384,128]{1,0:T(8,128)S(1)}, u32[]{:S(2)}, u32[]{:S(2)}) collective-permute-start(f32[384,128]{1,0:T(8,128)S(1)} %get-tuple-element.49.refs_8_.refs_3_), channel_id=1, source_target_pairs={{0,4},{2,6},{4,0},{6,2},{1,5},{3,7},{5,1},{7,3},{8,12},{10,14},{12... | collective-permute-start | bytes 589832 | tf_op jit(solution)/shard_map/ppermute | solution.py:79
  65.5 0.6 restrict.1.refs_0_
  66.9 2.7 %collective-permute-start.24 = (f32[96,128]{1,0:T(8,128)S(1)}, f32[96,128]{1,0:T(8,128)S(1)}, u32[]{:S(2)}, u32[]{:S(2)}) collective-permute-start(f32[96,128]{1,0:T(8,128)S(1)} %restrict.1.refs_0_), channel_id=1, source_target_pairs={{0,8},{8,0},{16,24},{24,16},{1,9},{9,1},{17,25},{25,17},{2,10},{10... | collective-permute-start | bytes 147464 | tf_op jit(solution)/shard_map/ppermute | solution.py:79
  69.7 1.3 %collective-permute-done.26.refs_3_ = f32[96,128]{1,0:T(8,128)S(1)} collective-permute-done((f32[96,128]{1,0:T(8,128)S(1)}, f32[96,128]{1,0:T(8,128)S(1)}, u32[]{:S(2)}, u32[]{:S(2)}) %collective-permute-start.26) | collective-permute-done | bytes 49184 | tf_op jit(solution)/shard_map/ppermute | solution.py:79
  71.0 0.6 collective-permute-done.25.refs_2_
  71.6 0.7 collective-permute-done.24.refs_1_
  72.9 1.7 %collective-permute-done.29.refs_5_ = f32[384,128]{1,0:T(8,128)S(1)} collective-permute-done((f32[384,128]{1,0:T(8,128)S(1)}, f32[384,128]{1,0:T(8,128)S(1)}, u32[]{:S(2)}, u32[]{:S(2)}) %collective-permute-start.29) | collective-permute-done | bytes 196640 | tf_op jit(solution)/shard_map/ppermute | solution.py:79
  74.7 1.1 %lift_coarse.3.refs_0_ = f32[2,1536,128]{2,1,0:T(8,128)S(1)} custom-call(f32[4,48,768]{2,1,0:T(8,128)S(1)} %get-tuple-element.35.refs_0_, bf16[2,1536,192]{2,1,0:T(8,128)(2,1)S(1)} %get-tuple-element.36.refs_1_, f32[4,96,128]{2,1,0:T(8,128)S(1)} %pile.3.refs_2_.refs_4_, f32[4,96,128]{2,1,0:T(8,128)S(1)} %collective-permute-done.27.refs_3_, ...), custom_call_target="tpu_custom_call" | custom-call | bytes 1200 | tf_op jit(solution)/shard_map/lift_coarse/pallas_call | solution.py:28
  76.1 3.2 %correct.3 = (f32[2,384,128]{2,1,0:T(8,128)}, bf16[1536,256]{1,0:T(8,128)(2,1)S(1)}, bf16[1536,256]{1,0:T(8,128)(2,1)S(1)}, f32[6,128,128]{2,1,0:T(8,128)S(1)}, ...) custom-call(f32[2,1536,128]{2,1,0:T(8,128)S(1)} %lift_coarse.3.refs_0_, ...), custom_call_target="tpu_custom_call" | custom-call | bytes 3000 | tf_op jit(solution)/shard_map/correct/pallas_call | solution.py:28
  79.4 2.2 %collective-permute-start.35 = (f32[6,128,128]{2,1,0:T(8,128)S(1)}, f32[6,128,128]{2,1,0:T(8,128)S(1)}, u32[]{:S(2)}, u32[]{:S(2)}) collective-permute-start(f32[6,128,128]{2,1,0:T(8,128)S(1)} %get-tuple-element.59), channel_id=1, source_target_pairs={{8,16},{16,8},{9,17},{17,9},{10,18},{18,10},{11,19},{19,11},{12,20... | collective-permute-start | bytes 1179656 | tf_op jit(solution)/shard_map/ppermute | solution.py:717
  81.6 1.4 %reduce_residual.3.refs_0_.refs_3_ = f32[2,384,128]{2,1,0:T(8,128)S(1)} custom-call(bf16[2,768,1536]{2,1,0:T(8,128)(2,1)S(1)} %split_stiffness.1.refs_3_.refs_1_.refs_0_, f32[2,384,128]{2,1,0:T(8,128)S(1)} %reduce_residual.2.refs_4_.refs_1_, bf16[1536,256]{1,0:T(8,128)(2,1)S(1)} %get-tuple-element.54.refs_2_, bf16[1536,256]{1,0:T(8,128)(2,1)S(1)} %get-tuple-element.55.refs_3_), custom_call_target="tpu_custom_call" | custom-call | bytes 1200 | tf_op jit(solution)/shard_map/reduce_residual/pallas_call | solution.py:28
  83.6 6.9 %collective-permute-done.34.refs_3_ = f32[6,128,128]{2,1,0:T(8,128)S(1)} collective-permute-done((f32[6,128,128]{2,1,0:T(8,128)S(1)}, f32[6,128,128]{2,1,0:T(8,128)S(1)}, u32[]{:S(2)}, u32[]{:S(2)}) %collective-permute-start.34) | collective-permute-done | bytes 393248 | tf_op jit(solution)/shard_map/ppermute | solution.py:717
  90.5 1.9 %collective-permute-done.35.refs_4_ = f32[6,128,128]{2,1,0:T(8,128)S(1)} collective-permute-done((f32[6,128,128]{2,1,0:T(8,128)S(1)}, f32[6,128,128]{2,1,0:T(8,128)S(1)}, u32[]{:S(2)}, u32[]{:S(2)}) %collective-permute-start.35) | collective-permute-done | bytes 393248 | tf_op jit(solution)/shard_map/ppermute | solution.py:717
  92.4 1.1 %couple.3.refs_2_ = f32[6,128,128]{2,1,0:T(8,128)S(1)} custom-call(s32[8,128]{1,0:T(8,128)S(1)} %get-tuple-element.39.refs_4_.refs_1_.refs_0_, f32[2,6,128,128]{3,2,1,0:T(8,128)S(1)} %copy-done.1, f32[6,128,128]{2,1,0:T(8,128)S(1)} %get-tuple-element.57.refs_2_, f32[6,128,128]{2,1,0:T(8,128)S(1)} %collective-permute-done.34.refs_3_, ...), custom_call_target="tpu_custom_call" | custom-call | bytes 800 | tf_op jit(solution)/shard_map/couple/pallas_call | solution.py:28
  94.0 1.4 %collective-permute-done.36.refs_2_ = f32[6,128,128]{2,1,0:T(8,128)S(1)} collective-permute-done((f32[6,128,128]{2,1,0:T(8,128)S(1)}, f32[6,128,128]{2,1,0:T(8,128)S(1)}, u32[]{:S(2)}, u32[]{:S(2)}) %collective-permute-start.36) | collective-permute-done | bytes 393248 | tf_op jit(solution)/shard_map/ppermute | solution.py:79
  95.4 1.1 %add_own_half.7 = f32[2,384,128]{2,1,0:T(8,128)} custom-call(f32[2,384,128]{2,1,0:T(8,128)S(1)} %add_own_half.5.refs_5_.refs_0_, bf16[2,384,768]{2,1,0:T(8,128)(2,1)S(1)} %get-tuple-element.56.refs_1_, f32[6,128,128]{2,1,0:T(8,128)S(1)} %collective-permute-done.36.refs_2_, f32[1,384,128]{2,1,0:T(8,128)S(1)} %add_own_half.6.refs_3_), custom_call_target="tpu_custom_call" | custom-call | bytes 800 | tf_op jit(solution)/shard_map/add_own_half/pallas_call | solution.py:28
  (68 shorter events, 7.0 us)
Async XLA Ops:
  0.6 12.2 %collective-permute-start.5 = (f32[2,384,128]{2,1,0:T(8,128)}, f32[2,384,128]{2,1,0:T(8,128)S(1)}, u32[]{:S(2)}, u32[]{:S(2)}) collective-permute-start(f32[2,384,128]{2,1,0:T(8,128)} %refs_1_.7), channel_id=1, source_target_pairs={{0,4},{2,6},{4,0},{6,2},{1,5},{3,7},{5,1},{7,3},{8,12},{10,14},{12... | collective-permute-start | bytes 1179656 | tf_op jit(solution)/shard_map/ppermute | solution.py:79
  3.7 1.3 %collective-permute-start = (f32[96,128]{1,0:T(8,128)S(1)}, f32[96,128]{1,0:T(8,128)S(1)}, u32[]{:S(2)}, u32[]{:S(2)}) collective-permute-start(f32[96,128]{1,0:T(8,128)S(1)} %get-tuple-element.33), channel_id=1, source_target_pairs={{0,2},{2,0},{4,6},{6,4},{1,3},{3,1},{5,7},{7,5},{8,10},{10,8},{12,... | collective-permute-start | bytes 147464 | tf_op jit(solution)/shard_map/ppermute | solution.py:79
  5.0 7.8 %collective-permute-start.1 = (f32[96,128]{1,0:T(8,128)S(1)}, f32[96,128]{1,0:T(8,128)S(1)}, u32[]{:S(2)}, u32[]{:S(2)}) collective-permute-start(f32[96,128]{1,0:T(8,128)S(1)} %add_up.2.refs_1_.refs_0_), channel_id=1, source_target_pairs={{0,4},{2,6},{4,0},{6,2},{1,5},{3,7},{5,1},{7,3},{8,12},{10,14},{12... | collective-permute-start | bytes 147464 | tf_op jit(solution)/shard_map/ppermute | solution.py:79
  5.6 8.9 %collective-permute-start.4 = (f32[2,384,128]{2,1,0:T(8,128)}, f32[2,384,128]{2,1,0:T(8,128)S(1)}, u32[]{:S(2)}, u32[]{:S(2)}) collective-permute-start(f32[2,384,128]{2,1,0:T(8,128)} %refs_1_.7), channel_id=1, source_target_pairs={{0,2},{2,0},{4,6},{6,4},{1,3},{3,1},{5,7},{7,5},{8,10},{10,8},{12,... | collective-permute-start | bytes 1179656 | tf_op jit(solution)/shard_map/ppermute | solution.py:79
  12.8 1.8 %copy-start = (f32[2,384,128]{2,1,0:T(8,128)S(1)}, f32[2,384,128]{2,1,0:T(8,128)}, u32[]{:S(2)}) copy-start(f32[2,384,128]{2,1,0:T(8,128)} %refs_1_.7) | copy-start | bytes 1179652
  12.9 1.8 %collective-permute-start.6 = (f32[2,384,128]{2,1,0:T(8,128)S(1)}, f32[2,384,128]{2,1,0:T(8,128)S(1)}, u32[]{:S(2)}, u32[]{:S(2)}) collective-permute-start(f32[2,384,128]{2,1,0:T(8,128)S(1)} %relay.9.refs_3_), channel_id=1, source_target_pairs={{0,2},{2,0},{4,6},{6,4},{1,3},{3,1},{5,7},{7,5},{8,10},{10,8},{12,... | collective-permute-start | bytes 1179656 | tf_op jit(solution)/shard_map/ppermute | solution.py:79
  13.0 21.4 %collective-permute-start.3 = (f32[288,384]{1,0:T(8,128)S(1)}, f32[288,384]{1,0:T(8,128)S(1)}, u32[]{:S(2)}, u32[]{:S(2)}) collective-permute-start(f32[288,384]{1,0:T(8,128)S(1)} %relay.8.refs_0_), channel_id=1, source_target_pairs={{0,4},{2,6},{4,0},{6,2},{1,5},{3,7},{5,1},{7,3},{8,12},{10,14},{12... | collective-permute-start | bytes 1327112 | tf_op jit(solution)/shard_map/ppermute | solution.py:79
  16.2 14.0 %collective-permute-start.11 = (f32[384,128]{1,0:T(8,128)S(1)}, f32[384,128]{1,0:T(8,128)S(1)}, u32[]{:S(2)}, u32[]{:S(2)}) collective-permute-start(f32[384,128]{1,0:T(8,128)S(1)} %local_solve.3.refs_1_.refs_7_), channel_id=1, source_target_pairs={{0,4},{2,6},{4,0},{6,2},{1,5},{3,7},{5,1},{7,3},{8,12},{10,14},{12... | collective-permute-start | bytes 589832 | tf_op jit(solution)/shard_map/ppermute | solution.py:79
  17.8 16.2 %collective-permute-start.10 = (f32[384,128]{1,0:T(8,128)S(1)}, f32[384,128]{1,0:T(8,128)S(1)}, u32[]{:S(2)}, u32[]{:S(2)}) collective-permute-start(f32[384,128]{1,0:T(8,128)S(1)} %local_solve.2.refs_5_.refs_3_), channel_id=1, source_target_pairs={{0,4},{2,6},{4,0},{6,2},{1,5},{3,7},{5,1},{7,3},{8,12},{10,14},{12... | collective-permute-start | bytes 589832 | tf_op jit(solution)/shard_map/ppermute | solution.py:79
  20.8 13.3 %collective-permute-start.9 = (f32[112,128]{1,0:T(8,128)S(1)}, f32[112,128]{1,0:T(8,128)S(1)}, u32[]{:S(2)}, u32[]{:S(2)}) collective-permute-start(f32[112,128]{1,0:T(8,128)S(1)} %add_up.3.refs_0_), channel_id=1, source_target_pairs={{0,24},{8,16},{16,8},{24,0},{1,25},{9,17},{17,9},{25,1},{2,26},{10... | collective-permute-start | bytes 172040 | tf_op jit(solution)/shard_map/ppermute | solution.py:79
  21.3 12.8 %collective-permute-start.8 = (f32[112,128]{1,0:T(8,128)S(1)}, f32[112,128]{1,0:T(8,128)S(1)}, u32[]{:S(2)}, u32[]{:S(2)}) collective-permute-start(f32[112,128]{1,0:T(8,128)S(1)} %add_up.3.refs_0_), channel_id=1, source_target_pairs={{0,16},{8,24},{16,0},{24,8},{1,17},{9,25},{17,1},{25,9},{2,18},{10... | collective-permute-start | bytes 172040 | tf_op jit(solution)/shard_map/ppermute | solution.py:79
  30.2 4.2 %collective-permute-start.7 = (f32[112,128]{1,0:T(8,128)S(1)}, f32[112,128]{1,0:T(8,128)S(1)}, u32[]{:S(2)}, u32[]{:S(2)}) collective-permute-start(f32[112,128]{1,0:T(8,128)S(1)} %add_up.3.refs_0_), channel_id=1, source_target_pairs={{0,8},{8,0},{16,24},{24,16},{1,9},{9,1},{17,25},{25,17},{2,10},{10... | collective-permute-start | bytes 172040 | tf_op jit(solution)/shard_map/ppermute | solution.py:79
  34.0 1.8 %collective-permute-start.2 = (f32[288,384]{1,0:T(8,128)S(1)}, f32[288,384]{1,0:T(8,128)S(1)}, u32[]{:S(2)}, u32[]{:S(2)}) collective-permute-start(f32[288,384]{1,0:T(8,128)S(1)} %relay.8.refs_0_), channel_id=1, source_target_pairs={{0,2},{2,0},{4,6},{6,4},{1,3},{3,1},{5,7},{7,5},{8,10},{10,8},{12,... | collective-permute-start | bytes 1327112 | tf_op jit(solution)/shard_map/ppermute | solution.py:79
  34.5 2.0 %collective-permute-start.12 = (f32[288,384]{1,0:T(8,128)S(1)}, f32[288,384]{1,0:T(8,128)S(1)}, u32[]{:S(2)}, u32[]{:S(2)}) collective-permute-start(f32[288,384]{1,0:T(8,128)S(1)} %relay.12.refs_2_), channel_id=1, source_target_pairs={{0,2},{2,0},{4,6},{6,4},{1,3},{3,1},{5,7},{7,5},{8,10},{10,8},{12,... | collective-permute-start | bytes 1327112 | tf_op jit(solution)/shard_map/ppermute | solution.py:79
  34.7 3.0 %collective-permute-start.13 = (f32[4,96,128]{2,1,0:T(8,128)S(1)}, f32[4,96,128]{2,1,0:T(8,128)S(1)}, u32[]{:S(2)}, u32[]{:S(2)}) collective-permute-start(f32[4,96,128]{2,1,0:T(8,128)S(1)} %pile.2.refs_1_.refs_4_.refs_2_), channel_id=1, source_target_pairs={{0,2},{2,0},{4,6},{6,4},{1,3},{3,1},{5,7},{7,5},{8,10},{10,8},{12,... | collective-permute-start | bytes 589832 | tf_op jit(solution)/shard_map/ppermute | solution.py:79
  35.0 3.8 %collective-permute-start.16 = (f32[384,128]{1,0:T(8,128)S(1)}, f32[384,128]{1,0:T(8,128)S(1)}, u32[]{:S(2)}, u32[]{:S(2)}) collective-permute-start(f32[384,128]{1,0:T(8,128)S(1)} %local_solve.3.refs_1_.refs_7_), channel_id=1, source_target_pairs={{0,2},{2,0},{4,6},{6,4},{1,3},{3,1},{5,7},{7,5},{8,10},{10,8},{12,... | collective-permute-start | bytes 589832 | tf_op jit(solution)/shard_map/ppermute | solution.py:79
  35.2 3.6 %collective-permute-start.14 = (f32[384,128]{1,0:T(8,128)S(1)}, f32[384,128]{1,0:T(8,128)S(1)}, u32[]{:S(2)}, u32[]{:S(2)}) collective-permute-start(f32[384,128]{1,0:T(8,128)S(1)} %local_solve.2.refs_5_.refs_3_), channel_id=1, source_target_pairs={{0,2},{2,0},{4,6},{6,4},{1,3},{3,1},{5,7},{7,5},{8,10},{10,8},{12,... | collective-permute-start | bytes 589832 | tf_op jit(solution)/shard_map/ppermute | solution.py:79
  35.8 3.0 %collective-permute-start.15 = (f32[384,128]{1,0:T(8,128)S(1)}, f32[384,128]{1,0:T(8,128)S(1)}, u32[]{:S(2)}, u32[]{:S(2)}) collective-permute-start(f32[384,128]{1,0:T(8,128)S(1)} %relay.10.refs_4_.refs_5_), channel_id=1, source_target_pairs={{0,2},{2,0},{4,6},{6,4},{1,3},{3,1},{5,7},{7,5},{8,10},{10,8},{12,... | collective-permute-start | bytes 589832 | tf_op jit(solution)/shard_map/ppermute | solution.py:79
  36.5 2.4 %collective-permute-start.17 = (f32[384,128]{1,0:T(8,128)S(1)}, f32[384,128]{1,0:T(8,128)S(1)}, u32[]{:S(2)}, u32[]{:S(2)}) collective-permute-start(f32[384,128]{1,0:T(8,128)S(1)} %relay.11.refs_5_.refs_9_), channel_id=1, source_target_pairs={{0,2},{2,0},{4,6},{6,4},{1,3},{3,1},{5,7},{7,5},{8,10},{10,8},{12,... | collective-permute-start | bytes 589832 | tf_op jit(solution)/shard_map/ppermute | solution.py:79
  41.3 6.0 %copy-start.2 = (s32[2,6,128]{2,0,1:T(2,128)S(1)}, s32[2,6,128]{2,0,1:T(2,128)}, u32[]{:S(2)}) copy-start(s32[2,6,128]{2,0,1:T(2,128)} %param.16) | copy-start | bytes 18436
  41.3 6.0 %copy-start.3 = (s32[2]{0:T(128)S(1)}, s32[2]{0:T(128)}, u32[]{:S(2)}) copy-start(s32[2]{0:T(128)} %refs_0_.7) | copy-start | bytes 28
  42.7 11.5 %collective-permute-start.22 = (f32[2,384,128]{2,1,0:T(8,128)S(1)}, f32[2,384,128]{2,1,0:T(8,128)S(1)}, u32[]{:S(2)}, u32[]{:S(2)}) collective-permute-start(f32[2,384,128]{2,1,0:T(8,128)S(1)} %reduce_residual.2.refs_4_.refs_1_), channel_id=1, source_target_pairs={{0,4},{2,6},{4,0},{6,2},{1,5},{3,7},{5,1},{7,3},{8,12},{10,14},{12... | collective-permute-start | bytes 1179656 | tf_op jit(solution)/shard_map/ppermute | solution.py:79
  44.3 11.1 %collective-permute-start.18 = (f32[6,128,128]{2,1,0:T(8,128)S(1)}, f32[6,128,128]{2,1,0:T(8,128)S(1)}, u32[]{:S(2)}, u32[]{:S(2)}) collective-permute-start(f32[6,128,128]{2,1,0:T(8,128)S(1)} %get-tuple-element.45), channel_id=1, source_target_pairs={{0,8},{8,0},{16,24},{24,16},{1,9},{9,1},{17,25},{25,17},{2,10},{10... | collective-permute-start | bytes 1179656 | tf_op jit(solution)/shard_map/ppermute | solution.py:717
  45.3 12.7 %collective-permute-start.19 = (f32[6,128,128]{2,1,0:T(8,128)S(1)}, f32[6,128,128]{2,1,0:T(8,128)S(1)}, u32[]{:S(2)}, u32[]{:S(2)}) collective-permute-start(f32[6,128,128]{2,1,0:T(8,128)S(1)} %get-tuple-element.46), channel_id=1, source_target_pairs={{8,16},{16,8},{9,17},{17,9},{10,18},{18,10},{11,19},{19,11},{12,20... | collective-permute-start | bytes 1179656 | tf_op jit(solution)/shard_map/ppermute | solution.py:717
  47.2 12.0 %collective-permute-start.21 = (f32[2,384,128]{2,1,0:T(8,128)S(1)}, f32[2,384,128]{2,1,0:T(8,128)S(1)}, u32[]{:S(2)}, u32[]{:S(2)}) collective-permute-start(f32[2,384,128]{2,1,0:T(8,128)S(1)} %reduce_residual.2.refs_4_.refs_1_), channel_id=1, source_target_pairs={{0,2},{2,0},{4,6},{6,4},{1,3},{3,1},{5,7},{7,5},{8,10},{10,8},{12,... | collective-permute-start | bytes 1179656 | tf_op jit(solution)/shard_map/ppermute | solution.py:79
  54.1 3.9 %copy-start.1 = (f32[2,6,128,128]{3,2,1,0:T(8,128)S(1)}, f32[2,6,128,128]{3,2,1,0:T(8,128)}, u32[]{:S(2)}) copy-start(f32[2,6,128,128]{3,2,1,0:T(8,128)} %refs_1_.9) | copy-start | bytes 2359300
  54.2 5.1 %collective-permute-start.23 = (f32[2,384,128]{2,1,0:T(8,128)S(1)}, f32[2,384,128]{2,1,0:T(8,128)S(1)}, u32[]{:S(2)}, u32[]{:S(2)}) collective-permute-start(f32[2,384,128]{2,1,0:T(8,128)S(1)} %relay.13.refs_6_), channel_id=1, source_target_pairs={{0,2},{2,0},{4,6},{6,4},{1,3},{3,1},{5,7},{7,5},{8,10},{10,8},{12,... | collective-permute-start | bytes 1179656 | tf_op jit(solution)/shard_map/ppermute | solution.py:79
  59.2 1.8 %collective-permute-start.20 = (f32[6,128,128]{2,1,0:T(8,128)S(1)}, f32[6,128,128]{2,1,0:T(8,128)S(1)}, u32[]{:S(2)}, u32[]{:S(2)}) collective-permute-start(f32[6,128,128]{2,1,0:T(8,128)S(1)} %couple.2.refs_2_.refs_8_), channel_id=1, source_target_pairs={{0,2},{2,0},{4,6},{6,4},{1,3},{3,1},{5,7},{7,5},{8,10},{10,8},{12,... | collective-permute-start | bytes 1179656 | tf_op jit(solution)/shard_map/ppermute | solution.py:79
  63.4 9.4 %collective-permute-start.32 = (f32[384,128]{1,0:T(8,128)S(1)}, f32[384,128]{1,0:T(8,128)S(1)}, u32[]{:S(2)}, u32[]{:S(2)}) collective-permute-start(f32[384,128]{1,0:T(8,128)S(1)} %get-tuple-element.51.refs_5_.refs_7_), channel_id=1, source_target_pairs={{0,4},{2,6},{4,0},{6,2},{1,5},{3,7},{5,1},{7,3},{8,12},{10,14},{12... | collective-permute-start | bytes 589832 | tf_op jit(solution)/shard_map/ppermute | solution.py:79
  64.0 10.6 %collective-permute-start.29 = (f32[384,128]{1,0:T(8,128)S(1)}, f32[384,128]{1,0:T(8,128)S(1)}, u32[]{:S(2)}, u32[]{:S(2)}) collective-permute-start(f32[384,128]{1,0:T(8,128)S(1)} %get-tuple-element.49.refs_8_.refs_3_), channel_id=1, source_target_pairs={{0,4},{2,6},{4,0},{6,2},{1,5},{3,7},{5,1},{7,3},{8,12},{10,14},{12... | collective-permute-start | bytes 589832 | tf_op jit(solution)/shard_map/ppermute | solution.py:79
  66.1 4.9 %collective-permute-start.26 = (f32[96,128]{1,0:T(8,128)S(1)}, f32[96,128]{1,0:T(8,128)S(1)}, u32[]{:S(2)}, u32[]{:S(2)}) collective-permute-start(f32[96,128]{1,0:T(8,128)S(1)} %restrict.1.refs_0_), channel_id=1, source_target_pairs={{0,24},{8,16},{16,8},{24,0},{1,25},{9,17},{17,9},{25,1},{2,26},{10... | collective-permute-start | bytes 147464 | tf_op jit(solution)/shard_map/ppermute | solution.py:79
  66.5 5.1 %collective-permute-start.25 = (f32[96,128]{1,0:T(8,128)S(1)}, f32[96,128]{1,0:T(8,128)S(1)}, u32[]{:S(2)}, u32[]{:S(2)}) collective-permute-start(f32[96,128]{1,0:T(8,128)S(1)} %restrict.1.refs_0_), channel_id=1, source_target_pairs={{0,16},{8,24},{16,0},{24,8},{1,17},{9,25},{17,1},{25,9},{2,18},{10... | collective-permute-start | bytes 147464 | tf_op jit(solution)/shard_map/ppermute | solution.py:79
  66.9 5.3 %collective-permute-start.24 = (f32[96,128]{1,0:T(8,128)S(1)}, f32[96,128]{1,0:T(8,128)S(1)}, u32[]{:S(2)}, u32[]{:S(2)}) collective-permute-start(f32[96,128]{1,0:T(8,128)S(1)} %restrict.1.refs_0_), channel_id=1, source_target_pairs={{0,8},{8,0},{16,24},{24,16},{1,9},{9,1},{17,25},{25,17},{2,10},{10... | collective-permute-start | bytes 147464 | tf_op jit(solution)/shard_map/ppermute | solution.py:79
  71.0 4.7 %collective-permute-start.31 = (f32[384,128]{1,0:T(8,128)S(1)}, f32[384,128]{1,0:T(8,128)S(1)}, u32[]{:S(2)}, u32[]{:S(2)}) collective-permute-start(f32[384,128]{1,0:T(8,128)S(1)} %get-tuple-element.51.refs_5_.refs_7_), channel_id=1, source_target_pairs={{0,2},{2,0},{4,6},{6,4},{1,3},{3,1},{5,7},{7,5},{8,10},{10,8},{12,... | collective-permute-start | bytes 589832 | tf_op jit(solution)/shard_map/ppermute | solution.py:79
  72.3 2.4 %collective-permute-start.27 = (f32[4,96,128]{2,1,0:T(8,128)S(1)}, f32[4,96,128]{2,1,0:T(8,128)S(1)}, u32[]{:S(2)}, u32[]{:S(2)}) collective-permute-start(f32[4,96,128]{2,1,0:T(8,128)S(1)} %pile.3.refs_2_.refs_4_), channel_id=1, source_target_pairs={{0,2},{2,0},{4,6},{6,4},{1,3},{3,1},{5,7},{7,5},{8,10},{10,8},{12,... | collective-permute-start | bytes 589832 | tf_op jit(solution)/shard_map/ppermute | solution.py:79
  72.4 3.4 %collective-permute-start.28 = (f32[384,128]{1,0:T(8,128)S(1)}, f32[384,128]{1,0:T(8,128)S(1)}, u32[]{:S(2)}, u32[]{:S(2)}) collective-permute-start(f32[384,128]{1,0:T(8,128)S(1)} %get-tuple-element.49.refs_8_.refs_3_), channel_id=1, source_target_pairs={{0,2},{2,0},{4,6},{6,4},{1,3},{3,1},{5,7},{7,5},{8,10},{10,8},{12,... | collective-permute-start | bytes 589832 | tf_op jit(solution)/shard_map/ppermute | solution.py:79
  72.9 2.9 %collective-permute-start.33 = (f32[384,128]{1,0:T(8,128)S(1)}, f32[384,128]{1,0:T(8,128)S(1)}, u32[]{:S(2)}, u32[]{:S(2)}) collective-permute-start(f32[384,128]{1,0:T(8,128)S(1)} %collective-permute-done.32.refs_9_), channel_id=1, source_target_pairs={{0,2},{2,0},{4,6},{6,4},{1,3},{3,1},{5,7},{7,5},{8,10},{10,8},{12,... | collective-permute-start | bytes 589832 | tf_op jit(solution)/shard_map/ppermute | solution.py:79
  74.7 1.4 %collective-permute-start.30 = (f32[384,128]{1,0:T(8,128)S(1)}, f32[384,128]{1,0:T(8,128)S(1)}, u32[]{:S(2)}, u32[]{:S(2)}) collective-permute-start(f32[384,128]{1,0:T(8,128)S(1)} %collective-permute-done.29.refs_5_), channel_id=1, source_target_pairs={{0,2},{2,0},{4,6},{6,4},{1,3},{3,1},{5,7},{7,5},{8,10},{10,8},{12,... | collective-permute-start | bytes 589832 | tf_op jit(solution)/shard_map/ppermute | solution.py:79
  79.3 11.3 %collective-permute-start.34 = (f32[6,128,128]{2,1,0:T(8,128)S(1)}, f32[6,128,128]{2,1,0:T(8,128)S(1)}, u32[]{:S(2)}, u32[]{:S(2)}) collective-permute-start(f32[6,128,128]{2,1,0:T(8,128)S(1)} %get-tuple-element.58), channel_id=1, source_target_pairs={{0,8},{8,0},{16,24},{24,16},{1,9},{9,1},{17,25},{25,17},{2,10},{10... | collective-permute-start | bytes 1179656 | tf_op jit(solution)/shard_map/ppermute | solution.py:717
  79.4 13.1 %collective-permute-start.35 = (f32[6,128,128]{2,1,0:T(8,128)S(1)}, f32[6,128,128]{2,1,0:T(8,128)S(1)}, u32[]{:S(2)}, u32[]{:S(2)}) collective-permute-start(f32[6,128,128]{2,1,0:T(8,128)S(1)} %get-tuple-element.59), channel_id=1, source_target_pairs={{8,16},{16,8},{9,17},{17,9},{10,18},{18,10},{11,19},{19,11},{12,20... | collective-permute-start | bytes 1179656 | tf_op jit(solution)/shard_map/ppermute | solution.py:717
  93.6 1.8 %collective-permute-start.36 = (f32[6,128,128]{2,1,0:T(8,128)S(1)}, f32[6,128,128]{2,1,0:T(8,128)S(1)}, u32[]{:S(2)}, u32[]{:S(2)}) collective-permute-start(f32[6,128,128]{2,1,0:T(8,128)S(1)} %couple.3.refs_2_), channel_id=1, source_target_pairs={{0,2},{2,0},{4,6},{6,4},{1,3},{3,1},{5,7},{7,5},{8,10},{10,8},{12,... | collective-permute-start | bytes 1179656 | tf_op jit(solution)/shard_map/ppermute | solution.py:79

commit v4 on v3

--- a/solution.py
+++ b/solution.py
@@ -472,20 +472,18 @@
     )[0]
 
 
-def correct(lifted, blocks, old, info, lists, after=()):
+def correct(lifted, blocks, info, lists, after=()):
     subs = len(blocks)
     count = len(blocks[0])
     rows, cases = blocks[0][0].shape
     order = rows * count
     ways, slots, _, width, _ = lists.shape
-    has_old = old is not None
 
     def kernel(up, facts, l, *refs):
         block_refs = refs[: subs * count]
         refs = refs[subs * count :]
-        old_ref, refs = (refs[0], refs[1:]) if has_old else (None, refs)
-        total, corrs, outs = refs[0], refs[1 : 1 + subs], refs[1 + subs : 1 + subs + ways]
-        where, sem = refs[1 + subs + ways :]
+        corrs, outs = refs[:subs], refs[subs : subs + ways]
+        where, sem = refs[subs + ways :]
         move = pltpu.make_async_copy(facts, where, sem)
         move.start()
         core = position()[1]
@@ -494,8 +492,6 @@
                 here = slice(q * rows, (q + 1) * rows)
                 value = block_refs[s * count + q][...] + up[s, here]
                 corrs[s][here] = beside(value)
-                if q == 0:
-                    total[s] = damping * value + old_ref[s] if has_old else damping * value
         move.wait()
         lane = lax.broadcasted_iota(jnp.int32, (width, width), 1).astype(f32).astype(bf16)
         none = jnp.zeros((width, width), bf16)
@@ -522,9 +518,8 @@
     return call(
         kernel,
         "correct",
-        [lifted, info, lists, *flat] + ([old] if has_old else []),
-        [((subs, rows, cases), f32)]
-        + [((order, 2 * cases), bf16)] * subs
+        [lifted, info, lists, *flat],
+        [((order, 2 * cases), bf16)] * subs
         + [((slots, width, cases), f32)] * ways,
         3.0,
         scratch=[pltpu.SMEM(info.shape, jnp.int32), pltpu.SemaphoreType.DMA(())],
@@ -532,21 +527,24 @@
     )
 
 
-def reduce_residual(split, corrs, residual, after=()):
+def reduce_residual(split, corrs, residual, lifted, own, old=None, after=()):
     subs, rows, cases = residual.shape
 
-    def kernel(m, res, *refs):
+    def kernel(m, res, up, *refs):
+        o, total = refs[-2:]
         for s in range(subs):
-            refs[subs][s] = res[s] - damping * folded(dot(m[s], refs[s][...]))
+            o[s] = res[s] - damping * folded(dot(m[s], refs[s][...]))
+            value = damping * (refs[subs + s][...] + up[s, :rows])
+            total[s] = value if old is None else refs[2 * subs][s] + value
 
     return call(
         kernel,
         "reduce_residual",
-        [split, residual, *corrs],
-        [(residual.shape, f32)],
+        [split, residual, lifted, *corrs, *own] + ([] if old is None else [old]),
+        [(residual.shape, f32), (residual.shape, f32)],
         1.2,
         after=after,
-    )[0]
+    )
 
 
 def couple(info, coupling, sources, after=()):
@@ -697,25 +695,25 @@
     mine = pile(halves, height, arrived)
     other = exchange(mine, "crow", 1)
     pieces = gathered(both, [mine])
-    down, lift, inverse = place_coarse(
-        pieces, subs, coarse_basis.shape[1], coarse_inverse.shape[0], [mine]
-    )
-
     if groups == 4:
         held = [packed, halves[1], halves[3]]
     else:
         held = [packed] + [lax.ppermute(packed, "sub", route) for route in routes]
-    lists, info = prepare(held, subs, slots, rows, crow_size, [down])
-
-    total, last = None, info
+    lists, info = prepare(held, subs, slots, rows, crow_size, [mine])
+    down, lift, inverse = place_coarse(
+        pieces, subs, coarse_basis.shape[1], coarse_inverse.shape[0], [info]
+    )
+
+    total, last = None, down
     for sweep_index in range(ITERS):
         if sweep_index:
             local_blocks = [gathered(v) for v in local]
         lifted = lift_coarse(inverse, lift, mine, other, [last])
-        total, *rest = correct(lifted, local_blocks, total, info, lists)
+        rest = correct(lifted, local_blocks, info, lists)
         corrs, chosen = rest[:subs], rest[subs:]
         sources = [chosen[0]] + [lax.ppermute(c, "sub", route) for c, route in zip(chosen[1:], routes)]
-        residual = reduce_residual(stiffness_split, corrs, residual)
+        own = [blocks[0] for blocks in local_blocks]
+        residual, total = reduce_residual(stiffness_split, corrs, residual, lifted, own, total)
         if sweep_index == 0:
             own_hits, folds, z_folds = fold_targets(
                 counts, targets, inverse_split, down, [residual]

time: 96.6 us -> 96.1 us (level); the launches traced: 96.5 us -> 94.7 us
  waiting for transfers between devices: 34.7 us -> 32.4 us
  Pallas kernels: 33.9 us -> 35.5 us
  starting transfers between devices: 26.7 us -> 25.7 us
    ppermute x4, waiting for transfers between devices: 12.1 us -> 9.91 us  [per_device(): lax.ppermute(c, 'sub', route)]
    pallas_call x34, Pallas kernels: 33.9 us -> 35.5 us  [call(): pl.pallas_call(body, in_specs=[IN_SMEM] * scalars + [IN_VMEM] * (used - s...]
    ppermute x4, starting transfers between devices: 5.23 us -> 4.14 us  [per_device(): lax.ppermute(c, 'sub', route)]
  transfers between devices with their start and end apart: 37 -> 37, of which waited for: 19 -> 19; matrix products, arithmetic and copies ran while one was open for 0% -> 0% of each run, Pallas kernels for 23% -> 24%
where the time goes in v4:
time: 96.1 us; the launch traced here: 94.7 us
  Pallas kernels  35.5 us (37%)
  waiting for transfers between devices  32.4 us (34%)
  starting transfers between devices  25.7 us (27%)
  between operations  1.09 us (1%)
    pallas_call x34, Pallas kernels, call(): pl.pallas_call(body, in_specs=[IN_SMEM] * scalars + [IN_VMEM] * (used - s...  35.5 us
    ppermute x33, waiting for transfers between devices, exchange(): lax.ppermute(x, axis, [(i, i ^ bit) for i in range(size) if i ^ bit < size])  22.5 us
    ppermute x33, starting transfers between devices, exchange(): lax.ppermute(x, axis, [(i, i ^ bit) for i in range(size) if i ^ bit < size])  21.5 us
    ppermute x4, waiting for transfers between devices, per_device(): lax.ppermute(c, 'sub', route)  9.91 us
    ppermute x4, starting transfers between devices, per_device(): lax.ppermute(c, 'sub', route)  4.14 us
  transfers between devices with their start and end apart: 37, of which 19 were waited for; matrix products, arithmetic and copies ran while one was open for 0% of the time, Pallas kernels for 24%

profile of v4, /device:TPU:16, one launch (start us, length us, event | category | flops | bytes accessed | tf_op | source)
XLA Modules:
  0.0 94.7 jit_solution(14633382102066860289)
XLA Ops:
  0.6 1.6 %collective-permute-start.2 = (f32[2,384,128]{2,1,0:T(8,128)}, f32[2,384,128]{2,1,0:T(8,128)S(1)}, u32[]{:S(2)}, u32[]{:S(2)}) collective-permute-start(f32[2,384,128]{2,1,0:T(8,128)} %refs_1_.7), channel_id=1, source_target_pairs={{0,4},{2,6},{4,0},{6,2},{1,5},{3,7},{5,1},{7,3},{8,12},{10,14},{12... | collective-permute-start | bytes 1179656 | tf_op jit(solution)/shard_map/ppermute | solution.py:79
  2.2 1.5 %begin.1 = (f32[96,128]{1,0:T(8,128)S(1)}, f32[96,128]{1,0:T(8,128)S(1)}, f32[2,384,128]{2,1,0:T(8,128)S(1)}, f32[16,128]{1,0:T(8,128)S(1)}, f32[288,384]{1,0:T(8,128)S(1)}) custom-call(s32[2,6]{1,0:T(2,128)} %refs_0_.4, s32[2]{0:T(128)} %refs_0_.7, s32[6,2,128]{2,1,0:T(2,128)} %bitcast.3, f32[2,96,384]{2,1,0:T(8,128)} %refs_3_.1, f32[2,384,128]{2,1,0:T(8,128)} %refs_1_.7, ...), custom_call_target="tpu_custom_call" | custom-call | bytes 2000 | tf_op jit(solution)/shard_map/begin/pallas_call | solution.py:28
  3.8 1.2 %collective-permute-done.refs_1_ = f32[96,128]{1,0:T(8,128)S(1)} collective-permute-done((f32[96,128]{1,0:T(8,128)S(1)}, f32[96,128]{1,0:T(8,128)S(1)}, u32[]{:S(2)}, u32[]{:S(2)}) %collective-permute-start) | collective-permute-done | bytes 49184 | tf_op jit(solution)/shard_map/ppermute | solution.py:79
  5.0 0.6 collective-permute-start.3
  5.6 2.5 %split_inverse.1.refs_1_.refs_0_.refs_2_ = bf16[2,768,1536]{2,1,0:T(8,128)(2,1)S(1)} custom-call(f32[2,384,1536]{2,1,0:T(8,128)} %refs_0_.5, f32[96,128]{1,0:T(8,128)S(1)} %add_up.2.refs_1_.refs_0_), custom_call_target="tpu_custom_call" | custom-call | bytes 2000 | tf_op jit(solution)/shard_map/split_inverse/pallas_call | solution.py:28
  8.1 4.7 %collective-permute-done.3.refs_0_ = f32[96,128]{1,0:T(8,128)S(1)} collective-permute-done((f32[96,128]{1,0:T(8,128)S(1)}, f32[96,128]{1,0:T(8,128)S(1)}, u32[]{:S(2)}, u32[]{:S(2)}) %collective-permute-start.3) | collective-permute-done | bytes 49184 | tf_op jit(solution)/shard_map/ppermute | solution.py:79
  13.0 1.6 %collective-permute-start.6 = (f32[288,384]{1,0:T(8,128)S(1)}, f32[288,384]{1,0:T(8,128)S(1)}, u32[]{:S(2)}, u32[]{:S(2)}) collective-permute-start(f32[288,384]{1,0:T(8,128)S(1)} %relay.9.refs_0_), channel_id=1, source_target_pairs={{0,4},{2,6},{4,0},{6,2},{1,5},{3,7},{5,1},{7,3},{8,12},{10,14},{12... | collective-permute-start | bytes 1327112 | tf_op jit(solution)/shard_map/ppermute | solution.py:79
  14.7 0.8 local_solve.2.refs_5_.refs_3_
  15.4 0.8 local_solve.3.refs_1_.refs_7_.refs_6_
  16.2 1.6 %collective-permute-start.11 = (f32[384,128]{1,0:T(8,128)S(1)}, f32[384,128]{1,0:T(8,128)S(1)}, u32[]{:S(2)}, u32[]{:S(2)}) collective-permute-start(f32[384,128]{1,0:T(8,128)S(1)} %local_solve.3.refs_1_.refs_7_.refs_6_), channel_id=1, source_target_pairs={{0,4},{2,6},{4,0},{6,2},{1,5},{3,7},{5,1},{7,3},{8,12},{10,14},{12... | collective-permute-start | bytes 589832 | tf_op jit(solution)/shard_map/ppermute | solution.py:79
  17.8 0.5 collective-permute-start.10
  18.3 2.5 %split_stiffness.1.refs_3_.refs_1_.refs_0_ = bf16[2,768,1536]{2,1,0:T(8,128)(2,1)S(1)} custom-call(f32[2,384,1536]{2,1,0:T(8,128)} %refs_0_.6, f32[384,128]{1,0:T(8,128)S(1)} %local_solve.3.refs_1_.refs_7_.refs_6_), custom_call_target="tpu_custom_call" | custom-call | bytes 9000000 | tf_op jit(solution)/shard_map/split_stiffness/pallas_call | solution.py:28
  20.8 0.5 collective-permute-start.9
  21.3 3.5 %collective-permute-start.8 = (f32[112,128]{1,0:T(8,128)S(1)}, f32[112,128]{1,0:T(8,128)S(1)}, u32[]{:S(2)}, u32[]{:S(2)}) collective-permute-start(f32[112,128]{1,0:T(8,128)S(1)} %add_up.3.refs_0_), channel_id=1, source_target_pairs={{0,16},{8,24},{16,0},{24,8},{1,17},{9,25},{17,1},{25,9},{2,18},{10... | collective-permute-start | bytes 172040 | tf_op jit(solution)/shard_map/ppermute | solution.py:79
  24.8 5.4 %collective-permute-done.11.refs_0_ = f32[384,128]{1,0:T(8,128)S(1)} collective-permute-done((f32[384,128]{1,0:T(8,128)S(1)}, f32[384,128]{1,0:T(8,128)S(1)}, u32[]{:S(2)}, u32[]{:S(2)}) %collective-permute-start.11) | collective-permute-done | bytes 196640 | tf_op jit(solution)/shard_map/ppermute | solution.py:79
  30.2 1.6 %collective-permute-start.7 = (f32[112,128]{1,0:T(8,128)S(1)}, f32[112,128]{1,0:T(8,128)S(1)}, u32[]{:S(2)}, u32[]{:S(2)}) collective-permute-start(f32[112,128]{1,0:T(8,128)S(1)} %add_up.3.refs_0_), channel_id=1, source_target_pairs={{0,8},{8,0},{16,24},{24,16},{1,9},{9,1},{17,25},{25,17},{2,10},{10... | collective-permute-start | bytes 172040 | tf_op jit(solution)/shard_map/ppermute | solution.py:79
  31.8 2.2 %collective-permute-done.10.refs_0_ = f32[384,128]{1,0:T(8,128)S(1)} collective-permute-done((f32[384,128]{1,0:T(8,128)S(1)}, f32[384,128]{1,0:T(8,128)S(1)}, u32[]{:S(2)}, u32[]{:S(2)}) %collective-permute-start.10) | collective-permute-done | bytes 196640 | tf_op jit(solution)/shard_map/ppermute | solution.py:79
  37.0 0.7 place_coarse.1
  37.7 1.1 %lift_coarse.2.refs_0_.refs_2_ = f32[2,1536,128]{2,1,0:T(8,128)S(1)} custom-call(f32[4,48,768]{2,1,0:T(8,128)S(1)} %get-tuple-element.39.refs_0_, bf16[2,1536,192]{2,1,0:T(8,128)(2,1)S(1)} %get-tuple-element.40.refs_1_, f32[4,96,128]{2,1,0:T(8,128)S(1)} %pile.2.refs_1_.refs_3_.refs_2_, f32[4,96,128]{2,1,0:T(8,128)S(1)} %collective-permute-done.13.refs_3_, ...), custom_call_target="tpu_custom_call" | custom-call | bytes 1200 | tf_op jit(solution)/shard_map/lift_coarse/pallas_call | solution.py:28
  38.8 3.2 %correct.2 = (bf16[1536,256]{1,0:T(8,128)(2,1)S(1)}, bf16[1536,256]{1,0:T(8,128)(2,1)S(1)}, f32[6,128,128]{2,1,0:T(8,128)S(1)}, f32[6,128,128]{2,1,0:T(8,128)S(1)}, f32[6,128,128]{2,1,0:T(8,128)S(1)}) custom-call(f32[2,1536,128]{2,1,0:T(8,128)S(1)} %lift_coarse.2.refs_0_.refs_2_, s32[8,128]{1,0:T(8,128)S(1)} %get-tuple-element.38.refs_4_.refs_1_.refs_0_, ...), custom_call_target="tpu_custom_call" | custom-call | bytes 3000 | tf_op jit(solution)/shard_map/correct/pallas_call | solution.py:28
  42.1 1.4 %reduce_residual.2 = (f32[2,384,128]{2,1,0:T(8,128)S(1)}, f32[2,384,128]{2,1,0:T(8,128)S(1)}) custom-call(bf16[2,768,1536]{2,1,0:T(8,128)(2,1)S(1)} %split_stiffness.1.refs_3_.refs_1_.refs_0_, f32[2,384,128]{2,1,0:T(8,128)S(1)} %get-tuple-element.35.refs_1_, f32[2,1536,128]{2,1,0:T(8,128)S(1)} %lift_coarse.2.refs_0_.refs_2_, ...), custom_call_target="tpu_custom_call" | custom-call | bytes 1200 | tf_op jit(solution)/shard_map/reduce_residual/pallas_call | solution.py:28
  43.5 1.6 %collective-permute-start.22 = (f32[2,384,128]{2,1,0:T(8,128)S(1)}, f32[2,384,128]{2,1,0:T(8,128)S(1)}, u32[]{:S(2)}, u32[]{:S(2)}) collective-permute-start(f32[2,384,128]{2,1,0:T(8,128)S(1)} %get-tuple-element.45.refs_4_.refs_1_), channel_id=1, source_target_pairs={{0,4},{2,6},{4,0},{6,2},{1,5},{3,7},{5,1},{7,3},{8,12},{10,14},{12... | collective-permute-start | bytes 1179656 | tf_op jit(solution)/shard_map/ppermute | solution.py:79
  45.3 1.9 %collective-permute-start.19 = (f32[6,128,128]{2,1,0:T(8,128)S(1)}, f32[6,128,128]{2,1,0:T(8,128)S(1)}, u32[]{:S(2)}, u32[]{:S(2)}) collective-permute-start(f32[6,128,128]{2,1,0:T(8,128)S(1)} %get-tuple-element.49), channel_id=1, source_target_pairs={{8,16},{16,8},{9,17},{17,9},{10,18},{18,10},{11,19},{19,11},{12,20... | collective-permute-start | bytes 1179656 | tf_op jit(solution)/shard_map/ppermute | solution.py:714
  47.3 6.7 %fold_targets.1 = (bf16[2,384,768]{2,1,0:T(8,128)(2,1)S(1)}, bf16[2,768,768]{2,1,0:T(8,128)(2,1)S(1)}, bf16[1,192,768]{2,1,0:T(8,128)(2,1)S(1)}) custom-call(s32[2]{0:T(128)S(1)} %copy-done.3, s32[6,2,128]{2,1,0:T(2,128)S(1)} %bitcast.2, bf16[2,768,1536]{2,1,0:T(8,128)(2,1)S(1)} %split_inverse.1.refs_1_.refs_0_.refs_2_, ...), custom_call_target="tpu_custom_call" | custom-call | bytes 4500 | tf_op jit(solution)/shard_map/fold_targets/pallas_call | solution.py:28
  54.1 0.5 collective-permute-start.23
  54.8 2.7 %collective-permute-done.19.refs_4_ = f32[6,128,128]{2,1,0:T(8,128)S(1)} collective-permute-done((f32[6,128,128]{2,1,0:T(8,128)S(1)}, f32[6,128,128]{2,1,0:T(8,128)S(1)}, u32[]{:S(2)}, u32[]{:S(2)}) %collective-permute-start.19) | collective-permute-done | bytes 393248 | tf_op jit(solution)/shard_map/ppermute | solution.py:714
  57.5 1.1 %couple.2.refs_2_.refs_8_ = f32[6,128,128]{2,1,0:T(8,128)S(1)} custom-call(s32[8,128]{1,0:T(8,128)S(1)} %get-tuple-element.38.refs_4_.refs_1_.refs_0_, f32[2,6,128,128]{3,2,1,0:T(8,128)S(1)} %copy-done.1, f32[6,128,128]{2,1,0:T(8,128)S(1)} %get-tuple-element.47.refs_2_, f32[6,128,128]{2,1,0:T(8,128)S(1)} %collective-permute-done.18.refs_3_, ...), custom_call_target="tpu_custom_call" | custom-call | bytes 800 | tf_op jit(solution)/shard_map/couple/pallas_call | solution.py:28
  58.7 1.7 %collective-permute-done.20.refs_3_.refs_2_ = f32[6,128,128]{2,1,0:T(8,128)S(1)} collective-permute-done((f32[6,128,128]{2,1,0:T(8,128)S(1)}, f32[6,128,128]{2,1,0:T(8,128)S(1)}, u32[]{:S(2)}, u32[]{:S(2)}) %collective-permute-start.20) | collective-permute-done | bytes 393248 | tf_op jit(solution)/shard_map/ppermute | solution.py:79
  60.4 1.2 %local_solve_inflow.2 = (f32[384,128]{1,0:T(8,128)S(1)}, bf16[1536,256]{1,0:T(8,128)(2,1)S(1)}) custom-call(bf16[2,768,1536]{2,1,0:T(8,128)(2,1)S(1)} %split_inverse.1.refs_1_.refs_0_.refs_2_, bf16[2,768,768]{2,1,0:T(8,128)(2,1)S(1)} %get-tuple-element.50.refs_5_.refs_1_, f32[6,128,128]{2,1,0:T(8,128)S(1)} %couple.2.refs_2_.refs_8_, ...), custom_call_target="tpu_custom_call" | custom-call | bytes 1200 | tf_op jit(solution)/shard_map/local_solve_inflow/pallas_call | solution.py:28
  61.7 1.2 %local_solve_inflow.3 = (f32[384,128]{1,0:T(8,128)S(1)}, bf16[1536,256]{1,0:T(8,128)(2,1)S(1)}) custom-call(bf16[2,768,1536]{2,1,0:T(8,128)(2,1)S(1)} %split_inverse.1.refs_1_.refs_0_.refs_2_, bf16[2,768,768]{2,1,0:T(8,128)(2,1)S(1)} %get-tuple-element.50.refs_5_.refs_1_, f32[6,128,128]{2,1,0:T(8,128)S(1)} %couple.2.refs_2_.refs_8_, ...), custom_call_target="tpu_custom_call" | custom-call | bytes 1200 | tf_op jit(solution)/shard_map/local_solve_inflow/pallas_call | solution.py:28
  62.9 0.6 collective-permute-start.32
  63.5 1.5 %collective-permute-start.29 = (f32[384,128]{1,0:T(8,128)S(1)}, f32[384,128]{1,0:T(8,128)S(1)}, u32[]{:S(2)}, u32[]{:S(2)}) collective-permute-start(f32[384,128]{1,0:T(8,128)S(1)} %get-tuple-element.52.refs_8_.refs_3_.refs_5_), channel_id=1, source_target_pairs={{0,4},{2,6},{4,0},{6,2},{1,5},{3,7},{5,1},{7,3},{8,12},{10,14},{12... | collective-permute-start | bytes 589832 | tf_op jit(solution)/shard_map/ppermute | solution.py:79
  65.0 0.6 restrict.1.refs_0_
  65.6 0.8 collective-permute-start.26
  66.4 2.8 %collective-permute-start.24 = (f32[96,128]{1,0:T(8,128)S(1)}, f32[96,128]{1,0:T(8,128)S(1)}, u32[]{:S(2)}, u32[]{:S(2)}) collective-permute-start(f32[96,128]{1,0:T(8,128)S(1)} %restrict.1.refs_0_), channel_id=1, source_target_pairs={{0,8},{8,0},{16,24},{24,16},{1,9},{9,1},{17,25},{25,17},{2,10},{10... | collective-permute-start | bytes 147464 | tf_op jit(solution)/shard_map/ppermute | solution.py:79
  69.2 1.3 %collective-permute-done.26.refs_3_ = f32[96,128]{1,0:T(8,128)S(1)} collective-permute-done((f32[96,128]{1,0:T(8,128)S(1)}, f32[96,128]{1,0:T(8,128)S(1)}, u32[]{:S(2)}, u32[]{:S(2)}) %collective-permute-start.26) | collective-permute-done | bytes 49184 | tf_op jit(solution)/shard_map/ppermute | solution.py:79
  70.5 1.0 %collective-permute-done.25.refs_2_ = f32[96,128]{1,0:T(8,128)S(1)} collective-permute-done((f32[96,128]{1,0:T(8,128)S(1)}, f32[96,128]{1,0:T(8,128)S(1)}, u32[]{:S(2)}, u32[]{:S(2)}) %collective-permute-start.25) | collective-permute-done | bytes 49184 | tf_op jit(solution)/shard_map/ppermute | solution.py:79
  71.8 0.5 collective-permute-start.28
  72.4 1.7 %collective-permute-done.29.refs_5_ = f32[384,128]{1,0:T(8,128)S(1)} collective-permute-done((f32[384,128]{1,0:T(8,128)S(1)}, f32[384,128]{1,0:T(8,128)S(1)}, u32[]{:S(2)}, u32[]{:S(2)}) %collective-permute-start.29) | collective-permute-done | bytes 196640 | tf_op jit(solution)/shard_map/ppermute | solution.py:79
  74.1 1.1 %lift_coarse.3.refs_0_.refs_2_ = f32[2,1536,128]{2,1,0:T(8,128)S(1)} custom-call(f32[4,48,768]{2,1,0:T(8,128)S(1)} %get-tuple-element.39.refs_0_, bf16[2,1536,192]{2,1,0:T(8,128)(2,1)S(1)} %get-tuple-element.40.refs_1_, f32[4,96,128]{2,1,0:T(8,128)S(1)} %pile.3.refs_2_.refs_4_, f32[4,96,128]{2,1,0:T(8,128)S(1)} %collective-permute-done.27.refs_3_, ...), custom_call_target="tpu_custom_call" | custom-call | bytes 1200 | tf_op jit(solution)/shard_map/lift_coarse/pallas_call | solution.py:28
  75.6 3.2 %correct.3 = (bf16[1536,256]{1,0:T(8,128)(2,1)S(1)}, bf16[1536,256]{1,0:T(8,128)(2,1)S(1)}, f32[6,128,128]{2,1,0:T(8,128)S(1)}, f32[6,128,128]{2,1,0:T(8,128)S(1)}, f32[6,128,128]{2,1,0:T(8,128)S(1)}) custom-call(f32[2,1536,128]{2,1,0:T(8,128)S(1)} %lift_coarse.3.refs_0_.refs_2_, s32[8,128]{1,0:T(8,128)S(1)} %get-tuple-element.38.refs_4_.refs_1_.refs_0_, ...), custom_call_target="tpu_custom_call" | custom-call | bytes 3000 | tf_op jit(solution)/shard_map/correct/pallas_call | solution.py:28
  78.9 1.9 %collective-permute-start.35 = (f32[6,128,128]{2,1,0:T(8,128)S(1)}, f32[6,128,128]{2,1,0:T(8,128)S(1)}, u32[]{:S(2)}, u32[]{:S(2)}) collective-permute-start(f32[6,128,128]{2,1,0:T(8,128)S(1)} %get-tuple-element.63), channel_id=1, source_target_pairs={{8,16},{16,8},{9,17},{17,9},{10,18},{18,10},{11,19},{19,11},{12,20... | collective-permute-start | bytes 1179656 | tf_op jit(solution)/shard_map/ppermute | solution.py:714
  80.8 2.2 %reduce_residual.3 = (f32[2,384,128]{2,1,0:T(8,128)S(1)}, f32[2,384,128]{2,1,0:T(8,128)}) custom-call(bf16[2,768,1536]{2,1,0:T(8,128)(2,1)S(1)} %split_stiffness.1.refs_3_.refs_1_.refs_0_, f32[2,384,128]{2,1,0:T(8,128)S(1)} %get-tuple-element.45.refs_4_.refs_1_, f32[2,1536,128]{2,1,0:T(8,128)S(1)} %lift_coarse.3.refs_0_.refs_2_, ...), custom_call_target="tpu_custom_call" | custom-call | bytes 1200 | tf_op jit(solution)/shard_map/reduce_residual/pallas_call | solution.py:28
  83.6 5.1 %collective-permute-done.34.refs_3_ = f32[6,128,128]{2,1,0:T(8,128)S(1)} collective-permute-done((f32[6,128,128]{2,1,0:T(8,128)S(1)}, f32[6,128,128]{2,1,0:T(8,128)S(1)}, u32[]{:S(2)}, u32[]{:S(2)}) %collective-permute-start.34) | collective-permute-done | bytes 393248 | tf_op jit(solution)/shard_map/ppermute | solution.py:714
  88.7 2.0 %collective-permute-done.35.refs_4_ = f32[6,128,128]{2,1,0:T(8,128)S(1)} collective-permute-done((f32[6,128,128]{2,1,0:T(8,128)S(1)}, f32[6,128,128]{2,1,0:T(8,128)S(1)}, u32[]{:S(2)}, u32[]{:S(2)}) %collective-permute-start.35) | collective-permute-done | bytes 393248 | tf_op jit(solution)/shard_map/ppermute | solution.py:714
  90.7 1.1 %couple.3.refs_2_ = f32[6,128,128]{2,1,0:T(8,128)S(1)} custom-call(s32[8,128]{1,0:T(8,128)S(1)} %get-tuple-element.38.refs_4_.refs_1_.refs_0_, f32[2,6,128,128]{3,2,1,0:T(8,128)S(1)} %copy-done.1, f32[6,128,128]{2,1,0:T(8,128)S(1)} %get-tuple-element.61.refs_2_, f32[6,128,128]{2,1,0:T(8,128)S(1)} %collective-permute-done.34.refs_3_, ...), custom_call_target="tpu_custom_call" | custom-call | bytes 800 | tf_op jit(solution)/shard_map/couple/pallas_call | solution.py:28
  92.3 1.4 %collective-permute-done.36.refs_2_ = f32[6,128,128]{2,1,0:T(8,128)S(1)} collective-permute-done((f32[6,128,128]{2,1,0:T(8,128)S(1)}, f32[6,128,128]{2,1,0:T(8,128)S(1)}, u32[]{:S(2)}, u32[]{:S(2)}) %collective-permute-start.36) | collective-permute-done | bytes 393248 | tf_op jit(solution)/shard_map/ppermute | solution.py:79
  93.6 1.1 %add_own_half.7 = f32[2,384,128]{2,1,0:T(8,128)} custom-call(f32[2,384,128]{2,1,0:T(8,128)S(1)} %add_own_half.5.refs_5_.refs_0_, bf16[2,384,768]{2,1,0:T(8,128)(2,1)S(1)} %get-tuple-element.60.refs_1_, f32[6,128,128]{2,1,0:T(8,128)S(1)} %collective-permute-done.36.refs_2_, f32[1,384,128]{2,1,0:T(8,128)S(1)} %add_own_half.6.refs_3_), custom_call_target="tpu_custom_call" | custom-call | bytes 800 | tf_op jit(solution)/shard_map/add_own_half/pallas_call | solution.py:28
  (68 shorter events, 5.8 us)
Async XLA Ops:
  0.6 12.2 %collective-permute-start.2 = (f32[2,384,128]{2,1,0:T(8,128)}, f32[2,384,128]{2,1,0:T(8,128)S(1)}, u32[]{:S(2)}, u32[]{:S(2)}) collective-permute-start(f32[2,384,128]{2,1,0:T(8,128)} %refs_1_.7), channel_id=1, source_target_pairs={{0,4},{2,6},{4,0},{6,2},{1,5},{3,7},{5,1},{7,3},{8,12},{10,14},{12... | collective-permute-start | bytes 1179656 | tf_op jit(solution)/shard_map/ppermute | solution.py:79
  3.7 1.3 %collective-permute-start = (f32[96,128]{1,0:T(8,128)S(1)}, f32[96,128]{1,0:T(8,128)S(1)}, u32[]{:S(2)}, u32[]{:S(2)}) collective-permute-start(f32[96,128]{1,0:T(8,128)S(1)} %get-tuple-element.34), channel_id=1, source_target_pairs={{0,2},{2,0},{4,6},{6,4},{1,3},{3,1},{5,7},{7,5},{8,10},{10,8},{12,... | collective-permute-start | bytes 147464 | tf_op jit(solution)/shard_map/ppermute | solution.py:79
  5.0 7.8 %collective-permute-start.3 = (f32[96,128]{1,0:T(8,128)S(1)}, f32[96,128]{1,0:T(8,128)S(1)}, u32[]{:S(2)}, u32[]{:S(2)}) collective-permute-start(f32[96,128]{1,0:T(8,128)S(1)} %add_up.2.refs_1_.refs_0_), channel_id=1, source_target_pairs={{0,4},{2,6},{4,0},{6,2},{1,5},{3,7},{5,1},{7,3},{8,12},{10,14},{12... | collective-permute-start | bytes 147464 | tf_op jit(solution)/shard_map/ppermute | solution.py:79
  5.6 8.9 %collective-permute-start.1 = (f32[2,384,128]{2,1,0:T(8,128)}, f32[2,384,128]{2,1,0:T(8,128)S(1)}, u32[]{:S(2)}, u32[]{:S(2)}) collective-permute-start(f32[2,384,128]{2,1,0:T(8,128)} %refs_1_.7), channel_id=1, source_target_pairs={{0,2},{2,0},{4,6},{6,4},{1,3},{3,1},{5,7},{7,5},{8,10},{10,8},{12,... | collective-permute-start | bytes 1179656 | tf_op jit(solution)/shard_map/ppermute | solution.py:79
  12.8 1.8 %copy-start = (f32[2,384,128]{2,1,0:T(8,128)S(1)}, f32[2,384,128]{2,1,0:T(8,128)}, u32[]{:S(2)}) copy-start(f32[2,384,128]{2,1,0:T(8,128)} %refs_1_.7) | copy-start | bytes 1179652
  12.9 1.8 %collective-permute-start.4 = (f32[2,384,128]{2,1,0:T(8,128)S(1)}, f32[2,384,128]{2,1,0:T(8,128)S(1)}, u32[]{:S(2)}, u32[]{:S(2)}) collective-permute-start(f32[2,384,128]{2,1,0:T(8,128)S(1)} %relay.8.refs_3_), channel_id=1, source_target_pairs={{0,2},{2,0},{4,6},{6,4},{1,3},{3,1},{5,7},{7,5},{8,10},{10,8},{12,... | collective-permute-start | bytes 1179656 | tf_op jit(solution)/shard_map/ppermute | solution.py:79
  13.0 21.4 %collective-permute-start.6 = (f32[288,384]{1,0:T(8,128)S(1)}, f32[288,384]{1,0:T(8,128)S(1)}, u32[]{:S(2)}, u32[]{:S(2)}) collective-permute-start(f32[288,384]{1,0:T(8,128)S(1)} %relay.9.refs_0_), channel_id=1, source_target_pairs={{0,4},{2,6},{4,0},{6,2},{1,5},{3,7},{5,1},{7,3},{8,12},{10,14},{12... | collective-permute-start | bytes 1327112 | tf_op jit(solution)/shard_map/ppermute | solution.py:79
  16.2 14.0 %collective-permute-start.11 = (f32[384,128]{1,0:T(8,128)S(1)}, f32[384,128]{1,0:T(8,128)S(1)}, u32[]{:S(2)}, u32[]{:S(2)}) collective-permute-start(f32[384,128]{1,0:T(8,128)S(1)} %local_solve.3.refs_1_.refs_7_.refs_6_), channel_id=1, source_target_pairs={{0,4},{2,6},{4,0},{6,2},{1,5},{3,7},{5,1},{7,3},{8,12},{10,14},{12... | collective-permute-start | bytes 589832 | tf_op jit(solution)/shard_map/ppermute | solution.py:79
  17.8 16.2 %collective-permute-start.10 = (f32[384,128]{1,0:T(8,128)S(1)}, f32[384,128]{1,0:T(8,128)S(1)}, u32[]{:S(2)}, u32[]{:S(2)}) collective-permute-start(f32[384,128]{1,0:T(8,128)S(1)} %local_solve.2.refs_5_.refs_3_), channel_id=1, source_target_pairs={{0,4},{2,6},{4,0},{6,2},{1,5},{3,7},{5,1},{7,3},{8,12},{10,14},{12... | collective-permute-start | bytes 589832 | tf_op jit(solution)/shard_map/ppermute | solution.py:79
  20.8 13.3 %collective-permute-start.9 = (f32[112,128]{1,0:T(8,128)S(1)}, f32[112,128]{1,0:T(8,128)S(1)}, u32[]{:S(2)}, u32[]{:S(2)}) collective-permute-start(f32[112,128]{1,0:T(8,128)S(1)} %add_up.3.refs_0_), channel_id=1, source_target_pairs={{0,24},{8,16},{16,8},{24,0},{1,25},{9,17},{17,9},{25,1},{2,26},{10... | collective-permute-start | bytes 172040 | tf_op jit(solution)/shard_map/ppermute | solution.py:79
  21.3 12.8 %collective-permute-start.8 = (f32[112,128]{1,0:T(8,128)S(1)}, f32[112,128]{1,0:T(8,128)S(1)}, u32[]{:S(2)}, u32[]{:S(2)}) collective-permute-start(f32[112,128]{1,0:T(8,128)S(1)} %add_up.3.refs_0_), channel_id=1, source_target_pairs={{0,16},{8,24},{16,0},{24,8},{1,17},{9,25},{17,1},{25,9},{2,18},{10... | collective-permute-start | bytes 172040 | tf_op jit(solution)/shard_map/ppermute | solution.py:79
  30.2 4.2 %collective-permute-start.7 = (f32[112,128]{1,0:T(8,128)S(1)}, f32[112,128]{1,0:T(8,128)S(1)}, u32[]{:S(2)}, u32[]{:S(2)}) collective-permute-start(f32[112,128]{1,0:T(8,128)S(1)} %add_up.3.refs_0_), channel_id=1, source_target_pairs={{0,8},{8,0},{16,24},{24,16},{1,9},{9,1},{17,25},{25,17},{2,10},{10... | collective-permute-start | bytes 172040 | tf_op jit(solution)/shard_map/ppermute | solution.py:79
  34.0 1.8 %collective-permute-start.5 = (f32[288,384]{1,0:T(8,128)S(1)}, f32[288,384]{1,0:T(8,128)S(1)}, u32[]{:S(2)}, u32[]{:S(2)}) collective-permute-start(f32[288,384]{1,0:T(8,128)S(1)} %relay.9.refs_0_), channel_id=1, source_target_pairs={{0,2},{2,0},{4,6},{6,4},{1,3},{3,1},{5,7},{7,5},{8,10},{10,8},{12,... | collective-permute-start | bytes 1327112 | tf_op jit(solution)/shard_map/ppermute | solution.py:79
  34.5 2.0 %collective-permute-start.12 = (f32[288,384]{1,0:T(8,128)S(1)}, f32[288,384]{1,0:T(8,128)S(1)}, u32[]{:S(2)}, u32[]{:S(2)}) collective-permute-start(f32[288,384]{1,0:T(8,128)S(1)} %relay.12.refs_2_), channel_id=1, source_target_pairs={{0,2},{2,0},{4,6},{6,4},{1,3},{3,1},{5,7},{7,5},{8,10},{10,8},{12,... | collective-permute-start | bytes 1327112 | tf_op jit(solution)/shard_map/ppermute | solution.py:79
  34.7 3.0 %collective-permute-start.13 = (f32[4,96,128]{2,1,0:T(8,128)S(1)}, f32[4,96,128]{2,1,0:T(8,128)S(1)}, u32[]{:S(2)}, u32[]{:S(2)}) collective-permute-start(f32[4,96,128]{2,1,0:T(8,128)S(1)} %pile.2.refs_1_.refs_3_.refs_2_), channel_id=1, source_target_pairs={{0,2},{2,0},{4,6},{6,4},{1,3},{3,1},{5,7},{7,5},{8,10},{10,8},{12,... | collective-permute-start | bytes 589832 | tf_op jit(solution)/shard_map/ppermute | solution.py:79
  35.0 3.7 %collective-permute-start.16 = (f32[384,128]{1,0:T(8,128)S(1)}, f32[384,128]{1,0:T(8,128)S(1)}, u32[]{:S(2)}, u32[]{:S(2)}) collective-permute-start(f32[384,128]{1,0:T(8,128)S(1)} %local_solve.3.refs_1_.refs_7_.refs_6_), channel_id=1, source_target_pairs={{0,2},{2,0},{4,6},{6,4},{1,3},{3,1},{5,7},{7,5},{8,10},{10,8},{12,... | collective-permute-start | bytes 589832 | tf_op jit(solution)/shard_map/ppermute | solution.py:79
  35.2 3.6 %collective-permute-start.14 = (f32[384,128]{1,0:T(8,128)S(1)}, f32[384,128]{1,0:T(8,128)S(1)}, u32[]{:S(2)}, u32[]{:S(2)}) collective-permute-start(f32[384,128]{1,0:T(8,128)S(1)} %local_solve.2.refs_5_.refs_3_), channel_id=1, source_target_pairs={{0,2},{2,0},{4,6},{6,4},{1,3},{3,1},{5,7},{7,5},{8,10},{10,8},{12,... | collective-permute-start | bytes 589832 | tf_op jit(solution)/shard_map/ppermute | solution.py:79
  35.8 3.0 %collective-permute-start.15 = (f32[384,128]{1,0:T(8,128)S(1)}, f32[384,128]{1,0:T(8,128)S(1)}, u32[]{:S(2)}, u32[]{:S(2)}) collective-permute-start(f32[384,128]{1,0:T(8,128)S(1)} %relay.10.refs_4_.refs_5_), channel_id=1, source_target_pairs={{0,2},{2,0},{4,6},{6,4},{1,3},{3,1},{5,7},{7,5},{8,10},{10,8},{12,... | collective-permute-start | bytes 589832 | tf_op jit(solution)/shard_map/ppermute | solution.py:79
  36.5 2.4 %collective-permute-start.17 = (f32[384,128]{1,0:T(8,128)S(1)}, f32[384,128]{1,0:T(8,128)S(1)}, u32[]{:S(2)}, u32[]{:S(2)}) collective-permute-start(f32[384,128]{1,0:T(8,128)S(1)} %relay.11.refs_5_.refs_9_), channel_id=1, source_target_pairs={{0,2},{2,0},{4,6},{6,4},{1,3},{3,1},{5,7},{7,5},{8,10},{10,8},{12,... | collective-permute-start | bytes 589832 | tf_op jit(solution)/shard_map/ppermute | solution.py:79
  42.1 5.2 %copy-start.2 = (s32[2,6,128]{2,0,1:T(2,128)S(1)}, s32[2,6,128]{2,0,1:T(2,128)}, u32[]{:S(2)}) copy-start(s32[2,6,128]{2,0,1:T(2,128)} %param.16) | copy-start | bytes 18436
  42.1 5.2 %copy-start.3 = (s32[2]{0:T(128)S(1)}, s32[2]{0:T(128)}, u32[]{:S(2)}) copy-start(s32[2]{0:T(128)} %refs_0_.7) | copy-start | bytes 28
  43.5 10.6 %collective-permute-start.22 = (f32[2,384,128]{2,1,0:T(8,128)S(1)}, f32[2,384,128]{2,1,0:T(8,128)S(1)}, u32[]{:S(2)}, u32[]{:S(2)}) collective-permute-start(f32[2,384,128]{2,1,0:T(8,128)S(1)} %get-tuple-element.45.refs_4_.refs_1_), channel_id=1, source_target_pairs={{0,4},{2,6},{4,0},{6,2},{1,5},{3,7},{5,1},{7,3},{8,12},{10,14},{12... | collective-permute-start | bytes 1179656 | tf_op jit(solution)/shard_map/ppermute | solution.py:79
  45.1 9.8 %collective-permute-start.18 = (f32[6,128,128]{2,1,0:T(8,128)S(1)}, f32[6,128,128]{2,1,0:T(8,128)S(1)}, u32[]{:S(2)}, u32[]{:S(2)}) collective-permute-start(f32[6,128,128]{2,1,0:T(8,128)S(1)} %get-tuple-element.48), channel_id=1, source_target_pairs={{0,8},{8,0},{16,24},{24,16},{1,9},{9,1},{17,25},{25,17},{2,10},{10... | collective-permute-start | bytes 1179656 | tf_op jit(solution)/shard_map/ppermute | solution.py:714
  45.3 12.2 %collective-permute-start.19 = (f32[6,128,128]{2,1,0:T(8,128)S(1)}, f32[6,128,128]{2,1,0:T(8,128)S(1)}, u32[]{:S(2)}, u32[]{:S(2)}) collective-permute-start(f32[6,128,128]{2,1,0:T(8,128)S(1)} %get-tuple-element.49), channel_id=1, source_target_pairs={{8,16},{16,8},{9,17},{17,9},{10,18},{18,10},{11,19},{19,11},{12,20... | collective-permute-start | bytes 1179656 | tf_op jit(solution)/shard_map/ppermute | solution.py:714
  47.2 11.5 %collective-permute-start.21 = (f32[2,384,128]{2,1,0:T(8,128)S(1)}, f32[2,384,128]{2,1,0:T(8,128)S(1)}, u32[]{:S(2)}, u32[]{:S(2)}) collective-permute-start(f32[2,384,128]{2,1,0:T(8,128)S(1)} %get-tuple-element.45.refs_4_.refs_1_), channel_id=1, source_target_pairs={{0,2},{2,0},{4,6},{6,4},{1,3},{3,1},{5,7},{7,5},{8,10},{10,8},{12,... | collective-permute-start | bytes 1179656 | tf_op jit(solution)/shard_map/ppermute | solution.py:79
  54.1 3.4 %copy-start.1 = (f32[2,6,128,128]{3,2,1,0:T(8,128)S(1)}, f32[2,6,128,128]{3,2,1,0:T(8,128)}, u32[]{:S(2)}) copy-start(f32[2,6,128,128]{3,2,1,0:T(8,128)} %refs_1_.9) | copy-start | bytes 2359300
  54.1 4.6 %collective-permute-start.23 = (f32[2,384,128]{2,1,0:T(8,128)S(1)}, f32[2,384,128]{2,1,0:T(8,128)S(1)}, u32[]{:S(2)}, u32[]{:S(2)}) collective-permute-start(f32[2,384,128]{2,1,0:T(8,128)S(1)} %relay.13.refs_6_), channel_id=1, source_target_pairs={{0,2},{2,0},{4,6},{6,4},{1,3},{3,1},{5,7},{7,5},{8,10},{10,8},{12,... | collective-permute-start | bytes 1179656 | tf_op jit(solution)/shard_map/ppermute | solution.py:79
  58.6 1.8 %collective-permute-start.20 = (f32[6,128,128]{2,1,0:T(8,128)S(1)}, f32[6,128,128]{2,1,0:T(8,128)S(1)}, u32[]{:S(2)}, u32[]{:S(2)}) collective-permute-start(f32[6,128,128]{2,1,0:T(8,128)S(1)} %couple.2.refs_2_.refs_8_), channel_id=1, source_target_pairs={{0,2},{2,0},{4,6},{6,4},{1,3},{3,1},{5,7},{7,5},{8,10},{10,8},{12,... | collective-permute-start | bytes 1179656 | tf_op jit(solution)/shard_map/ppermute | solution.py:79
  62.9 9.4 %collective-permute-start.32 = (f32[384,128]{1,0:T(8,128)S(1)}, f32[384,128]{1,0:T(8,128)S(1)}, u32[]{:S(2)}, u32[]{:S(2)}) collective-permute-start(f32[384,128]{1,0:T(8,128)S(1)} %get-tuple-element.54.refs_5_.refs_7_.refs_6_), channel_id=1, source_target_pairs={{0,4},{2,6},{4,0},{6,2},{1,5},{3,7},{5,1},{7,3},{8,12},{10,14},{12... | collective-permute-start | bytes 589832 | tf_op jit(solution)/shard_map/ppermute | solution.py:79
  63.5 10.6 %collective-permute-start.29 = (f32[384,128]{1,0:T(8,128)S(1)}, f32[384,128]{1,0:T(8,128)S(1)}, u32[]{:S(2)}, u32[]{:S(2)}) collective-permute-start(f32[384,128]{1,0:T(8,128)S(1)} %get-tuple-element.52.refs_8_.refs_3_.refs_5_), channel_id=1, source_target_pairs={{0,4},{2,6},{4,0},{6,2},{1,5},{3,7},{5,1},{7,3},{8,12},{10,14},{12... | collective-permute-start | bytes 589832 | tf_op jit(solution)/shard_map/ppermute | solution.py:79
  65.6 4.8 %collective-permute-start.26 = (f32[96,128]{1,0:T(8,128)S(1)}, f32[96,128]{1,0:T(8,128)S(1)}, u32[]{:S(2)}, u32[]{:S(2)}) collective-permute-start(f32[96,128]{1,0:T(8,128)S(1)} %restrict.1.refs_0_), channel_id=1, source_target_pairs={{0,24},{8,16},{16,8},{24,0},{1,25},{9,17},{17,9},{25,1},{2,26},{10... | collective-permute-start | bytes 147464 | tf_op jit(solution)/shard_map/ppermute | solution.py:79
  66.4 5.1 %collective-permute-start.25 = (f32[96,128]{1,0:T(8,128)S(1)}, f32[96,128]{1,0:T(8,128)S(1)}, u32[]{:S(2)}, u32[]{:S(2)}) collective-permute-start(f32[96,128]{1,0:T(8,128)S(1)} %restrict.1.refs_0_), channel_id=1, source_target_pairs={{0,16},{8,24},{16,0},{24,8},{1,17},{9,25},{17,1},{25,9},{2,18},{10... | collective-permute-start | bytes 147464 | tf_op jit(solution)/shard_map/ppermute | solution.py:79
  66.4 5.3 %collective-permute-start.24 = (f32[96,128]{1,0:T(8,128)S(1)}, f32[96,128]{1,0:T(8,128)S(1)}, u32[]{:S(2)}, u32[]{:S(2)}) collective-permute-start(f32[96,128]{1,0:T(8,128)S(1)} %restrict.1.refs_0_), channel_id=1, source_target_pairs={{0,8},{8,0},{16,24},{24,16},{1,9},{9,1},{17,25},{25,17},{2,10},{10... | collective-permute-start | bytes 147464 | tf_op jit(solution)/shard_map/ppermute | solution.py:79
  70.5 4.7 %collective-permute-start.31 = (f32[384,128]{1,0:T(8,128)S(1)}, f32[384,128]{1,0:T(8,128)S(1)}, u32[]{:S(2)}, u32[]{:S(2)}) collective-permute-start(f32[384,128]{1,0:T(8,128)S(1)} %get-tuple-element.54.refs_5_.refs_7_.refs_6_), channel_id=1, source_target_pairs={{0,2},{2,0},{4,6},{6,4},{1,3},{3,1},{5,7},{7,5},{8,10},{10,8},{12,... | collective-permute-start | bytes 589832 | tf_op jit(solution)/shard_map/ppermute | solution.py:79
  71.8 2.4 %collective-permute-start.27 = (f32[4,96,128]{2,1,0:T(8,128)S(1)}, f32[4,96,128]{2,1,0:T(8,128)S(1)}, u32[]{:S(2)}, u32[]{:S(2)}) collective-permute-start(f32[4,96,128]{2,1,0:T(8,128)S(1)} %pile.3.refs_2_.refs_4_), channel_id=1, source_target_pairs={{0,2},{2,0},{4,6},{6,4},{1,3},{3,1},{5,7},{7,5},{8,10},{10,8},{12,... | collective-permute-start | bytes 589832 | tf_op jit(solution)/shard_map/ppermute | solution.py:79
  71.8 3.4 %collective-permute-start.28 = (f32[384,128]{1,0:T(8,128)S(1)}, f32[384,128]{1,0:T(8,128)S(1)}, u32[]{:S(2)}, u32[]{:S(2)}) collective-permute-start(f32[384,128]{1,0:T(8,128)S(1)} %get-tuple-element.52.refs_8_.refs_3_.refs_5_), channel_id=1, source_target_pairs={{0,2},{2,0},{4,6},{6,4},{1,3},{3,1},{5,7},{7,5},{8,10},{10,8},{12,... | collective-permute-start | bytes 589832 | tf_op jit(solution)/shard_map/ppermute | solution.py:79
  72.4 2.9 %collective-permute-start.33 = (f32[384,128]{1,0:T(8,128)S(1)}, f32[384,128]{1,0:T(8,128)S(1)}, u32[]{:S(2)}, u32[]{:S(2)}) collective-permute-start(f32[384,128]{1,0:T(8,128)S(1)} %collective-permute-done.32.refs_9_), channel_id=1, source_target_pairs={{0,2},{2,0},{4,6},{6,4},{1,3},{3,1},{5,7},{7,5},{8,10},{10,8},{12,... | collective-permute-start | bytes 589832 | tf_op jit(solution)/shard_map/ppermute | solution.py:79
  74.1 1.4 %collective-permute-start.30 = (f32[384,128]{1,0:T(8,128)S(1)}, f32[384,128]{1,0:T(8,128)S(1)}, u32[]{:S(2)}, u32[]{:S(2)}) collective-permute-start(f32[384,128]{1,0:T(8,128)S(1)} %collective-permute-done.29.refs_5_), channel_id=1, source_target_pairs={{0,2},{2,0},{4,6},{6,4},{1,3},{3,1},{5,7},{7,5},{8,10},{10,8},{12,... | collective-permute-start | bytes 589832 | tf_op jit(solution)/shard_map/ppermute | solution.py:79
  78.8 9.9 %collective-permute-start.34 = (f32[6,128,128]{2,1,0:T(8,128)S(1)}, f32[6,128,128]{2,1,0:T(8,128)S(1)}, u32[]{:S(2)}, u32[]{:S(2)}) collective-permute-start(f32[6,128,128]{2,1,0:T(8,128)S(1)} %get-tuple-element.62), channel_id=1, source_target_pairs={{0,8},{8,0},{16,24},{24,16},{1,9},{9,1},{17,25},{25,17},{2,10},{10... | collective-permute-start | bytes 1179656 | tf_op jit(solution)/shard_map/ppermute | solution.py:714
  78.9 11.8 %collective-permute-start.35 = (f32[6,128,128]{2,1,0:T(8,128)S(1)}, f32[6,128,128]{2,1,0:T(8,128)S(1)}, u32[]{:S(2)}, u32[]{:S(2)}) collective-permute-start(f32[6,128,128]{2,1,0:T(8,128)S(1)} %get-tuple-element.63), channel_id=1, source_target_pairs={{8,16},{16,8},{9,17},{17,9},{10,18},{18,10},{11,19},{19,11},{12,20... | collective-permute-start | bytes 1179656 | tf_op jit(solution)/shard_map/ppermute | solution.py:714
  91.8 1.8 %collective-permute-start.36 = (f32[6,128,128]{2,1,0:T(8,128)S(1)}, f32[6,128,128]{2,1,0:T(8,128)S(1)}, u32[]{:S(2)}, u32[]{:S(2)}) collective-permute-start(f32[6,128,128]{2,1,0:T(8,128)S(1)} %couple.3.refs_2_), channel_id=1, source_target_pairs={{0,2},{2,0},{4,6},{6,4},{1,3},{3,1},{5,7},{7,5},{8,10},{10,8},{12,... | collective-permute-start | bytes 1179656 | tf_op jit(solution)/shard_map/ppermute | solution.py:79

commit v5 on v4

--- a/solution.py
+++ b/solution.py
@@ -690,7 +690,7 @@
     local_blocks = [gathered(v, [stiffness_split]) for v in local]
     arrived = [b[crow_size // 2] for b in local_blocks]
 
-    halves = spread_over_sub(add_up(keep, more, packed, [stiffness_split]))
+    halves = spread_over_sub(add_up(keep, more, packed, [local[-1]]))
     height = give.shape[0]
     mine = pile(halves, height, arrived)
     other = exchange(mine, "crow", 1)

time: 96.1 us -> 96.4 us (level); the launches traced: 94.7 us -> 96.5 us
  starting transfers between devices: 25.7 us -> 28 us
  Pallas kernels: 35.5 us -> 33.4 us
  waiting for transfers between devices: 32.4 us -> 34 us
    ppermute x4, starting transfers between devices: 4.14 us -> 6.54 us  [per_device(): lax.ppermute(c, 'sub', route)]
    pallas_call x34, Pallas kernels: 35.5 us -> 33.4 us  [call(): pl.pallas_call(body, in_specs=[IN_SMEM] * scalars + [IN_VMEM] * (used - s...]
    ppermute x4, waiting for transfers between devices: 9.91 us -> 11.1 us  [per_device(): lax.ppermute(c, 'sub', route)]
  transfers between devices with their start and end apart: 37 -> 37, of which waited for: 19 -> 18; matrix products, arithmetic and copies ran while one was open for 0% -> 0% of each run, Pallas kernels for 24% -> 24%
where the time goes in v5:
time: 96.4 us; the launch traced here: 96.5 us
  waiting for transfers between devices  34 us (35%)
  Pallas kernels  33.4 us (35%)
  starting transfers between devices  28 us (29%)
  between operations  1.09 us (1%)
    pallas_call x34, Pallas kernels, call(): pl.pallas_call(body, in_specs=[IN_SMEM] * scalars + [IN_VMEM] * (used - s...  33.4 us
    ppermute x33, waiting for transfers between devices, exchange(): lax.ppermute(x, axis, [(i, i ^ bit) for i in range(size) if i ^ bit < size])  22.9 us
    ppermute x33, starting transfers between devices, exchange(): lax.ppermute(x, axis, [(i, i ^ bit) for i in range(size) if i ^ bit < size])  21.5 us
    ppermute x4, waiting for transfers between devices, per_device(): lax.ppermute(c, 'sub', route)  11.1 us
    ppermute x4, starting transfers between devices, per_device(): lax.ppermute(c, 'sub', route)  6.54 us
  transfers between devices with their start and end apart: 37, of which 18 were waited for; matrix products, arithmetic and copies ran while one was open for 0% of the time, Pallas kernels for 24%

profile of v5, /device:TPU:16, one launch (start us, length us, event | category | flops | bytes accessed | tf_op | source)
XLA Modules:
  0.0 96.5 jit_solution(17242835836017337891)
XLA Ops:
  0.6 1.6 %collective-permute-start.2 = (f32[2,384,128]{2,1,0:T(8,128)}, f32[2,384,128]{2,1,0:T(8,128)S(1)}, u32[]{:S(2)}, u32[]{:S(2)}) collective-permute-start(f32[2,384,128]{2,1,0:T(8,128)} %refs_1_.7), channel_id=1, source_target_pairs={{0,4},{2,6},{4,0},{6,2},{1,5},{3,7},{5,1},{7,3},{8,12},{10,14},{12... | collective-permute-start | bytes 1179656 | tf_op jit(solution)/shard_map/ppermute | solution.py:79
  2.2 1.5 %begin.1 = (f32[96,128]{1,0:T(8,128)S(1)}, f32[96,128]{1,0:T(8,128)S(1)}, f32[2,384,128]{2,1,0:T(8,128)S(1)}, f32[16,128]{1,0:T(8,128)S(1)}, f32[288,384]{1,0:T(8,128)S(1)}) custom-call(s32[2,6]{1,0:T(2,128)} %refs_0_.4, s32[2]{0:T(128)} %refs_0_.7, s32[6,2,128]{2,1,0:T(2,128)} %bitcast.3, f32[2,96,384]{2,1,0:T(8,128)} %refs_3_.1, f32[2,384,128]{2,1,0:T(8,128)} %refs_1_.7, ...), custom_call_target="tpu_custom_call" | custom-call | bytes 2000 | tf_op jit(solution)/shard_map/begin/pallas_call | solution.py:28
  3.8 1.2 %collective-permute-done.refs_1_ = f32[96,128]{1,0:T(8,128)S(1)} collective-permute-done((f32[96,128]{1,0:T(8,128)S(1)}, f32[96,128]{1,0:T(8,128)S(1)}, u32[]{:S(2)}, u32[]{:S(2)}) %collective-permute-start) | collective-permute-done | bytes 49184 | tf_op jit(solution)/shard_map/ppermute | solution.py:79
  5.0 0.6 collective-permute-start.3
  5.6 2.5 %split_inverse.1.refs_1_.refs_0_.refs_2_ = bf16[2,768,1536]{2,1,0:T(8,128)(2,1)S(1)} custom-call(f32[2,384,1536]{2,1,0:T(8,128)} %refs_0_.5, f32[96,128]{1,0:T(8,128)S(1)} %add_up.2.refs_1_.refs_0_), custom_call_target="tpu_custom_call" | custom-call | bytes 2000 | tf_op jit(solution)/shard_map/split_inverse/pallas_call | solution.py:28
  8.1 4.7 %collective-permute-done.3.refs_0_ = f32[96,128]{1,0:T(8,128)S(1)} collective-permute-done((f32[96,128]{1,0:T(8,128)S(1)}, f32[96,128]{1,0:T(8,128)S(1)}, u32[]{:S(2)}, u32[]{:S(2)}) %collective-permute-start.3) | collective-permute-done | bytes 49184 | tf_op jit(solution)/shard_map/ppermute | solution.py:79
  13.0 1.6 %collective-permute-start.6 = (f32[288,384]{1,0:T(8,128)S(1)}, f32[288,384]{1,0:T(8,128)S(1)}, u32[]{:S(2)}, u32[]{:S(2)}) collective-permute-start(f32[288,384]{1,0:T(8,128)S(1)} %relay.9.refs_0_), channel_id=1, source_target_pairs={{0,4},{2,6},{4,0},{6,2},{1,5},{3,7},{5,1},{7,3},{8,12},{10,14},{12... | collective-permute-start | bytes 1327112 | tf_op jit(solution)/shard_map/ppermute | solution.py:79
  14.7 0.8 local_solve.2.refs_5_.refs_3_
  15.4 0.8 local_solve.3.refs_1_.refs_3_.refs_7_.refs_6_
  16.2 1.6 %collective-permute-start.11 = (f32[384,128]{1,0:T(8,128)S(1)}, f32[384,128]{1,0:T(8,128)S(1)}, u32[]{:S(2)}, u32[]{:S(2)}) collective-permute-start(f32[384,128]{1,0:T(8,128)S(1)} %local_solve.3.refs_1_.refs_3_.refs_7_.refs_6_), channel_id=1, source_target_pairs={{0,4},{2,6},{4,0},{6,2},{1,5},{3,7},{5,1},{7,3},{8,12},{10,14},{12... | collective-permute-start | bytes 589832 | tf_op jit(solution)/shard_map/ppermute | solution.py:79
  17.8 0.5 collective-permute-start.10
  18.8 3.5 %collective-permute-start.8 = (f32[112,128]{1,0:T(8,128)S(1)}, f32[112,128]{1,0:T(8,128)S(1)}, u32[]{:S(2)}, u32[]{:S(2)}) collective-permute-start(f32[112,128]{1,0:T(8,128)S(1)} %add_up.3.refs_0_), channel_id=1, source_target_pairs={{0,16},{8,24},{16,0},{24,8},{1,17},{9,25},{17,1},{25,9},{2,18},{10... | collective-permute-start | bytes 172040 | tf_op jit(solution)/shard_map/ppermute | solution.py:79
  22.3 7.9 %collective-permute-done.11.refs_0_ = f32[384,128]{1,0:T(8,128)S(1)} collective-permute-done((f32[384,128]{1,0:T(8,128)S(1)}, f32[384,128]{1,0:T(8,128)S(1)}, u32[]{:S(2)}, u32[]{:S(2)}) %collective-permute-start.11) | collective-permute-done | bytes 196640 | tf_op jit(solution)/shard_map/ppermute | solution.py:79
  30.2 1.6 %collective-permute-start.7 = (f32[112,128]{1,0:T(8,128)S(1)}, f32[112,128]{1,0:T(8,128)S(1)}, u32[]{:S(2)}, u32[]{:S(2)}) collective-permute-start(f32[112,128]{1,0:T(8,128)S(1)} %add_up.3.refs_0_), channel_id=1, source_target_pairs={{0,8},{8,0},{16,24},{24,16},{1,9},{9,1},{17,25},{25,17},{2,10},{10... | collective-permute-start | bytes 172040 | tf_op jit(solution)/shard_map/ppermute | solution.py:79
  31.8 2.5 %split_stiffness.1.refs_1_.refs_0_ = bf16[2,768,1536]{2,1,0:T(8,128)(2,1)S(1)} custom-call(f32[2,384,1536]{2,1,0:T(8,128)} %refs_0_.6, f32[384,128]{1,0:T(8,128)S(1)} %local_solve.3.refs_1_.refs_3_.refs_7_.refs_6_), custom_call_target="tpu_custom_call" | custom-call | bytes 9000000 | tf_op jit(solution)/shard_map/split_stiffness/pallas_call | solution.py:28
  34.5 0.6 collective-permute-start.12
  37.3 0.7 place_coarse.1
  38.1 1.1 %lift_coarse.2.refs_0_.refs_2_ = f32[2,1536,128]{2,1,0:T(8,128)S(1)} custom-call(f32[4,48,768]{2,1,0:T(8,128)S(1)} %get-tuple-element.39.refs_0_, bf16[2,1536,192]{2,1,0:T(8,128)(2,1)S(1)} %get-tuple-element.40.refs_1_, f32[4,96,128]{2,1,0:T(8,128)S(1)} %pile.2.refs_1_.refs_3_.refs_2_, f32[4,96,128]{2,1,0:T(8,128)S(1)} %collective-permute-done.13.refs_3_, ...), custom_call_target="tpu_custom_call" | custom-call | bytes 1200 | tf_op jit(solution)/shard_map/lift_coarse/pallas_call | solution.py:28
  39.2 2.2 %correct.2 = (bf16[1536,256]{1,0:T(8,128)(2,1)S(1)}, bf16[1536,256]{1,0:T(8,128)(2,1)S(1)}, f32[6,128,128]{2,1,0:T(8,128)S(1)}, f32[6,128,128]{2,1,0:T(8,128)S(1)}, f32[6,128,128]{2,1,0:T(8,128)S(1)}) custom-call(f32[2,1536,128]{2,1,0:T(8,128)S(1)} %lift_coarse.2.refs_0_.refs_2_, s32[8,128]{1,0:T(8,128)S(1)} %get-tuple-element.38.refs_4_.refs_1_.refs_0_, ...), custom_call_target="tpu_custom_call" | custom-call | bytes 3000 | tf_op jit(solution)/shard_map/correct/pallas_call | solution.py:28
  41.3 1.4 %reduce_residual.2 = (f32[2,384,128]{2,1,0:T(8,128)S(1)}, f32[2,384,128]{2,1,0:T(8,128)S(1)}) custom-call(bf16[2,768,1536]{2,1,0:T(8,128)(2,1)S(1)} %split_stiffness.1.refs_1_.refs_0_, f32[2,384,128]{2,1,0:T(8,128)S(1)} %get-tuple-element.35.refs_1_, f32[2,1536,128]{2,1,0:T(8,128)S(1)} %lift_coarse.2.refs_0_.refs_2_, ...), custom_call_target="tpu_custom_call" | custom-call | bytes 1200 | tf_op jit(solution)/shard_map/reduce_residual/pallas_call | solution.py:28
  42.8 1.6 %collective-permute-start.22 = (f32[2,384,128]{2,1,0:T(8,128)S(1)}, f32[2,384,128]{2,1,0:T(8,128)S(1)}, u32[]{:S(2)}, u32[]{:S(2)}) collective-permute-start(f32[2,384,128]{2,1,0:T(8,128)S(1)} %get-tuple-element.45.refs_4_.refs_1_), channel_id=1, source_target_pairs={{0,4},{2,6},{4,0},{6,2},{1,5},{3,7},{5,1},{7,3},{8,12},{10,14},{12... | collective-permute-start | bytes 1179656 | tf_op jit(solution)/shard_map/ppermute | solution.py:79
  44.3 1.5 %collective-permute-start.18 = (f32[6,128,128]{2,1,0:T(8,128)S(1)}, f32[6,128,128]{2,1,0:T(8,128)S(1)}, u32[]{:S(2)}, u32[]{:S(2)}) collective-permute-start(f32[6,128,128]{2,1,0:T(8,128)S(1)} %get-tuple-element.48), channel_id=1, source_target_pairs={{0,8},{8,0},{16,24},{24,16},{1,9},{9,1},{17,25},{25,17},{2,10},{10... | collective-permute-start | bytes 1179656 | tf_op jit(solution)/shard_map/ppermute | solution.py:714
  45.9 1.9 %collective-permute-start.19 = (f32[6,128,128]{2,1,0:T(8,128)S(1)}, f32[6,128,128]{2,1,0:T(8,128)S(1)}, u32[]{:S(2)}, u32[]{:S(2)}) collective-permute-start(f32[6,128,128]{2,1,0:T(8,128)S(1)} %get-tuple-element.49), channel_id=1, source_target_pairs={{8,16},{16,8},{9,17},{17,9},{10,18},{18,10},{11,19},{19,11},{12,20... | collective-permute-start | bytes 1179656 | tf_op jit(solution)/shard_map/ppermute | solution.py:714
  47.9 6.7 %fold_targets.1 = (bf16[2,384,768]{2,1,0:T(8,128)(2,1)S(1)}, bf16[2,768,768]{2,1,0:T(8,128)(2,1)S(1)}, bf16[1,192,768]{2,1,0:T(8,128)(2,1)S(1)}) custom-call(s32[2]{0:T(128)S(1)} %copy-done.3, s32[6,2,128]{2,1,0:T(2,128)S(1)} %bitcast.2, bf16[2,768,1536]{2,1,0:T(8,128)(2,1)S(1)} %split_inverse.1.refs_1_.refs_0_.refs_2_, ...), custom_call_target="tpu_custom_call" | custom-call | bytes 4500 | tf_op jit(solution)/shard_map/fold_targets/pallas_call | solution.py:28
  55.2 0.7 collective-permute-done.18.refs_3_
  56.0 2.6 %collective-permute-done.19.refs_4_ = f32[6,128,128]{2,1,0:T(8,128)S(1)} collective-permute-done((f32[6,128,128]{2,1,0:T(8,128)S(1)}, f32[6,128,128]{2,1,0:T(8,128)S(1)}, u32[]{:S(2)}, u32[]{:S(2)}) %collective-permute-start.19) | collective-permute-done | bytes 393248 | tf_op jit(solution)/shard_map/ppermute | solution.py:714
  58.6 1.1 %couple.2.refs_2_.refs_8_ = f32[6,128,128]{2,1,0:T(8,128)S(1)} custom-call(s32[8,128]{1,0:T(8,128)S(1)} %get-tuple-element.38.refs_4_.refs_1_.refs_0_, f32[2,6,128,128]{3,2,1,0:T(8,128)S(1)} %copy-done.1, f32[6,128,128]{2,1,0:T(8,128)S(1)} %get-tuple-element.47.refs_2_, f32[6,128,128]{2,1,0:T(8,128)S(1)} %collective-permute-done.18.refs_3_, ...), custom_call_target="tpu_custom_call" | custom-call | bytes 800 | tf_op jit(solution)/shard_map/couple/pallas_call | solution.py:28
  59.8 1.7 %collective-permute-done.20.refs_3_.refs_2_ = f32[6,128,128]{2,1,0:T(8,128)S(1)} collective-permute-done((f32[6,128,128]{2,1,0:T(8,128)S(1)}, f32[6,128,128]{2,1,0:T(8,128)S(1)}, u32[]{:S(2)}, u32[]{:S(2)}) %collective-permute-start.20) | collective-permute-done | bytes 393248 | tf_op jit(solution)/shard_map/ppermute | solution.py:79
  61.5 1.2 %local_solve_inflow.2 = (f32[384,128]{1,0:T(8,128)S(1)}, bf16[1536,256]{1,0:T(8,128)(2,1)S(1)}) custom-call(bf16[2,768,1536]{2,1,0:T(8,128)(2,1)S(1)} %split_inverse.1.refs_1_.refs_0_.refs_2_, bf16[2,768,768]{2,1,0:T(8,128)(2,1)S(1)} %get-tuple-element.50.refs_5_.refs_1_, f32[6,128,128]{2,1,0:T(8,128)S(1)} %couple.2.refs_2_.refs_8_, ...), custom_call_target="tpu_custom_call" | custom-call | bytes 1200 | tf_op jit(solution)/shard_map/local_solve_inflow/pallas_call | solution.py:28
  62.7 1.2 %local_solve_inflow.3 = (f32[384,128]{1,0:T(8,128)S(1)}, bf16[1536,256]{1,0:T(8,128)(2,1)S(1)}) custom-call(bf16[2,768,1536]{2,1,0:T(8,128)(2,1)S(1)} %split_inverse.1.refs_1_.refs_0_.refs_2_, bf16[2,768,768]{2,1,0:T(8,128)(2,1)S(1)} %get-tuple-element.50.refs_5_.refs_1_, f32[6,128,128]{2,1,0:T(8,128)S(1)} %couple.2.refs_2_.refs_8_, ...), custom_call_target="tpu_custom_call" | custom-call | bytes 1200 | tf_op jit(solution)/shard_map/local_solve_inflow/pallas_call | solution.py:28
  64.0 0.6 collective-permute-start.32
  64.6 1.5 %collective-permute-start.29 = (f32[384,128]{1,0:T(8,128)S(1)}, f32[384,128]{1,0:T(8,128)S(1)}, u32[]{:S(2)}, u32[]{:S(2)}) collective-permute-start(f32[384,128]{1,0:T(8,128)S(1)} %get-tuple-element.52.refs_8_.refs_3_.refs_5_), channel_id=1, source_target_pairs={{0,4},{2,6},{4,0},{6,2},{1,5},{3,7},{5,1},{7,3},{8,12},{10,14},{12... | collective-permute-start | bytes 589832 | tf_op jit(solution)/shard_map/ppermute | solution.py:79
  66.1 0.6 restrict.1.refs_0_
  67.5 2.7 %collective-permute-start.24 = (f32[96,128]{1,0:T(8,128)S(1)}, f32[96,128]{1,0:T(8,128)S(1)}, u32[]{:S(2)}, u32[]{:S(2)}) collective-permute-start(f32[96,128]{1,0:T(8,128)S(1)} %restrict.1.refs_0_), channel_id=1, source_target_pairs={{0,8},{8,0},{16,24},{24,16},{1,9},{9,1},{17,25},{25,17},{2,10},{10... | collective-permute-start | bytes 147464 | tf_op jit(solution)/shard_map/ppermute | solution.py:79
  70.2 1.3 %collective-permute-done.26.refs_3_ = f32[96,128]{1,0:T(8,128)S(1)} collective-permute-done((f32[96,128]{1,0:T(8,128)S(1)}, f32[96,128]{1,0:T(8,128)S(1)}, u32[]{:S(2)}, u32[]{:S(2)}) %collective-permute-start.26) | collective-permute-done | bytes 49184 | tf_op jit(solution)/shard_map/ppermute | solution.py:79
  71.5 0.6 collective-permute-done.25.refs_2_
  72.1 0.7 collective-permute-done.24.refs_1_
  73.5 1.7 %collective-permute-done.29.refs_5_ = f32[384,128]{1,0:T(8,128)S(1)} collective-permute-done((f32[384,128]{1,0:T(8,128)S(1)}, f32[384,128]{1,0:T(8,128)S(1)}, u32[]{:S(2)}, u32[]{:S(2)}) %collective-permute-start.29) | collective-permute-done | bytes 196640 | tf_op jit(solution)/shard_map/ppermute | solution.py:79
  75.2 1.1 %lift_coarse.3.refs_0_.refs_2_ = f32[2,1536,128]{2,1,0:T(8,128)S(1)} custom-call(f32[4,48,768]{2,1,0:T(8,128)S(1)} %get-tuple-element.39.refs_0_, bf16[2,1536,192]{2,1,0:T(8,128)(2,1)S(1)} %get-tuple-element.40.refs_1_, f32[4,96,128]{2,1,0:T(8,128)S(1)} %pile.3.refs_2_.refs_4_, f32[4,96,128]{2,1,0:T(8,128)S(1)} %collective-permute-done.27.refs_3_, ...), custom_call_target="tpu_custom_call" | custom-call | bytes 1200 | tf_op jit(solution)/shard_map/lift_coarse/pallas_call | solution.py:28
  76.6 2.1 %correct.3 = (bf16[1536,256]{1,0:T(8,128)(2,1)S(1)}, bf16[1536,256]{1,0:T(8,128)(2,1)S(1)}, f32[6,128,128]{2,1,0:T(8,128)S(1)}, f32[6,128,128]{2,1,0:T(8,128)S(1)}, f32[6,128,128]{2,1,0:T(8,128)S(1)}) custom-call(f32[2,1536,128]{2,1,0:T(8,128)S(1)} %lift_coarse.3.refs_0_.refs_2_, s32[8,128]{1,0:T(8,128)S(1)} %get-tuple-element.38.refs_4_.refs_1_.refs_0_, ...), custom_call_target="tpu_custom_call" | custom-call | bytes 3000 | tf_op jit(solution)/shard_map/correct/pallas_call | solution.py:28
  78.8 0.9 collective-permute-start.34
  79.7 2.2 %collective-permute-start.35 = (f32[6,128,128]{2,1,0:T(8,128)S(1)}, f32[6,128,128]{2,1,0:T(8,128)S(1)}, u32[]{:S(2)}, u32[]{:S(2)}) collective-permute-start(f32[6,128,128]{2,1,0:T(8,128)S(1)} %get-tuple-element.63), channel_id=1, source_target_pairs={{8,16},{16,8},{9,17},{17,9},{10,18},{18,10},{11,19},{19,11},{12,20... | collective-permute-start | bytes 1179656 | tf_op jit(solution)/shard_map/ppermute | solution.py:714
  81.9 2.2 %reduce_residual.3 = (f32[2,384,128]{2,1,0:T(8,128)S(1)}, f32[2,384,128]{2,1,0:T(8,128)}) custom-call(bf16[2,768,1536]{2,1,0:T(8,128)(2,1)S(1)} %split_stiffness.1.refs_1_.refs_0_, f32[2,384,128]{2,1,0:T(8,128)S(1)} %get-tuple-element.45.refs_4_.refs_1_, f32[2,1536,128]{2,1,0:T(8,128)S(1)} %lift_coarse.3.refs_0_.refs_2_, ...), custom_call_target="tpu_custom_call" | custom-call | bytes 1200 | tf_op jit(solution)/shard_map/reduce_residual/pallas_call | solution.py:28
  84.7 5.9 %collective-permute-done.34.refs_3_ = f32[6,128,128]{2,1,0:T(8,128)S(1)} collective-permute-done((f32[6,128,128]{2,1,0:T(8,128)S(1)}, f32[6,128,128]{2,1,0:T(8,128)S(1)}, u32[]{:S(2)}, u32[]{:S(2)}) %collective-permute-start.34) | collective-permute-done | bytes 393248 | tf_op jit(solution)/shard_map/ppermute | solution.py:714
  90.6 1.9 %collective-permute-done.35.refs_4_ = f32[6,128,128]{2,1,0:T(8,128)S(1)} collective-permute-done((f32[6,128,128]{2,1,0:T(8,128)S(1)}, f32[6,128,128]{2,1,0:T(8,128)S(1)}, u32[]{:S(2)}, u32[]{:S(2)}) %collective-permute-start.35) | collective-permute-done | bytes 393248 | tf_op jit(solution)/shard_map/ppermute | solution.py:714
  92.5 1.1 %couple.3.refs_2_ = f32[6,128,128]{2,1,0:T(8,128)S(1)} custom-call(s32[8,128]{1,0:T(8,128)S(1)} %get-tuple-element.38.refs_4_.refs_1_.refs_0_, f32[2,6,128,128]{3,2,1,0:T(8,128)S(1)} %copy-done.1, f32[6,128,128]{2,1,0:T(8,128)S(1)} %get-tuple-element.61.refs_2_, f32[6,128,128]{2,1,0:T(8,128)S(1)} %collective-permute-done.34.refs_3_, ...), custom_call_target="tpu_custom_call" | custom-call | bytes 800 | tf_op jit(solution)/shard_map/couple/pallas_call | solution.py:28
  94.0 1.4 %collective-permute-done.36.refs_2_ = f32[6,128,128]{2,1,0:T(8,128)S(1)} collective-permute-done((f32[6,128,128]{2,1,0:T(8,128)S(1)}, f32[6,128,128]{2,1,0:T(8,128)S(1)}, u32[]{:S(2)}, u32[]{:S(2)}) %collective-permute-start.36) | collective-permute-done | bytes 393248 | tf_op jit(solution)/shard_map/ppermute | solution.py:79
  95.4 1.1 %add_own_half.7 = f32[2,384,128]{2,1,0:T(8,128)} custom-call(f32[2,384,128]{2,1,0:T(8,128)S(1)} %add_own_half.5.refs_5_.refs_0_, bf16[2,384,768]{2,1,0:T(8,128)(2,1)S(1)} %get-tuple-element.60.refs_1_, f32[6,128,128]{2,1,0:T(8,128)S(1)} %collective-permute-done.36.refs_2_, f32[1,384,128]{2,1,0:T(8,128)S(1)} %add_own_half.6.refs_3_), custom_call_target="tpu_custom_call" | custom-call | bytes 800 | tf_op jit(solution)/shard_map/add_own_half/pallas_call | solution.py:28
  (68 shorter events, 7.0 us)
Async XLA Ops:
  0.6 12.2 %collective-permute-start.2 = (f32[2,384,128]{2,1,0:T(8,128)}, f32[2,384,128]{2,1,0:T(8,128)S(1)}, u32[]{:S(2)}, u32[]{:S(2)}) collective-permute-start(f32[2,384,128]{2,1,0:T(8,128)} %refs_1_.7), channel_id=1, source_target_pairs={{0,4},{2,6},{4,0},{6,2},{1,5},{3,7},{5,1},{7,3},{8,12},{10,14},{12... | collective-permute-start | bytes 1179656 | tf_op jit(solution)/shard_map/ppermute | solution.py:79
  3.7 1.3 %collective-permute-start = (f32[96,128]{1,0:T(8,128)S(1)}, f32[96,128]{1,0:T(8,128)S(1)}, u32[]{:S(2)}, u32[]{:S(2)}) collective-permute-start(f32[96,128]{1,0:T(8,128)S(1)} %get-tuple-element.34), channel_id=1, source_target_pairs={{0,2},{2,0},{4,6},{6,4},{1,3},{3,1},{5,7},{7,5},{8,10},{10,8},{12,... | collective-permute-start | bytes 147464 | tf_op jit(solution)/shard_map/ppermute | solution.py:79
  5.0 7.8 %collective-permute-start.3 = (f32[96,128]{1,0:T(8,128)S(1)}, f32[96,128]{1,0:T(8,128)S(1)}, u32[]{:S(2)}, u32[]{:S(2)}) collective-permute-start(f32[96,128]{1,0:T(8,128)S(1)} %add_up.2.refs_1_.refs_0_), channel_id=1, source_target_pairs={{0,4},{2,6},{4,0},{6,2},{1,5},{3,7},{5,1},{7,3},{8,12},{10,14},{12... | collective-permute-start | bytes 147464 | tf_op jit(solution)/shard_map/ppermute | solution.py:79
  5.6 8.9 %collective-permute-start.1 = (f32[2,384,128]{2,1,0:T(8,128)}, f32[2,384,128]{2,1,0:T(8,128)S(1)}, u32[]{:S(2)}, u32[]{:S(2)}) collective-permute-start(f32[2,384,128]{2,1,0:T(8,128)} %refs_1_.7), channel_id=1, source_target_pairs={{0,2},{2,0},{4,6},{6,4},{1,3},{3,1},{5,7},{7,5},{8,10},{10,8},{12,... | collective-permute-start | bytes 1179656 | tf_op jit(solution)/shard_map/ppermute | solution.py:79
  12.8 1.8 %copy-start = (f32[2,384,128]{2,1,0:T(8,128)S(1)}, f32[2,384,128]{2,1,0:T(8,128)}, u32[]{:S(2)}) copy-start(f32[2,384,128]{2,1,0:T(8,128)} %refs_1_.7) | copy-start | bytes 1179652
  12.9 1.8 %collective-permute-start.4 = (f32[2,384,128]{2,1,0:T(8,128)S(1)}, f32[2,384,128]{2,1,0:T(8,128)S(1)}, u32[]{:S(2)}, u32[]{:S(2)}) collective-permute-start(f32[2,384,128]{2,1,0:T(8,128)S(1)} %relay.8.refs_3_), channel_id=1, source_target_pairs={{0,2},{2,0},{4,6},{6,4},{1,3},{3,1},{5,7},{7,5},{8,10},{10,8},{12,... | collective-permute-start | bytes 1179656 | tf_op jit(solution)/shard_map/ppermute | solution.py:79
  13.0 21.5 %collective-permute-start.6 = (f32[288,384]{1,0:T(8,128)S(1)}, f32[288,384]{1,0:T(8,128)S(1)}, u32[]{:S(2)}, u32[]{:S(2)}) collective-permute-start(f32[288,384]{1,0:T(8,128)S(1)} %relay.9.refs_0_), channel_id=1, source_target_pairs={{0,4},{2,6},{4,0},{6,2},{1,5},{3,7},{5,1},{7,3},{8,12},{10,14},{12... | collective-permute-start | bytes 1327112 | tf_op jit(solution)/shard_map/ppermute | solution.py:79
  16.2 14.0 %collective-permute-start.11 = (f32[384,128]{1,0:T(8,128)S(1)}, f32[384,128]{1,0:T(8,128)S(1)}, u32[]{:S(2)}, u32[]{:S(2)}) collective-permute-start(f32[384,128]{1,0:T(8,128)S(1)} %local_solve.3.refs_1_.refs_3_.refs_7_.refs_6_), channel_id=1, source_target_pairs={{0,4},{2,6},{4,0},{6,2},{1,5},{3,7},{5,1},{7,3},{8,12},{10,14},{12... | collective-permute-start | bytes 589832 | tf_op jit(solution)/shard_map/ppermute | solution.py:79
  17.8 16.5 %collective-permute-start.10 = (f32[384,128]{1,0:T(8,128)S(1)}, f32[384,128]{1,0:T(8,128)S(1)}, u32[]{:S(2)}, u32[]{:S(2)}) collective-permute-start(f32[384,128]{1,0:T(8,128)S(1)} %local_solve.2.refs_5_.refs_3_), channel_id=1, source_target_pairs={{0,4},{2,6},{4,0},{6,2},{1,5},{3,7},{5,1},{7,3},{8,12},{10,14},{12... | collective-permute-start | bytes 589832 | tf_op jit(solution)/shard_map/ppermute | solution.py:79
  18.3 16.1 %collective-permute-start.9 = (f32[112,128]{1,0:T(8,128)S(1)}, f32[112,128]{1,0:T(8,128)S(1)}, u32[]{:S(2)}, u32[]{:S(2)}) collective-permute-start(f32[112,128]{1,0:T(8,128)S(1)} %add_up.3.refs_0_), channel_id=1, source_target_pairs={{0,24},{8,16},{16,8},{24,0},{1,25},{9,17},{17,9},{25,1},{2,26},{10... | collective-permute-start | bytes 172040 | tf_op jit(solution)/shard_map/ppermute | solution.py:79
  18.8 15.6 %collective-permute-start.8 = (f32[112,128]{1,0:T(8,128)S(1)}, f32[112,128]{1,0:T(8,128)S(1)}, u32[]{:S(2)}, u32[]{:S(2)}) collective-permute-start(f32[112,128]{1,0:T(8,128)S(1)} %add_up.3.refs_0_), channel_id=1, source_target_pairs={{0,16},{8,24},{16,0},{24,8},{1,17},{9,25},{17,1},{25,9},{2,18},{10... | collective-permute-start | bytes 172040 | tf_op jit(solution)/shard_map/ppermute | solution.py:79
  30.2 4.2 %collective-permute-start.7 = (f32[112,128]{1,0:T(8,128)S(1)}, f32[112,128]{1,0:T(8,128)S(1)}, u32[]{:S(2)}, u32[]{:S(2)}) collective-permute-start(f32[112,128]{1,0:T(8,128)S(1)} %add_up.3.refs_0_), channel_id=1, source_target_pairs={{0,8},{8,0},{16,24},{24,16},{1,9},{9,1},{17,25},{25,17},{2,10},{10... | collective-permute-start | bytes 172040 | tf_op jit(solution)/shard_map/ppermute | solution.py:79
  34.3 1.9 %collective-permute-start.5 = (f32[288,384]{1,0:T(8,128)S(1)}, f32[288,384]{1,0:T(8,128)S(1)}, u32[]{:S(2)}, u32[]{:S(2)}) collective-permute-start(f32[288,384]{1,0:T(8,128)S(1)} %relay.9.refs_0_), channel_id=1, source_target_pairs={{0,2},{2,0},{4,6},{6,4},{1,3},{3,1},{5,7},{7,5},{8,10},{10,8},{12,... | collective-permute-start | bytes 1327112 | tf_op jit(solution)/shard_map/ppermute | solution.py:79
  34.5 2.3 %collective-permute-start.12 = (f32[288,384]{1,0:T(8,128)S(1)}, f32[288,384]{1,0:T(8,128)S(1)}, u32[]{:S(2)}, u32[]{:S(2)}) collective-permute-start(f32[288,384]{1,0:T(8,128)S(1)} %relay.12.refs_2_), channel_id=1, source_target_pairs={{0,2},{2,0},{4,6},{6,4},{1,3},{3,1},{5,7},{7,5},{8,10},{10,8},{12,... | collective-permute-start | bytes 1327112 | tf_op jit(solution)/shard_map/ppermute | solution.py:79
  35.1 3.0 %collective-permute-start.13 = (f32[4,96,128]{2,1,0:T(8,128)S(1)}, f32[4,96,128]{2,1,0:T(8,128)S(1)}, u32[]{:S(2)}, u32[]{:S(2)}) collective-permute-start(f32[4,96,128]{2,1,0:T(8,128)S(1)} %pile.2.refs_1_.refs_3_.refs_2_), channel_id=1, source_target_pairs={{0,2},{2,0},{4,6},{6,4},{1,3},{3,1},{5,7},{7,5},{8,10},{10,8},{12,... | collective-permute-start | bytes 589832 | tf_op jit(solution)/shard_map/ppermute | solution.py:79
  35.1 4.0 %collective-permute-start.16 = (f32[384,128]{1,0:T(8,128)S(1)}, f32[384,128]{1,0:T(8,128)S(1)}, u32[]{:S(2)}, u32[]{:S(2)}) collective-permute-start(f32[384,128]{1,0:T(8,128)S(1)} %local_solve.3.refs_1_.refs_3_.refs_7_.refs_6_), channel_id=1, source_target_pairs={{0,2},{2,0},{4,6},{6,4},{1,3},{3,1},{5,7},{7,5},{8,10},{10,8},{12,... | collective-permute-start | bytes 589832 | tf_op jit(solution)/shard_map/ppermute | solution.py:79
  35.6 3.6 %collective-permute-start.14 = (f32[384,128]{1,0:T(8,128)S(1)}, f32[384,128]{1,0:T(8,128)S(1)}, u32[]{:S(2)}, u32[]{:S(2)}) collective-permute-start(f32[384,128]{1,0:T(8,128)S(1)} %local_solve.2.refs_5_.refs_3_), channel_id=1, source_target_pairs={{0,2},{2,0},{4,6},{6,4},{1,3},{3,1},{5,7},{7,5},{8,10},{10,8},{12,... | collective-permute-start | bytes 589832 | tf_op jit(solution)/shard_map/ppermute | solution.py:79
  36.2 3.0 %collective-permute-start.15 = (f32[384,128]{1,0:T(8,128)S(1)}, f32[384,128]{1,0:T(8,128)S(1)}, u32[]{:S(2)}, u32[]{:S(2)}) collective-permute-start(f32[384,128]{1,0:T(8,128)S(1)} %relay.10.refs_4_.refs_5_), channel_id=1, source_target_pairs={{0,2},{2,0},{4,6},{6,4},{1,3},{3,1},{5,7},{7,5},{8,10},{10,8},{12,... | collective-permute-start | bytes 589832 | tf_op jit(solution)/shard_map/ppermute | solution.py:79
  36.8 2.4 %collective-permute-start.17 = (f32[384,128]{1,0:T(8,128)S(1)}, f32[384,128]{1,0:T(8,128)S(1)}, u32[]{:S(2)}, u32[]{:S(2)}) collective-permute-start(f32[384,128]{1,0:T(8,128)S(1)} %relay.11.refs_5_.refs_9_), channel_id=1, source_target_pairs={{0,2},{2,0},{4,6},{6,4},{1,3},{3,1},{5,7},{7,5},{8,10},{10,8},{12,... | collective-permute-start | bytes 589832 | tf_op jit(solution)/shard_map/ppermute | solution.py:79
  41.3 6.5 %copy-start.2 = (s32[2,6,128]{2,0,1:T(2,128)S(1)}, s32[2,6,128]{2,0,1:T(2,128)}, u32[]{:S(2)}) copy-start(s32[2,6,128]{2,0,1:T(2,128)} %param.16) | copy-start | bytes 18436
  41.3 6.5 %copy-start.3 = (s32[2]{0:T(128)S(1)}, s32[2]{0:T(128)}, u32[]{:S(2)}) copy-start(s32[2]{0:T(128)} %refs_0_.7) | copy-start | bytes 28
  42.8 12.0 %collective-permute-start.22 = (f32[2,384,128]{2,1,0:T(8,128)S(1)}, f32[2,384,128]{2,1,0:T(8,128)S(1)}, u32[]{:S(2)}, u32[]{:S(2)}) collective-permute-start(f32[2,384,128]{2,1,0:T(8,128)S(1)} %get-tuple-element.45.refs_4_.refs_1_), channel_id=1, source_target_pairs={{0,4},{2,6},{4,0},{6,2},{1,5},{3,7},{5,1},{7,3},{8,12},{10,14},{12... | collective-permute-start | bytes 1179656 | tf_op jit(solution)/shard_map/ppermute | solution.py:79
  44.3 11.6 %collective-permute-start.18 = (f32[6,128,128]{2,1,0:T(8,128)S(1)}, f32[6,128,128]{2,1,0:T(8,128)S(1)}, u32[]{:S(2)}, u32[]{:S(2)}) collective-permute-start(f32[6,128,128]{2,1,0:T(8,128)S(1)} %get-tuple-element.48), channel_id=1, source_target_pairs={{0,8},{8,0},{16,24},{24,16},{1,9},{9,1},{17,25},{25,17},{2,10},{10... | collective-permute-start | bytes 1179656 | tf_op jit(solution)/shard_map/ppermute | solution.py:714
  45.9 12.7 %collective-permute-start.19 = (f32[6,128,128]{2,1,0:T(8,128)S(1)}, f32[6,128,128]{2,1,0:T(8,128)S(1)}, u32[]{:S(2)}, u32[]{:S(2)}) collective-permute-start(f32[6,128,128]{2,1,0:T(8,128)S(1)} %get-tuple-element.49), channel_id=1, source_target_pairs={{8,16},{16,8},{9,17},{17,9},{10,18},{18,10},{11,19},{19,11},{12,20... | collective-permute-start | bytes 1179656 | tf_op jit(solution)/shard_map/ppermute | solution.py:714
  47.8 12.0 %collective-permute-start.21 = (f32[2,384,128]{2,1,0:T(8,128)S(1)}, f32[2,384,128]{2,1,0:T(8,128)S(1)}, u32[]{:S(2)}, u32[]{:S(2)}) collective-permute-start(f32[2,384,128]{2,1,0:T(8,128)S(1)} %get-tuple-element.45.refs_4_.refs_1_), channel_id=1, source_target_pairs={{0,2},{2,0},{4,6},{6,4},{1,3},{3,1},{5,7},{7,5},{8,10},{10,8},{12,... | collective-permute-start | bytes 1179656 | tf_op jit(solution)/shard_map/ppermute | solution.py:79
  54.8 3.8 %copy-start.1 = (f32[2,6,128,128]{3,2,1,0:T(8,128)S(1)}, f32[2,6,128,128]{3,2,1,0:T(8,128)}, u32[]{:S(2)}) copy-start(f32[2,6,128,128]{3,2,1,0:T(8,128)} %refs_1_.9) | copy-start | bytes 2359300
  54.8 5.0 %collective-permute-start.23 = (f32[2,384,128]{2,1,0:T(8,128)S(1)}, f32[2,384,128]{2,1,0:T(8,128)S(1)}, u32[]{:S(2)}, u32[]{:S(2)}) collective-permute-start(f32[2,384,128]{2,1,0:T(8,128)S(1)} %relay.13.refs_6_), channel_id=1, source_target_pairs={{0,2},{2,0},{4,6},{6,4},{1,3},{3,1},{5,7},{7,5},{8,10},{10,8},{12,... | collective-permute-start | bytes 1179656 | tf_op jit(solution)/shard_map/ppermute | solution.py:79
  59.7 1.8 %collective-permute-start.20 = (f32[6,128,128]{2,1,0:T(8,128)S(1)}, f32[6,128,128]{2,1,0:T(8,128)S(1)}, u32[]{:S(2)}, u32[]{:S(2)}) collective-permute-start(f32[6,128,128]{2,1,0:T(8,128)S(1)} %couple.2.refs_2_.refs_8_), channel_id=1, source_target_pairs={{0,2},{2,0},{4,6},{6,4},{1,3},{3,1},{5,7},{7,5},{8,10},{10,8},{12,... | collective-permute-start | bytes 1179656 | tf_op jit(solution)/shard_map/ppermute | solution.py:79
  64.0 9.4 %collective-permute-start.32 = (f32[384,128]{1,0:T(8,128)S(1)}, f32[384,128]{1,0:T(8,128)S(1)}, u32[]{:S(2)}, u32[]{:S(2)}) collective-permute-start(f32[384,128]{1,0:T(8,128)S(1)} %get-tuple-element.54.refs_5_.refs_7_.refs_6_), channel_id=1, source_target_pairs={{0,4},{2,6},{4,0},{6,2},{1,5},{3,7},{5,1},{7,3},{8,12},{10,14},{12... | collective-permute-start | bytes 589832 | tf_op jit(solution)/shard_map/ppermute | solution.py:79
  64.6 10.6 %collective-permute-start.29 = (f32[384,128]{1,0:T(8,128)S(1)}, f32[384,128]{1,0:T(8,128)S(1)}, u32[]{:S(2)}, u32[]{:S(2)}) collective-permute-start(f32[384,128]{1,0:T(8,128)S(1)} %get-tuple-element.52.refs_8_.refs_3_.refs_5_), channel_id=1, source_target_pairs={{0,4},{2,6},{4,0},{6,2},{1,5},{3,7},{5,1},{7,3},{8,12},{10,14},{12... | collective-permute-start | bytes 589832 | tf_op jit(solution)/shard_map/ppermute | solution.py:79
  66.6 4.9 %collective-permute-start.26 = (f32[96,128]{1,0:T(8,128)S(1)}, f32[96,128]{1,0:T(8,128)S(1)}, u32[]{:S(2)}, u32[]{:S(2)}) collective-permute-start(f32[96,128]{1,0:T(8,128)S(1)} %restrict.1.refs_0_), channel_id=1, source_target_pairs={{0,24},{8,16},{16,8},{24,0},{1,25},{9,17},{17,9},{25,1},{2,26},{10... | collective-permute-start | bytes 147464 | tf_op jit(solution)/shard_map/ppermute | solution.py:79
  67.0 5.1 %collective-permute-start.25 = (f32[96,128]{1,0:T(8,128)S(1)}, f32[96,128]{1,0:T(8,128)S(1)}, u32[]{:S(2)}, u32[]{:S(2)}) collective-permute-start(f32[96,128]{1,0:T(8,128)S(1)} %restrict.1.refs_0_), channel_id=1, source_target_pairs={{0,16},{8,24},{16,0},{24,8},{1,17},{9,25},{17,1},{25,9},{2,18},{10... | collective-permute-start | bytes 147464 | tf_op jit(solution)/shard_map/ppermute | solution.py:79
  67.5 5.3 %collective-permute-start.24 = (f32[96,128]{1,0:T(8,128)S(1)}, f32[96,128]{1,0:T(8,128)S(1)}, u32[]{:S(2)}, u32[]{:S(2)}) collective-permute-start(f32[96,128]{1,0:T(8,128)S(1)} %restrict.1.refs_0_), channel_id=1, source_target_pairs={{0,8},{8,0},{16,24},{24,16},{1,9},{9,1},{17,25},{25,17},{2,10},{10... | collective-permute-start | bytes 147464 | tf_op jit(solution)/shard_map/ppermute | solution.py:79
  71.5 4.7 %collective-permute-start.31 = (f32[384,128]{1,0:T(8,128)S(1)}, f32[384,128]{1,0:T(8,128)S(1)}, u32[]{:S(2)}, u32[]{:S(2)}) collective-permute-start(f32[384,128]{1,0:T(8,128)S(1)} %get-tuple-element.54.refs_5_.refs_7_.refs_6_), channel_id=1, source_target_pairs={{0,2},{2,0},{4,6},{6,4},{1,3},{3,1},{5,7},{7,5},{8,10},{10,8},{12,... | collective-permute-start | bytes 589832 | tf_op jit(solution)/shard_map/ppermute | solution.py:79
  72.8 2.4 %collective-permute-start.27 = (f32[4,96,128]{2,1,0:T(8,128)S(1)}, f32[4,96,128]{2,1,0:T(8,128)S(1)}, u32[]{:S(2)}, u32[]{:S(2)}) collective-permute-start(f32[4,96,128]{2,1,0:T(8,128)S(1)} %pile.3.refs_2_.refs_4_), channel_id=1, source_target_pairs={{0,2},{2,0},{4,6},{6,4},{1,3},{3,1},{5,7},{7,5},{8,10},{10,8},{12,... | collective-permute-start | bytes 589832 | tf_op jit(solution)/shard_map/ppermute | solution.py:79
  72.9 3.4 %collective-permute-start.28 = (f32[384,128]{1,0:T(8,128)S(1)}, f32[384,128]{1,0:T(8,128)S(1)}, u32[]{:S(2)}, u32[]{:S(2)}) collective-permute-start(f32[384,128]{1,0:T(8,128)S(1)} %get-tuple-element.52.refs_8_.refs_3_.refs_5_), channel_id=1, source_target_pairs={{0,2},{2,0},{4,6},{6,4},{1,3},{3,1},{5,7},{7,5},{8,10},{10,8},{12,... | collective-permute-start | bytes 589832 | tf_op jit(solution)/shard_map/ppermute | solution.py:79
  73.4 2.9 %collective-permute-start.33 = (f32[384,128]{1,0:T(8,128)S(1)}, f32[384,128]{1,0:T(8,128)S(1)}, u32[]{:S(2)}, u32[]{:S(2)}) collective-permute-start(f32[384,128]{1,0:T(8,128)S(1)} %collective-permute-done.32.refs_9_), channel_id=1, source_target_pairs={{0,2},{2,0},{4,6},{6,4},{1,3},{3,1},{5,7},{7,5},{8,10},{10,8},{12,... | collective-permute-start | bytes 589832 | tf_op jit(solution)/shard_map/ppermute | solution.py:79
  75.2 1.4 %collective-permute-start.30 = (f32[384,128]{1,0:T(8,128)S(1)}, f32[384,128]{1,0:T(8,128)S(1)}, u32[]{:S(2)}, u32[]{:S(2)}) collective-permute-start(f32[384,128]{1,0:T(8,128)S(1)} %collective-permute-done.29.refs_5_), channel_id=1, source_target_pairs={{0,2},{2,0},{4,6},{6,4},{1,3},{3,1},{5,7},{7,5},{8,10},{10,8},{12,... | collective-permute-start | bytes 589832 | tf_op jit(solution)/shard_map/ppermute | solution.py:79
  78.8 11.8 %collective-permute-start.34 = (f32[6,128,128]{2,1,0:T(8,128)S(1)}, f32[6,128,128]{2,1,0:T(8,128)S(1)}, u32[]{:S(2)}, u32[]{:S(2)}) collective-permute-start(f32[6,128,128]{2,1,0:T(8,128)S(1)} %get-tuple-element.62), channel_id=1, source_target_pairs={{0,8},{8,0},{16,24},{24,16},{1,9},{9,1},{17,25},{25,17},{2,10},{10... | collective-permute-start | bytes 1179656 | tf_op jit(solution)/shard_map/ppermute | solution.py:714
  79.7 12.8 %collective-permute-start.35 = (f32[6,128,128]{2,1,0:T(8,128)S(1)}, f32[6,128,128]{2,1,0:T(8,128)S(1)}, u32[]{:S(2)}, u32[]{:S(2)}) collective-permute-start(f32[6,128,128]{2,1,0:T(8,128)S(1)} %get-tuple-element.63), channel_id=1, source_target_pairs={{8,16},{16,8},{9,17},{17,9},{10,18},{18,10},{11,19},{19,11},{12,20... | collective-permute-start | bytes 1179656 | tf_op jit(solution)/shard_map/ppermute | solution.py:714
  93.6 1.8 %collective-permute-start.36 = (f32[6,128,128]{2,1,0:T(8,128)S(1)}, f32[6,128,128]{2,1,0:T(8,128)S(1)}, u32[]{:S(2)}, u32[]{:S(2)}) collective-permute-start(f32[6,128,128]{2,1,0:T(8,128)S(1)} %couple.3.refs_2_), channel_id=1, source_target_pairs={{0,2},{2,0},{4,6},{6,4},{1,3},{3,1},{5,7},{7,5},{8,10},{10,8},{12,... | collective-permute-start | bytes 1179656 | tf_op jit(solution)/shard_map/ppermute | solution.py:79
